TPU v7x, 256 devices: a whole 4x4x8 slice. The times are simulated.
256 devices in a mesh: dp: 64 (over y, x_hi, z), emb: 4 (over x_lo, core).
Axes of the slice: x: 4 (x_hi: 2, x_lo: 2; x = x_hi * 2 + x_lo), y: 4, z: 8, core: 2. Of those that a mesh axis runs over, the one named last changes fastest.
Arguments:
- visual_features: bfloat16 [8192, 1280], P('dp'), may hold values from -10 to 10
- sound_features: bfloat16 [8192, 1280], P('dp'), may hold values from -10 to 10
- tactile_features: bfloat16 [8192, 1280], P('dp'), may hold values from -10 to 10
- visual_mapping_matrix: bfloat16 [1280, 1024], P(None, 'emb'), may hold values from -1 to 1
- sound_mapping_matrix: bfloat16 [1280, 1024], P(None, 'emb'), may hold values from -1 to 1
- tactile_mapping_matrix: bfloat16 [1280, 1024], P(None, 'emb'), may hold values from -1 to 1
- couple_sharpness: float32 [3], replicated, may hold values from 10 to 30
Outputs:
- total_loss: float32 [], replicated
- video_grad: float32 [1280, 1024], P('dp', 'emb')
- audio_head_gradient: float32 [1280, 1024], P('dp', 'emb')
- touch_grad: float32 [1280, 1024], P('dp', 'emb')
All inputs are finite; a program needn't handle non-finite values.
Results may differ from a plain program's by a relative error of at most 0.0025.
The roundings to bfloat16 on the way count: a program that leaves them out, or rounds other values in their place, can miss the bound.
Values may be sent and summed in bfloat16 or wider, within the bound.
No kernel may reach another device: no remote copies, remote signals or barrier semaphores. Data moves between devices by JAX's collectives and lax.ppermute only.
A program may use at most 128 MiB of HBM per device.

v0:
```python
import jax
import jax.numpy as jnp
from jax import lax
from jax.sharding import PartitionSpec as P

epsilon = 1e-06
couples = ((0, 1), (0, 2), (1, 2))
orderings = ((0, 1), (1, 0), (0, 2), (2, 0), (1, 2), (2, 1))


def normalize(embedded):
    values = embedded.astype(jnp.float32)
    length = jnp.sqrt(jnp.sum(values * values, axis=1, keepdims=True) + epsilon)
    return (values / length, length)


def contract_last(left_units, right_units):
    return lax.dot_general(
        left_units, right_units, (((1,), (1,)), ((), ())), preferred_element_type=jnp.float32
    )


def shards(
    visual_features,
    sound_features,
    tactile_features,
    visual_mapping_matrix,
    sound_mapping_matrix,
    tactile_mapping_matrix,
    couple_sharpness,
):
    inputs = (visual_features, sound_features, tactile_features)
    weights = (visual_mapping_matrix, sound_mapping_matrix, tactile_mapping_matrix)
    own_emb = [
        jnp.dot(sample, matrix, preferred_element_type=jnp.float32).astype(jnp.bfloat16)
        for sample, matrix in zip(inputs, weights)
    ]
    clip_rows = visual_features.shape[0]
    quarter = visual_mapping_matrix.shape[1]
    replicas = lax.axis_size("dp")
    emb_index = lax.axis_index("emb")
    data_index = lax.axis_index("dp")
    full_rows = (
        lax.all_gather(own_emb[0], "emb", axis=1, tiled=True),
        lax.all_gather(own_emb[1], "emb", axis=1, tiled=True),
        lax.all_gather(own_emb[2], "emb", axis=1, tiled=True),
    )
    spread = (
        lax.all_gather(own_emb[0], "dp", axis=0, tiled=True),
        lax.all_gather(own_emb[1], "dp", axis=0, tiled=True),
        lax.all_gather(own_emb[2], "dp", axis=0, tiled=True),
    )
    column_emb = (
        lax.all_to_all(spread[0], "emb", split_axis=0, concat_axis=1, tiled=True),
        lax.all_to_all(spread[1], "emb", split_axis=0, concat_axis=1, tiled=True),
        lax.all_to_all(spread[2], "emb", split_axis=0, concat_axis=1, tiled=True),
    )
    width_cols = column_emb[0].shape[0]
    positions = jnp.arange(width_cols, dtype=jnp.int32)
    column_ids = emb_index * width_cols + positions
    row_norm = [normalize(item) for item in full_rows]
    unit_rows = [normed_pair[0].astype(jnp.bfloat16) for normed_pair in row_norm]
    unit_cols = [normalize(item)[0].astype(jnp.bfloat16) for item in column_emb]
    row_ids = data_index * clip_rows + jnp.arange(clip_rows, dtype=jnp.int32)
    logit_multipliers = jnp.repeat(couple_sharpness, 2)
    scores = [
        logit_multipliers[order] * contract_last(unit_rows[source], unit_cols[target])
        for order, (source, target) in enumerate(orderings)
    ]
    partial_value = jnp.stack(
        [jnp.sum(jnp.exp(scores[order] - logit_multipliers[order]), axis=1) for order in range(6)]
    )
    totals = lax.psum(partial_value, "emb")
    row_lse = logit_multipliers[:, None] + jnp.log(totals)
    diagonal = [
        couple_sharpness[sense_couple]
        * jnp.sum(
            unit_rows[source].astype(jnp.float32) * unit_rows[target].astype(jnp.float32), axis=1
        )
        for sense_couple, (source, target) in enumerate(couples)
    ]
    local_loss = jnp.zeros((), jnp.float32)
    for order in range(6):
        local_loss = local_loss + jnp.sum(row_lse[order] - diagonal[order // 2])
    local_loss = local_loss / (2 * clip_rows * replicas)
    total_loss = lax.psum(local_loss, "dp")
    every_lse = lax.all_gather(row_lse, "dp", axis=1, tiled=True)
    column_lse = lax.dynamic_slice_in_dim(every_lse, emb_index * width_cols, width_cols, 1)
    positive = (row_ids[:, None] == column_ids[None, :]).astype(jnp.float32)
    row_grads = [jnp.zeros(full_rows[0].shape, jnp.float32) for modality in range(3)]
    for order, (source, target) in enumerate(orderings):
        partner = order ^ 1
        gradient = (
            0.5
            * (
                jnp.exp(scores[order] - row_lse[order][:, None])
                + jnp.exp(scores[order] - column_lse[partner][None, :])
            )
            - positive
        ).astype(jnp.bfloat16)
        row_grads[source] = row_grads[source] + logit_multipliers[order] * jnp.dot(
            gradient, unit_cols[target], preferred_element_type=jnp.float32
        )
    d_own = []
    shares = (
        lax.psum_scatter(row_grads[0], "emb", scatter_dimension=1, tiled=True),
        lax.psum_scatter(row_grads[1], "emb", scatter_dimension=1, tiled=True),
        lax.psum_scatter(row_grads[2], "emb", scatter_dimension=1, tiled=True),
    )
    own_units = [
        lax.dynamic_slice_in_dim(row_norm[modality][0], emb_index * quarter, quarter, 1)
        for modality in range(3)
    ]
    inner_parts = jnp.stack(
        [jnp.sum(own_units[modality] * shares[modality], axis=1) for modality in range(3)]
    )
    inner_dot = lax.psum(inner_parts, "emb")
    for modality in range(3):
        d_own.append(
            (
                (shares[modality] - own_units[modality] * inner_dot[modality][:, None])
                / row_norm[modality][1]
            ).astype(jnp.bfloat16)
        )
    stacked = lax.psum_scatter(
        jnp.concatenate(
            [
                lax.dot_general(
                    inputs[modality],
                    d_own[modality],
                    (((0,), (0,)), ((), ())),
                    preferred_element_type=jnp.float32,
                )
                for modality in range(3)
            ],
            axis=1,
        ),
        "dp",
        scatter_dimension=0,
        tiled=True,
    )
    return (
        total_loss,
        stacked[:, :quarter],
        stacked[:, quarter : 2 * quarter],
        stacked[:, 2 * quarter :],
    )


def solution(mesh):
    placed = (
        P("dp", None),
        P("dp", None),
        P("dp", None),
        P(None, "emb"),
        P(None, "emb"),
        P(None, "emb"),
        P(),
    )
    return jax.shard_map(
        shards,
        mesh=mesh,
        in_specs=placed,
        out_specs=(P(), P("dp", "emb"), P("dp", "emb"), P("dp", "emb")),
        check_vma=False,
    )
```

profile of v0, /device:TPU:32, one launch (start us, length us, event | category | flops | bytes accessed | tf_op | source)
XLA Modules:
  0.0 1487.4 jit_solution(6606972373913452857)
XLA Ops:
  7.2 1.0 copy-done
  8.3 1.9 convolution_convert_fusion.2
  10.2 2.1 convolution_convert_fusion.1
  12.3 2.1 convolution_convert_fusion
  14.4 127.4 %all-gather.6.cloned.1.call-done = bf16[8192,256]{1,0:T(8,128)(2,1)} async-done(((bf16[128,256]{1,0:T(8,128)(2,1)}), bf16[8192,256]{1,0:T(8,128)(2,1)}) %all-gather.6.cloned.1.call-update) | async-done | bytes 4194320 | tf_op jit(solution)/shard_map/all_gather | solution.py:49
  141.8 6.3 copy.21
  148.1 4.9 all-to-all-start.1
  152.9 119.9 %all-gather.4.cloned.1.call-done = bf16[8192,256]{1,0:T(8,128)(2,1)} async-done(((bf16[128,256]{1,0:T(8,128)(2,1)}), bf16[8192,256]{1,0:T(8,128)(2,1)}) %all-gather.4.cloned.1.call-update) | async-done | bytes 4194320 | tf_op jit(solution)/shard_map/all_gather | solution.py:50
  272.9 6.3 copy.20
  279.2 4.8 all-to-all-start
  284.0 119.9 %all-gather.8.cloned.1.call-done = bf16[8192,256]{1,0:T(8,128)(2,1)} async-done(((bf16[128,256]{1,0:T(8,128)(2,1)}), bf16[8192,256]{1,0:T(8,128)(2,1)}) %all-gather.8.cloned.1.call-update) | async-done | bytes 4194320 | tf_op jit(solution)/shard_map/all_gather | solution.py:51
  403.9 6.3 copy.22
  410.2 5.1 all-to-all-start.2
  415.3 0.1 broadcast_in_dim.2
  415.4 0.1 add.142
  415.5 50.1 %all_gather.26 = bf16[128,1024]{1,0:T(8,128)(2,1)S(1)} all-gather(bf16[128,256]{1,0:T(8,128)(2,1)S(1)} %copy-done.14), channel_id=1, replica_groups=mesh['dp'=64,'emb'=4] {'emb'}, dimensions={1}, use_global_device_ids=true | all-gather | bytes 327680 | tf_op jit(solution)/shard_map/all_gather | solution.py:46
  465.6 5.8 all_gather.23
  471.5 6.0 all_gather.21
  477.5 0.6 fusion.81
  478.1 0.1 fusion.14
  478.3 0.1 fusion.13
  478.4 0.1 fusion.12
  478.6 3.1 multiply_reduce_fusion.1
  481.7 3.1 multiply_reduce_fusion.2
  484.8 3.1 multiply_reduce_fusion
  487.8 3.3 fusion
  491.2 2.6 exponential_reduce_fusion.3
  493.7 3.3 fusion.2
  497.1 2.6 exponential_reduce_fusion.5
  499.7 2.5 exponential_reduce_fusion.1
  502.2 3.3 fusion.1
  505.5 1.5 exponential_reduce_fusion.4
  507.1 1.6 exponential_reduce_fusion.2
  508.8 2.6 exponential_reduce_fusion
  511.4 6.0 psum.21
  517.4 0.1 log_add_fusion
  517.5 176.7 %all_gather.27 = f32[6,8192]{1,0:T(8,128)S(1)} all-gather(f32[6,128]{1,0:T(8,128)S(1)} %log_add_fusion), channel_id=1, replica_groups=mesh['dp'=64,'emb'=4] {'dp'}, dimensions={1}, use_global_device_ids=true | all-gather | bytes 199680 | tf_op jit(solution)/shard_map/all_gather | solution.py:87
  694.2 0.2 fusion.79
  694.4 4.7 convolution_multiply_fusion.10
  699.1 3.1 fusion.3
  702.3 5.0 convolution_multiply_fusion.8
  707.3 2.9 fusion.4
  710.3 5.1 convolution_multiply_fusion.6
  715.4 3.1 fusion.5
  718.6 0.4 fusion.17
  719.0 1.0 multiply_reduce_fusion.5
  720.0 21.9 %reduce-scatter.7.cloned.1.call-done = f32[128,256]{1,0:T(8,128)} async-done(((f32[128,1024]{1,0:T(8,128)}), f32[128,256]{1,0:T(8,128)}) %reduce-scatter.7.cloned.1.call-update) | async-done | bytes 131088 | tf_op jit(solution)/shard_map/reduce_scatter | solution.py:107
  741.9 1.1 multiply_reduce_fusion.4
  743.0 23.0 %reduce-scatter.9.cloned.1.call-done = f32[128,256]{1,0:T(8,128)} async-done(((f32[128,1024]{1,0:T(8,128)}), f32[128,256]{1,0:T(8,128)}) %reduce-scatter.9.cloned.1.call-update) | async-done | bytes 131088 | tf_op jit(solution)/shard_map/reduce_scatter | solution.py:108
  766.0 1.0 multiply_reduce_fusion.3
  767.0 6.4 psum.23
  773.4 1.3 convolution_bitcast_fusion.2
  774.7 1.4 convolution_bitcast_fusion
  776.1 0.4 convolution_bitcast_fusion.1
  776.6 2.2 pad_maximum_fusion
  778.8 0.6 dynamic-slice
  779.4 0.6 fusion.80
  780.0 2.6 subtract_reduce_fusion
  787.1 179.2 %psum.22 = f32[]{:T(128)} all-reduce(f32[]{:T(128)S(6)} %div.87), channel_id=1, replica_groups=mesh['dp'=64,'emb'=4] {'dp'}, use_global_device_ids=true, to_apply=%region_22.0 | all-reduce | flops 1 | bytes 8 | tf_op jit(solution)/shard_map/psum | solution.py:86
  966.3 511.0 %all-reduce.3.cloned.1.call-done = f32[1280,768]{0,1:T(8,128)} async-done(((f32[1280,768]{0,1:T(8,128)}), f32[1280,768]{0,1:T(8,128)}) %all-reduce.3.cloned.1.call-update) | async-done | bytes 3932176
  1477.2 1.3 fusion.78
  1478.5 0.7 copy.25
  1479.2 0.7 copy.24
  1479.9 0.7 copy.23
  (65 shorter events, 0.6 us)
Async XLA Ops:
  7.2 1.1 copy-start
  7.2 134.6 %all-gather.6.cloned.1.call-start = ((), (), s32[]{:S(2)}) async-start(), calls=%async_computation.7 | async-start | bytes 4259840 | tf_op jit(solution)/shard_map/all_gather | solution.py:49
  10.1 262.7 %all-gather.4.cloned.1.call-start = ((), (), s32[]{:S(2)}) async-start(), calls=%async_computation.6 | async-start | bytes 4259840 | tf_op jit(solution)/shard_map/all_gather | solution.py:50
  12.3 391.6 %all-gather.8.cloned.1.call-start = ((), (), s32[]{:S(2)}) async-start(), calls=%async_computation.8 | async-start | bytes 4259840 | tf_op jit(solution)/shard_map/all_gather | solution.py:51
  148.1 131.1 %all-to-all-start.1 = ((bf16[4,2048,256]{1,2,0:T(8,128)(2,1)}), bf16[4,2048,256]{1,2,0:T(8,128)(2,1)}, u32[]{:S(2)}, u32[]{:S(2)}) async-start(bf16[4,2048,256]{1,2,0:T(8,128)(2,1)} %copy.21), calls=%async_computation.1 | async-start | bytes 8388608 | tf_op jit(solution)/shard_map/all_to_all | solution.py:54
  279.2 131.0 %all-to-all-start = ((bf16[4,2048,256]{1,2,0:T(8,128)(2,1)}), bf16[4,2048,256]{1,2,0:T(8,128)(2,1)}, u32[]{:S(2)}, u32[]{:S(2)}) async-start(bf16[4,2048,256]{1,2,0:T(8,128)(2,1)} %copy.20), calls=%async_computation | async-start | bytes 8388608 | tf_op jit(solution)/shard_map/all_to_all | solution.py:55
  410.2 5.2 copy-start.16
  410.2 5.3 copy-start.14
  410.2 55.5 %copy-start.13 = (bf16[128,256]{1,0:T(8,128)(2,1)S(1)}, bf16[128,256]{1,0:T(8,128)(2,1)}, u32[]{:S(2)}) copy-start(bf16[128,256]{1,0:T(8,128)(2,1)} %convolution_convert_fusion.1) | copy-start | bytes 196612
  410.2 61.3 %copy-start.12 = (bf16[128,256]{1,0:T(8,128)(2,1)S(1)}, bf16[128,256]{1,0:T(8,128)(2,1)}, u32[]{:S(2)}) copy-start(bf16[128,256]{1,0:T(8,128)(2,1)} %convolution_convert_fusion.2) | copy-start | bytes 196612
  410.2 74.6 %all-to-all-start.2 = ((bf16[4,2048,256]{1,2,0:T(8,128)(2,1)}), bf16[4,2048,256]{1,2,0:T(8,128)(2,1)}, u32[]{:S(2)}, u32[]{:S(2)}) async-start(bf16[4,2048,256]{1,2,0:T(8,128)(2,1)} %copy.22), calls=%async_computation.2 | async-start | bytes 8388608 | tf_op jit(solution)/shard_map/all_to_all | solution.py:56
  415.3 303.7 %reduce-scatter.5.cloned.1.call-start = ((), (), s32[]{:S(2)}) async-start(), calls=%async_computation.9 | async-start | bytes 655360 | tf_op jit(solution)/shard_map/reduce_scatter | solution.py:106
  491.2 8.5 copy-start.7
  497.1 11.7 copy-start.5
  505.5 3.2 copy-start.2
  517.4 181.7 %copy-start.6 = (bf16[2048,1024]{0,1:T(8,128)(2,1)S(1)}, bf16[2048,1024]{0,1:T(8,128)(2,1)}, u32[]{:S(2)}) copy-start(bf16[2048,1024]{0,1:T(8,128)(2,1)} %copy-done.5) | copy-start | bytes 12582916
  517.4 181.7 %copy-start.11 = (f32[128,2048]{1,0:T(8,128)S(1)}, f32[128,2048]{1,0:T(8,128)}, u32[]{:S(2)}) copy-start(f32[128,2048]{1,0:T(8,128)} %get-tuple-element.60) | copy-start | bytes 3145732
  702.2 39.7 %reduce-scatter.7.cloned.1.call-start = ((), (), s32[]{:S(2)}) async-start(), calls=%async_computation.10 | async-start | bytes 655360 | tf_op jit(solution)/shard_map/reduce_scatter | solution.py:107
  702.3 5.0 copy-start.3
  710.3 55.7 %reduce-scatter.9.cloned.1.call-start = ((), (), s32[]{:S(2)}) async-start(), calls=%async_computation.11 | async-start | bytes 655360 | tf_op jit(solution)/shard_map/reduce_scatter | solution.py:108
  710.3 5.1 copy-start.4
  715.4 58.0 %copy-start.8 = (bf16[128,1280]{1,0:T(8,128)(2,1)S(1)}, bf16[128,1280]{1,0:T(8,128)(2,1)}, u32[]{:S(2)}) copy-start(bf16[128,1280]{1,0:T(8,128)(2,1)} %param.7) | copy-start | bytes 983044
  718.5 56.2 %copy-start.9 = (bf16[128,1280]{1,0:T(8,128)(2,1)S(1)}, bf16[128,1280]{1,0:T(8,128)(2,1)}, u32[]{:S(2)}) copy-start(bf16[128,1280]{1,0:T(8,128)(2,1)} %param.9) | copy-start | bytes 983044
  718.5 57.6 %copy-start.10 = (bf16[128,1280]{1,0:T(8,128)(2,1)S(1)}, bf16[128,1280]{1,0:T(8,128)(2,1)}, u32[]{:S(2)}) copy-start(bf16[128,1280]{1,0:T(8,128)(2,1)} %param.8) | copy-start | bytes 983044
  718.6 758.7 %all-reduce.3.cloned.1.call-start = ((), (), s32[]{:S(2)}) async-start(), calls=%async_computation.12 | async-start | bytes 7864320
  741.9 34.2 %copy-start.15 = (f32[128,256]{1,0:T(8,128)S(1)}, f32[128,256]{1,0:T(8,128)}, u32[]{:S(2)}) copy-start(f32[128,256]{1,0:T(8,128)} %reduce-scatter.7.cloned.1.call-done) | copy-start | bytes 393220
  776.6 2.2 copy-start.17
  776.6 704.0 %copy-start.1 = (bf16[1280,256]{1,0:T(8,128)(2,1)S(1)}, bf16[1280,256]{1,0:T(8,128)(2,1)}, u32[]{:S(2)}) copy-start(bf16[1280,256]{1,0:T(8,128)(2,1)} %param.10) | copy-start | bytes 1966084
Sparse Core Ops, SparseCore 0:
  11.5 130.2 all-gather.5
  145.3 127.4 all-gather.3
  276.4 127.4 all-gather.7
  702.3 15.5 reduce-scatter.4
  720.3 21.5 reduce-scatter.6
  744.3 21.6 reduce-scatter.8
  778.9 698.2 all-reduce.2
where the time goes:
time: 1490 us
  waiting for transfers between devices  923 us (62%)
  blocking collectives  430 us (29%)
  matrix products  46.5 us (3%)
  other arithmetic  28 us (2%)
  local copies, waits for them, and re-layouts  25.5 us (2%)
  between operations  18.9 us (1%)
  starting transfers between devices  15.1 us (1%)
    unnamed x8, waiting for transfers between devices  511 us
    psum x1, blocking collectives, shards(): total_loss = lax.psum(local_loss, 'dp')  179 us
    all_gather x1, blocking collectives, shards(): every_lse = lax.all_gather(row_lse, 'dp', axis=1, tiled=True)  177 us
    all_gather x1, waiting for transfers between devices, shards(): lax.all_gather(own_emb[0], 'dp', axis=0, tiled=True)  127 us
    all_gather x1, waiting for transfers between devices, shards(): lax.all_gather(own_emb[1], 'dp', axis=0, tiled=True)  120 us
    all_gather x1, waiting for transfers between devices, shards(): lax.all_gather(own_emb[2], 'dp', axis=0, tiled=True)  120 us
    all_gather x1, blocking collectives, shards(): lax.all_gather(own_emb[2], 'emb', axis=1, tiled=True)  50.1 us
  transfers between devices with their start and end apart: 10, of which 6 were waited for; matrix products, arithmetic and copies ran while one was open for 4% of the time, Pallas kernels for 0%

commit v1 on v0

v1 whole, which is shorter than its diff:
```python
import jax
import jax.numpy as jnp
from jax import lax
from jax.sharding import Mesh, PartitionSpec as P

epsilon = 1e-06
couples = ((0, 1), (0, 2), (1, 2))
EMB = ("xl", "core")
DP = ("y", "xh", "z")
ROW = ("y", "xh", "xl")
COL = ("z", "core")
NEAR = ("y", "xl", "core")
bf16 = jnp.bfloat16
f32 = jnp.float32


def exchange(pieces, axes):
    return lax.all_to_all(pieces, axes, split_axis=0, concat_axis=0, tiled=True)


def spread(value, axes):
    count = lax.axis_size(axes)
    return exchange(jnp.broadcast_to(value[None], (count, *value.shape)), axes)


def contract(left, right, dims):
    return lax.dot_general(left, right, (dims, ((), ())), preferred_element_type=f32)


def shards(f0, f1, f2, h0, h1, h2, sharpness):
    features, heads = (f0, f1, f2), (h0, h1, h2)
    clips, feat = f0.shape
    quarter = h0.shape[1]
    emb_size = lax.axis_size(EMB)
    near_y = lax.axis_size("y")
    n_row, n_col = lax.axis_size(ROW), lax.axis_size(COL)
    own = clips // emb_size
    width = quarter * emb_size
    block_r, block_c = n_row * own, n_col * own

    slices = jnp.stack([f.reshape(clips, near_y, feat // near_y) for f in features], axis=0)
    slices = slices.transpose(2, 0, 3, 1)
    my_y = lax.axis_index("y")
    wide = [lax.dynamic_index_in_dim(slices, my_y, 0, keepdims=False)]
    for step in range(1, near_y):
        piece = lax.dynamic_index_in_dim(slices, (my_y + step) % near_y, 0, keepdims=False)
        wide.append(
            lax.ppermute(piece, "y", [(i, (i + step) % near_y) for i in range(near_y)])
        )

    emb = jnp.stack(
        [contract(f, h, ((1,), (0,))).astype(bf16) for f, h in zip(features, heads)]
    )
    emb = emb.reshape(3, emb_size, own, quarter).transpose(1, 0, 2, 3)
    emb = exchange(emb, EMB).transpose(1, 2, 0, 3).reshape(3, own, width)
    values = emb.astype(f32)
    length = jnp.sqrt(jnp.sum(values * values, axis=2, keepdims=True) + epsilon)
    unit_value = values / length
    u = lax.reduce_precision(unit_value, 8, 7)
    unit = u.astype(bf16)

    cols = lax.all_gather(unit[1:], COL, axis=0)
    rows = spread(unit[:2], ROW)
    rows, wide = lax.optimization_barrier((rows, wide))
    r0, r1 = rows[:, 0].reshape(block_r, width), rows[:, 1].reshape(block_r, width)
    c1, c2 = cols[:, 0].reshape(block_c, width), cols[:, 1].reshape(block_c, width)

    t = [sharpness[p] for p in range(3)]
    pairs = ((r0, c1), (r0, c2), (r1, c2))
    shifted = [
        jnp.exp(t[p] * contract(a, b, ((1,), (1,))) - t[p]) for p, (a, b) in enumerate(pairs)
    ]
    self_score = [
        t[p] * jnp.sum(u[a] * u[b], axis=1, keepdims=True) for p, (a, b) in enumerate(couples)
    ]
    diagonal = sum(jnp.sum(d) for d in self_score)
    row_part = jnp.stack(
        [jnp.sum(e, axis=1) for e in shifted] + [jnp.full((block_r,), diagonal)]
    )
    col_part = jnp.stack([jnp.sum(e, axis=0) for e in shifted])
    row_sum = jnp.sum(spread(row_part, ROW), axis=0)
    col_sum = jnp.sum(spread(col_part, COL), axis=0)

    scale = 1.0 / (2 * clips * lax.axis_size(DP))
    row_lse = sum(block_r * t[p] + jnp.sum(jnp.log(row_sum[p])) for p in range(3))
    col_lse = sum(block_c * t[p] + jnp.sum(jnp.log(col_sum[p])) for p in range(3))
    loss = ((row_lse - 2.0 * row_sum[3, 0]) / n_row + col_lse / n_col) * scale

    my_row, my_col = lax.axis_index(ROW), lax.axis_index(COL)
    row_id = lax.broadcasted_iota(jnp.int32, (block_r, block_c), 0) - my_row * own
    col_id = lax.broadcasted_iota(jnp.int32, (block_r, block_c), 1) - my_col * own
    other = jnp.where((row_id == col_id) & (row_id >= 0) & (row_id < own), 0.0, 1.0)
    grad = [
        (
            other * shifted[p] * (0.5 / row_sum[p][:, None] + 0.5 / col_sum[p][None, :])
        ).astype(bf16)
        for p in range(3)
    ]
    self_grad = []
    for p in range(3):
        z_row = lax.dynamic_slice_in_dim(row_sum[p], my_row * own, own, 0)[:, None]
        z_col = lax.dynamic_slice_in_dim(col_sum[p], my_col * own, own, 0)[:, None]
        e_self = jnp.exp(self_score[p] - t[p])
        g_self = e_self * (0.5 / z_row + 0.5 / z_col) - 1.0
        self_grad.append(t[p] * lax.reduce_precision(g_self, 8, 7))
    d_r0 = t[0] * contract(grad[0], c1, ((1,), (0,))) + t[1] * contract(grad[1], c2, ((1,), (0,)))
    d_r1 = t[2] * contract(grad[2], c2, ((1,), (0,)))
    d_c1 = t[0] * contract(grad[0], r0, ((0,), (0,)))
    d_c2 = t[1] * contract(grad[1], r0, ((0,), (0,))) + t[2] * contract(grad[2], r1, ((0,), (0,)))

    d_cols = jnp.stack([d_c1.reshape(n_col, own, width), d_c2.reshape(n_col, own, width)], axis=1)
    d_rows = jnp.stack([d_r0.reshape(n_row, own, width), d_r1.reshape(n_row, own, width)], axis=1)
    n_z = lax.axis_size("z")
    my_core = lax.axis_index("core")
    d_cols = d_cols.reshape(n_z, 2, 2 * own, width)
    mine = lax.dynamic_index_in_dim(d_cols, my_core, 1, keepdims=False)
    theirs = lax.dynamic_index_in_dim(d_cols, 1 - my_core, 1, keepdims=False)
    mine = mine + lax.ppermute(theirs, "core", [(0, 1), (1, 0)])
    d_cols = lax.psum_scatter(mine, "z", scatter_dimension=0).reshape(2, own, width)
    d_rows = jnp.sum(exchange(d_rows.astype(bf16), ROW).astype(f32), axis=0)
    d_unit = jnp.stack(
        [
            d_rows[0] + self_grad[0] * u[1] + self_grad[1] * u[2],
            d_rows[1] + d_cols[0] + self_grad[0] * u[0] + self_grad[2] * u[2],
            d_cols[1] + self_grad[1] * u[0] + self_grad[2] * u[1],
        ]
    )

    inner = jnp.sum(unit_value * d_unit, axis=2, keepdims=True)
    d_emb = ((d_unit - unit_value * inner) / length).astype(bf16)

    parts = []
    rest = loss
    for _ in range(3):
        part = lax.reduce_precision(rest, 8, 7)
        parts.append(part.astype(bf16))
        rest = rest - part
    tail = jnp.stack(parts + [jnp.zeros((), bf16)] * 13)
    tail = jnp.broadcast_to(tail[:, None], (16, quarter))
    d_emb = d_emb.reshape(3 * own, emb_size, quarter).transpose(1, 0, 2)
    d_emb = jnp.concatenate(
        [d_emb, jnp.broadcast_to(tail[None], (emb_size, 16, quarter))], axis=1
    )
    height = d_emb.shape[1]
    d_emb = jnp.broadcast_to(d_emb[None], (near_y, *d_emb.shape))
    d_emb = exchange(d_emb.reshape(near_y * emb_size, height, quarter), NEAR)
    loss = jnp.sum(d_emb[:, 3 * own : 3 * own + 3, 0].astype(f32))
    d_emb = d_emb.reshape(near_y, emb_size, height, quarter)
    partial = []
    for m in range(3):
        total = jnp.zeros((feat // near_y, quarter), f32)
        for step in range(near_y):
            source = (my_y - step) % near_y
            there = lax.dynamic_index_in_dim(d_emb, source, 0, keepdims=False)
            there = there[:, m * own : (m + 1) * own].reshape(clips, quarter)
            total = total + contract(wide[step][m], there, ((1,), (0,)))
        partial.append(total)

    n_x = lax.axis_size("xh")
    share = feat // near_y // n_x // n_z
    partial = jnp.stack([p.reshape(n_x, n_z, share, quarter) for p in partial], axis=2)
    partial = partial.reshape(n_x, n_z, 3 * share, quarter)
    extra = jnp.broadcast_to(loss, (n_x, n_z, 4, quarter))
    partial = jnp.concatenate([partial, extra], axis=2)
    my_x = lax.axis_index("xh")
    kept = lax.dynamic_index_in_dim(partial, my_x, 0, keepdims=False)
    sent = lax.dynamic_index_in_dim(partial, 1 - my_x, 0, keepdims=False)
    kept = kept + lax.ppermute(sent, "xh", [(0, 1), (1, 0)])
    kept = jnp.sum(exchange(kept, "z"), axis=0)
    out = kept[: 3 * share].reshape(3, share, quarter)
    return kept[3 * share, 0], out[0], out[1], out[2]


def solution(mesh):
    fine = Mesh(mesh.devices.reshape(4, 2, 8, 2, 2), ("y", "xh", "z", "xl", "core"))
    clip_rows, columns = P(DP, None), P(None, EMB)
    out = P(DP, EMB)
    return jax.shard_map(
        shards,
        mesh=fine,
        in_specs=(clip_rows,) * 3 + (columns,) * 3 + (P(),),
        out_specs=(P(), out, out, out),
        check_vma=False,
    )
```

time: 1490 us -> 256 us (0.17)
  waiting for transfers between devices: 923 us -> 85.4 us
  blocking collectives: 430 us -> 27.2 us
  starting transfers between devices: 15.1 us -> 34.9 us
    unnamed x8 -> x2, waiting for transfers between devices: 511 us -> 0.03 us
    all_gather x3 -> x1, waiting for transfers between devices: 367 us -> 0.01 us  [shards(): cols = lax.all_gather(unit[1:], COL, axis=0)]
    all_gather x4 -> x0, blocking collectives: 239 us -> none  [the longest x1 177 us: shards(): every_lse = lax.all_gather(row_lse, 'dp', axis=1, tiled=True)]
    psum x3 -> x0, blocking collectives: 192 us -> none  [the longest x1 179 us: shards(): total_loss = lax.psum(local_loss, 'dp')]
    all_to_all x3 -> x5, waiting for transfers between devices: 0.01 us -> 50.4 us  [exchange(): return lax.all_to_all(pieces, axes, split_axis=0, concat_axis=0, tiled=True)]
    reduce_scatter x3 -> x1, waiting for transfers between devices: 44.9 us -> 0.01 us  [shards(): lax.psum_scatter(mine, 'z', scatter_dimension=0).reshape(2, own, width)]
    ppermute x0 -> x5, waiting for transfers between devices: none -> 35 us  [the longest x3 17.4 us: shards(): lax.ppermute(piece, 'y', [(i, (i + step) % near_y) for i in range(near_y)])]
    all_to_all x0 -> x2, blocking collectives: none -> 27.2 us  [exchange(): return lax.all_to_all(pieces, axes, split_axis=0, concat_axis=0, tiled=True)]
  transfers between devices with their start and end apart: 10 -> 12, of which waited for: 6 -> 8; matrix products, arithmetic and copies ran while one was open for 4% -> 11% of each run, Pallas kernels for 0% -> 0%
where the time goes in v1:
time: 256 us; the launch traced here: 253 us
  waiting for transfers between devices  85.4 us (33%)
  starting transfers between devices  34.9 us (14%)
  matrix products  33.6 us (13%)
  blocking collectives  27.2 us (11%)
  between operations  26.9 us (11%)
  local copies, waits for them, and re-layouts  25 us (10%)
  other arithmetic  20 us (8%)
    all_to_all x5, waiting for transfers between devices, exchange(): return lax.all_to_all(pieces, axes, split_axis=0, concat_axis=0, tiled=True)  50.4 us
    dot_general x24, matrix products, contract(): lax.dot_general(left, right, (dims, ((), ())), preferred_element_type=f32)  33.6 us
    all_to_all x5, starting transfers between devices, exchange(): return lax.all_to_all(pieces, axes, split_axis=0, concat_axis=0, tiled=True)  27.8 us
    all_to_all x2, blocking collectives, exchange(): return lax.all_to_all(pieces, axes, split_axis=0, concat_axis=0, tiled=True)  27.2 us
    ppermute x3, waiting for transfers between devices, shards(): lax.ppermute(piece, 'y', [(i, (i + step) % near_y) for i in range(near_y)])  17.4 us
    ppermute x1, waiting for transfers between devices, shards(): kept = kept + lax.ppermute(sent, 'xh', [(0, 1), (1, 0)])  13.5 us
    unnamed x34, local copies, waits for them, and re-layouts  9.49 us
  transfers between devices with their start and end apart: 12, of which 8 were waited for; matrix products, arithmetic and copies ran while one was open for 11% of the time, Pallas kernels for 0%

profile of v1, /device:TPU:32, one launch (start us, length us, event | category | flops | bytes accessed | tf_op | source)
XLA Modules:
  0.0 253.0 jit_solution(3074164570225719456)
XLA Ops:
  7.2 1.0 copy-done
  8.3 1.2 convolution_convert_fusion.2
  9.5 1.4 convolution_convert_fusion.1
  11.3 7.9 %all_to_all.35 = bf16[4,3,32,256]{3,2,1,0:T(8,128)(2,1)S(1)} all-to-all(bf16[4,3,32,256]{3,2,1,0:T(8,128)(2,1)S(1)} %maximum_bitcast_fusion), channel_id=1, replica_groups=mesh['y'=4,'xh'=2,'z'=8,'xl'=2,'core'=2] {'xl','core'}, dimensions={0} | all-to-all | bytes 393216 | tf_op jit(solution)/shard_map/all_to_all | solution.py:18
  20.2 1.6 broadcast_in_dim.14
  21.8 6.8 %all-to-all-start.1 = ((bf16[16,2,32,1024]{3,2,1,0:T(8,128)(2,1)}), bf16[16,2,32,1024]{3,2,1,0:T(8,128)(2,1)S(1)}, u32[]{:S(2)}, u32[]{:S(2)}) async-start(bf16[16,2,32,1024]{3,2,1,0:T(8,128)(2,1)} %broadcast_in_dim.14), calls=%async_computation.1 | async-start | bytes 4194304 | tf_op jit(solution)/shard_map/all_to_all | solution.py:18
  28.7 1.9 copy.145
  30.6 1.9 copy.146
  32.4 1.9 copy.147
  34.3 1.3 pad_maximum_fusion.3
  35.6 1.0 dynamic-slice_bitcast_fusion.1
  36.6 3.1 %collective-permute-start.2 = (bf16[3,320,128]{2,1,0:T(8,128)(2,1)}, bf16[3,320,128]{2,1,0:T(8,128)(2,1)}, u32[]{:S(2)}, u32[]{:S(2)}) collective-permute-start(bf16[3,320,128]{2,1,0:T(8,128)(2,1)} %get-tuple-element.37), channel_id=1, source_target_pairs={{0,192},{64,0},{128,64},{192,128},{1,193},{65,1},{129,65},{193,129... | collective-permute-start | bytes 737288 | tf_op jit(solution)/shard_map/ppermute | solution.py:48
  39.7 0.9 collective-permute-start.1
  40.5 0.9 collective-permute-start
  42.2 1.3 multiply_reduce_fusion.6
  43.4 1.3 multiply_reduce_fusion.5
  46.1 1.2 multiply_reduce_fusion.4
  48.0 12.2 %collective-permute-done.2 = bf16[3,320,128]{2,1,0:T(8,128)(2,1)} collective-permute-done((bf16[3,320,128]{2,1,0:T(8,128)(2,1)}, bf16[3,320,128]{2,1,0:T(8,128)(2,1)}, u32[]{:S(2)}, u32[]{:S(2)}) %collective-permute-start.2) | collective-permute-done | bytes 245792 | tf_op jit(solution)/shard_map/ppermute | solution.py:48
  60.2 5.2 %collective-permute-done = bf16[3,320,128]{2,1,0:T(8,128)(2,1)} collective-permute-done((bf16[3,320,128]{2,1,0:T(8,128)(2,1)}, bf16[3,320,128]{2,1,0:T(8,128)(2,1)}, u32[]{:S(2)}, u32[]{:S(2)}) %collective-permute-start) | collective-permute-done | bytes 245792 | tf_op jit(solution)/shard_map/ppermute | solution.py:48
  65.4 1.5 fusion.72
  66.9 1.8 fusion.71
  68.8 2.6 %fusion.69 = (f32[512]{0:T(512)S(1)}, f32[512]{0:T(512)S(1)}, f32[512,512]{1,0:T(8,128)}) fusion(bf16[512,1024]{1,0:T(8,128)(2,1)S(1)} %bitcast.226, bf16[512,1024]{1,0:T(8,128)(2,1)S(1)} %bitcast.239, f32[]{:T(128)} %bitcast.28), kind=kOutput, calls=%fused_computation.155 | convolution fusion | flops 537918464 | bytes 3149828 | tf_op jit(solution)/shard_map/dot_general | solution.py:27
  71.4 2.4 fusion.68
  73.8 2.4 fusion.67
  77.0 5.0 %all-to-all-start.2 = ((f32[16,4,512]{2,1,0:T(4,128)}), f32[16,4,512]{2,1,0:T(4,128)S(1)}, u32[]{:S(2)}, u32[]{:S(2)}) async-start(f32[16,4,512]{2,1,0:T(4,128)} %broadcast_in_dim.17), calls=%async_computation.2 | async-start | bytes 262144 | tf_op jit(solution)/shard_map/all_to_all | solution.py:18
  82.0 8.0 %all-to-all-done.2 = f32[16,4,512]{2,1,0:T(4,128)S(1)} async-done(((f32[16,4,512]{2,1,0:T(4,128)}), f32[16,4,512]{2,1,0:T(4,128)S(1)}, u32[]{:S(2)}, u32[]{:S(2)}) %all-to-all-start.2) | async-done | bytes 131104 | tf_op jit(solution)/shard_map/all_to_all | solution.py:18
  90.6 8.6 %all-to-all-start.3 = ((f32[16,3,512]{2,1,0:T(4,128)}), f32[16,3,512]{2,1,0:T(4,128)}, u32[]{:S(2)}, u32[]{:S(2)}) async-start(f32[16,3,512]{2,1,0:T(4,128)} %broadcast_in_dim.20), calls=%async_computation.3 | async-start | bytes 262144 | tf_op jit(solution)/shard_map/all_to_all | solution.py:18
  100.0 6.7 %all-to-all-done.3 = f32[16,3,512]{2,1,0:T(4,128)} async-done(((f32[16,3,512]{2,1,0:T(4,128)}), f32[16,3,512]{2,1,0:T(4,128)}, u32[]{:S(2)}, u32[]{:S(2)}) %all-to-all-start.3) | async-done | bytes 98336 | tf_op jit(solution)/shard_map/all_to_all | solution.py:18
  106.7 0.9 reduce_sum.239
  108.3 3.3 %convolution_multiply_fusion = f32[512,1024]{1,0:T(8,128)S(1)} fusion(bf16[512,1024]{1,0:T(8,128)(2,1)} %bitcast.243, f32[]{:T(128)} %bitcast.20, f32[512,512]{1,0:T(8,128)} %get-tuple-element.82, f32[512]{0:T(512)S(1)} %bitcast.273, f32[512]{0:T(512)S(1)} %bitcast.269, s32[512]{0:T(512)S(1)} %get-tuple-element.87, s32[512]{0:T(512)S(1)} %get-tuple-element.88, ...), kind=kOutput, calls=%fused_computation.11 | convolution fusion | flops 539492352 | bytes 4203524 | tf_op jit(solution)/shard_map/dot_general | solution.py:27
  111.6 1.0 fusion.61
  112.8 2.3 multiply_add_fusion
  115.8 1.6 dynamic-slice_bitcast_fusion
  117.4 1.0 copy-done.1
  119.0 4.1 %collective-permute-done.3 = f32[8,64,1024]{2,1,0:T(8,128)} collective-permute-done((f32[8,64,1024]{2,1,0:T(8,128)}, f32[8,64,1024]{2,1,0:T(8,128)}, u32[]{:S(2)}, u32[]{:S(2)}) %collective-permute-start.3) | collective-permute-done | bytes 2097184 | tf_op jit(solution)/shard_map/ppermute | solution.py:118
  123.1 4.1 %bitcast_add_fusion = f32[8,64,1024]{2,1,0:T(8,128)} fusion(f32[8,64,1024]{2,1,0:T(8,128)} %collective-permute-done.3, f32[8,2,64,1024]{3,2,1,0:T(8,128)} %bitcast.222, s32[]{:T(128)S(6)} %select_n.119), kind=kLoop, calls=%fused_computation.3 | loop fusion | flops 524288 | bytes 6291460 | tf_op jit(solution)/shard_map/add | solution.py:118
  127.3 1.2 copy-done.6
  128.5 2.9 %multiply_convert_fusion = bf16[512,1024]{1,0:T(8,128)(2,1)S(1)} fusion(bf16[512,1024]{1,0:T(8,128)(2,1)S(1)} %bitcast.241, f32[]{:T(128)} %bitcast.28, f32[512,512]{1,0:T(8,128)} %get-tuple-element.80, f32[512]{0:T(512)S(1)} %bitcast.276, f32[512]{0:T(512)S(1)} %bitcast.272, s32[512]{0:T(512)S(1)} %get-tuple-element.87, s32[512]{0:T(512)S(1)} %get-tuple-element.88, ...), kind=kOutput, calls=%fused_computation.6 | convolution fusion | flops 540016640 | bytes 3154948 | tf_op jit(solution)/shard_map/dot_general | solution.py:27
  131.4 1.0 fusion.65
  132.6 2.6 %add_convert_fusion = bf16[512,1024]{1,0:T(8,128)(2,1)S(1)} fusion(f32[512,1024]{1,0:T(8,128)S(1)} %fusion.65, bf16[512,1024]{1,0:T(8,128)(2,1)S(1)} %bitcast.242, f32[]{:T(128)} %bitcast.25, f32[]{:T(128)} %bitcast.20, f32[512,512]{1,0:T(8,128)S(1)} %copy-done.14, f32[512]{0:T(512)S(1)} %bitcast.280, f32[512]{0:T(512)S(1)} %bitcast.278, ...), kind=kOutput, calls=%fused_computation.7 | convolution fusion | flops 541065216 | bytes 5252104 | tf_op jit(solution)/shard_map/dot_general | solution.py:27
  135.2 1.5 pad_maximum_fusion.1
  136.8 3.7 %all-to-all-start.4 = ((bf16[16,2,32,1024]{3,2,1,0:T(8,128)(2,1)}), bf16[16,2,32,1024]{3,2,1,0:T(8,128)(2,1)S(1)}, u32[]{:S(2)}, u32[]{:S(2)}) async-start(bf16[16,2,32,1024]{3,2,1,0:T(8,128)(2,1)} %pad_maximum_fusion.1), calls=%async_computation.4 | async-start | bytes 4194304 | tf_op jit(solution)/shard_map/all_to_all | solution.py:18
  151.3 0.7 stack.101
  152.1 0.7 fusion.58
  152.8 1.4 fusion.56
  154.2 20.6 %all-to-all-done.4 = bf16[16,2,32,1024]{3,2,1,0:T(8,128)(2,1)S(1)} async-done(((bf16[16,2,32,1024]{3,2,1,0:T(8,128)(2,1)}), bf16[16,2,32,1024]{3,2,1,0:T(8,128)(2,1)S(1)}, u32[]{:S(2)}, u32[]{:S(2)}) %all-to-all-start.4) | async-done | bytes 2097184 | tf_op jit(solution)/shard_map/all_to_all | solution.py:18
  174.9 1.1 convert_reduce_fusion
  175.9 1.2 fusion.20
  178.1 1.0 broadcast_in_dim.21
  179.1 3.6 %all-to-all-start.5 = ((bf16[16,112,256]{2,1,0:T(8,128)(2,1)}), bf16[16,112,256]{2,1,0:T(8,128)(2,1)S(1)}, u32[]{:S(2)}, u32[]{:S(2)}) async-start(bf16[16,112,256]{2,1,0:T(8,128)(2,1)} %bitcast.61), calls=%async_computation.6 | async-start | bytes 1835008 | tf_op jit(solution)/shard_map/all_to_all | solution.py:18
  182.8 15.0 %all-to-all-done.5 = bf16[16,112,256]{2,1,0:T(8,128)(2,1)S(1)} async-done(((bf16[16,112,256]{2,1,0:T(8,128)(2,1)}), bf16[16,112,256]{2,1,0:T(8,128)(2,1)S(1)}, u32[]{:S(2)}, u32[]{:S(2)}) %all-to-all-start.5) | async-done | bytes 917536 | tf_op jit(solution)/shard_map/all_to_all | solution.py:18
  198.9 1.1 convolution_add_fusion.2
  200.0 1.1 convolution_add_fusion.1
  201.1 1.1 convolution_add_fusion
  202.5 1.1 convolution_add_fusion.5
  203.6 1.1 convolution_add_fusion.4
  204.7 1.1 convolution_add_fusion.3
  205.8 1.1 convolution_add_fusion.8
  206.9 1.1 convolution_add_fusion.7
  207.9 1.1 convolution_add_fusion.6
  209.5 0.7 pad_dynamic-slice_fusion.1
  210.4 1.6 collective-permute-start.4
  212.0 13.5 %collective-permute-done.4 = f32[8,64,256]{2,1,0:T(8,128)S(1)} collective-permute-done((f32[8,64,256]{2,1,0:T(8,128)S(1)}, f32[8,64,256]{2,1,0:T(8,128)S(1)}, u32[]{:S(2)}, u32[]{:S(2)}) %collective-permute-start.4) | collective-permute-done | bytes 524320 | tf_op jit(solution)/shard_map/ppermute | solution.py:168
  225.6 19.3 %all_to_all.36 = f32[8,64,256]{2,1,0:T(8,128)S(1)} all-to-all(f32[8,64,256]{2,1,0:T(8,128)S(1)} %bitcast_add_fusion.1), channel_id=1, replica_groups=mesh['y'=4,'xh'=2,'z'=8,'xl'=2,'core'=2] {'z'}, dimensions={0} | all-to-all | bytes 1048576 | tf_op jit(solution)/shard_map/all_to_all | solution.py:18
  (92 shorter events, 11.7 us)
Async XLA Ops:
  7.2 1.1 copy-start
  7.2 3.8 %copy-start.3 = (bf16[128,1280]{1,0:T(8,128)(2,1)S(1)}, bf16[128,1280]{1,0:T(8,128)(2,1)}, u32[]{:S(2)}) copy-start(bf16[128,1280]{1,0:T(8,128)(2,1)} %param.9) | copy-start | bytes 983044
  7.2 3.8 %copy-start.11 = (bf16[1280,256]{1,0:T(8,128)(2,1)S(1)}, bf16[1280,256]{1,0:T(8,128)(2,1)}, u32[]{:S(2)}) copy-start(bf16[1280,256]{1,0:T(8,128)(2,1)} %param.12) | copy-start | bytes 1966084
  7.2 59.7 %all-gather.3.cloned.1.call-start = ((), (), s32[]{:S(2)}) async-start(), calls=%async_computation.9 | async-start | bytes 2228224 | tf_op jit(solution)/shard_map/all_gather | solution.py:62
  21.8 43.6 %all-to-all-start.1 = ((bf16[16,2,32,1024]{3,2,1,0:T(8,128)(2,1)}), bf16[16,2,32,1024]{3,2,1,0:T(8,128)(2,1)S(1)}, u32[]{:S(2)}, u32[]{:S(2)}) async-start(bf16[16,2,32,1024]{3,2,1,0:T(8,128)(2,1)} %broadcast_in_dim.14), calls=%async_computation.1 | async-start | bytes 4194304 | tf_op jit(solution)/shard_map/all_to_all | solution.py:18
  34.3 7.1 %copy-start.12 = (f32[3]{0:T(128)S(1)}, f32[3]{0:T(128)}, u32[]{:S(2)}) copy-start(f32[3]{0:T(128)} %param.13) | copy-start | bytes 40
  36.6 23.6 %collective-permute-start.2 = (bf16[3,320,128]{2,1,0:T(8,128)(2,1)}, bf16[3,320,128]{2,1,0:T(8,128)(2,1)}, u32[]{:S(2)}, u32[]{:S(2)}) collective-permute-start(bf16[3,320,128]{2,1,0:T(8,128)(2,1)} %get-tuple-element.37), channel_id=1, source_target_pairs={{0,192},{64,0},{128,64},{192,128},{1,193},{65,1},{129,65},{193,129... | collective-permute-start | bytes 737288 | tf_op jit(solution)/shard_map/ppermute | solution.py:48
  39.7 20.5 %collective-permute-start.1 = (bf16[3,320,128]{2,1,0:T(8,128)(2,1)}, bf16[3,320,128]{2,1,0:T(8,128)(2,1)}, u32[]{:S(2)}, u32[]{:S(2)}) collective-permute-start(bf16[3,320,128]{2,1,0:T(8,128)(2,1)} %get-tuple-element.38), channel_id=1, source_target_pairs={{0,128},{64,192},{128,0},{192,64},{1,129},{65,193},{129,1},{193,65... | collective-permute-start | bytes 737288 | tf_op jit(solution)/shard_map/ppermute | solution.py:48
  40.5 24.9 %collective-permute-start = (bf16[3,320,128]{2,1,0:T(8,128)(2,1)}, bf16[3,320,128]{2,1,0:T(8,128)(2,1)}, u32[]{:S(2)}, u32[]{:S(2)}) collective-permute-start(bf16[3,320,128]{2,1,0:T(8,128)(2,1)} %get-tuple-element.39), channel_id=1, source_target_pairs={{0,64},{64,128},{128,192},{192,0},{1,65},{65,129},{129,193},{193,1... | collective-permute-start | bytes 737288 | tf_op jit(solution)/shard_map/ppermute | solution.py:48
  66.9 1.9 copy-start.2
  68.8 2.6 %copy-start.5 = (bf16[16,1,32,1024]{3,2,1,0:T(8,128)(2,1)}, bf16[16,1,32,1024]{3,2,1,0:T(8,128)(2,1)S(1)}, u32[]{:S(2)}) copy-start(bf16[16,1,32,1024]{3,2,1,0:T(8,128)(2,1)S(1)} %get-tuple-element.32) | copy-start | bytes 3145732
  68.8 2.6 %copy-start.8 = (bf16[16,1,32,1024]{3,2,1,0:T(8,128)(2,1)S(1)}, bf16[16,1,32,1024]{3,2,1,0:T(8,128)(2,1)}, u32[]{:S(2)}) copy-start(bf16[16,1,32,1024]{3,2,1,0:T(8,128)(2,1)} %get-tuple-element.34) | copy-start | bytes 3145732
  77.0 13.0 %all-to-all-start.2 = ((f32[16,4,512]{2,1,0:T(4,128)}), f32[16,4,512]{2,1,0:T(4,128)S(1)}, u32[]{:S(2)}, u32[]{:S(2)}) async-start(f32[16,4,512]{2,1,0:T(4,128)} %broadcast_in_dim.17), calls=%async_computation.2 | async-start | bytes 262144 | tf_op jit(solution)/shard_map/all_to_all | solution.py:18
  90.6 16.1 %all-to-all-start.3 = ((f32[16,3,512]{2,1,0:T(4,128)}), f32[16,3,512]{2,1,0:T(4,128)}, u32[]{:S(2)}, u32[]{:S(2)}) async-start(f32[16,3,512]{2,1,0:T(4,128)} %broadcast_in_dim.20), calls=%async_computation.3 | async-start | bytes 262144 | tf_op jit(solution)/shard_map/all_to_all | solution.py:18
  99.2 76.7 %reduce-scatter.2.cloned.1.call-start = ((), (), s32[]{:S(2)}) async-start(), calls=%async_computation.8 | async-start | bytes 2359296 | tf_op jit(solution)/shard_map/reduce_scatter | solution.py:119
  108.3 3.3 %copy-start.9 = (bf16[16,1,32,1024]{3,2,1,0:T(8,128)(2,1)S(1)}, bf16[16,1,32,1024]{3,2,1,0:T(8,128)(2,1)}, u32[]{:S(2)}) copy-start(bf16[16,1,32,1024]{3,2,1,0:T(8,128)(2,1)} %get-tuple-element.34) | copy-start | bytes 3145732
  108.3 3.3 %copy-start.13 = (f32[512,512]{1,0:T(8,128)S(1)}, f32[512,512]{1,0:T(8,128)}, u32[]{:S(2)}) copy-start(f32[512,512]{1,0:T(8,128)} %get-tuple-element.81) | copy-start | bytes 3145732
  111.6 1.2 copy-start.7
  115.8 2.6 %copy-start.1 = (f32[16,2,32,1024]{3,2,1,0:T(8,128)}, f32[16,2,32,1024]{3,2,1,0:T(8,128)S(1)}, u32[]{:S(2)}) copy-start(f32[16,2,32,1024]{3,2,1,0:T(8,128)S(1)} %pad_maximum_fusion) | copy-start | bytes 12582916
  118.4 4.8 %collective-permute-start.3 = (f32[8,64,1024]{2,1,0:T(8,128)}, f32[8,64,1024]{2,1,0:T(8,128)}, u32[]{:S(2)}, u32[]{:S(2)}) collective-permute-start(f32[8,64,1024]{2,1,0:T(8,128)} %dynamic-slice_bitcast_fusion), channel_id=1, source_target_pairs={{0,1},{1,0},{2,3},{3,2},{4,5},{5,4},{6,7},{7,6},{8,9},{9,8},{10,11... | collective-permute-start | bytes 6291464 | tf_op jit(solution)/shard_map/ppermute | solution.py:118
  127.2 1.2 copy-start.6
  128.5 2.9 %copy-start.4 = (f32[512,512]{1,0:T(8,128)S(1)}, f32[512,512]{1,0:T(8,128)}, u32[]{:S(2)}) copy-start(f32[512,512]{1,0:T(8,128)} %get-tuple-element.82) | copy-start | bytes 3145732
  131.4 1.2 copy-start.14
  136.8 38.1 %all-to-all-start.4 = ((bf16[16,2,32,1024]{3,2,1,0:T(8,128)(2,1)}), bf16[16,2,32,1024]{3,2,1,0:T(8,128)(2,1)S(1)}, u32[]{:S(2)}, u32[]{:S(2)}) async-start(bf16[16,2,32,1024]{3,2,1,0:T(8,128)(2,1)} %pad_maximum_fusion.1), calls=%async_computation.4 | async-start | bytes 4194304 | tf_op jit(solution)/shard_map/all_to_all | solution.py:18
  179.1 18.8 %all-to-all-start.5 = ((bf16[16,112,256]{2,1,0:T(8,128)(2,1)}), bf16[16,112,256]{2,1,0:T(8,128)(2,1)S(1)}, u32[]{:S(2)}, u32[]{:S(2)}) async-start(bf16[16,112,256]{2,1,0:T(8,128)(2,1)} %bitcast.61), calls=%async_computation.6 | async-start | bytes 1835008 | tf_op jit(solution)/shard_map/all_to_all | solution.py:18
  182.7 16.0 %copy-start.10 = (bf16[3,320,128]{2,1,0:T(8,128)(2,1)S(1)}, bf16[3,320,128]{2,1,0:T(8,128)(2,1)}, u32[]{:S(2)}) copy-start(bf16[3,320,128]{2,1,0:T(8,128)(2,1)} %get-tuple-element.9) | copy-start | bytes 737284
  210.4 15.0 %collective-permute-start.4 = (f32[8,64,256]{2,1,0:T(8,128)S(1)}, f32[8,64,256]{2,1,0:T(8,128)S(1)}, u32[]{:S(2)}, u32[]{:S(2)}) collective-permute-start(f32[8,64,256]{2,1,0:T(8,128)S(1)} %bitcast.250), channel_id=1, source_target_pairs={{0,32},{32,0},{1,33},{33,1},{2,34},{34,2},{3,35},{35,3},{4,36},{36... | collective-permute-start | bytes 1572872 | tf_op jit(solution)/shard_map/ppermute | solution.py:168
Sparse Core Ops, SparseCore 0:
  20.3 41.5 all-gather.2
  127.4 36.0 reduce-scatter.1

commit v2 on v1

v2 whole, which is shorter than its diff:
```python
import functools

import jax
import jax.numpy as jnp
import numpy as np
from jax import lax
from jax.experimental import pallas as pl
from jax.experimental.pallas import tpu as pltpu
from jax.sharding import Mesh, PartitionSpec as P

epsilon = 1e-06
couples = ((0, 1), (0, 2), (1, 2))
EMB = ("xl", "core")
DP = ("y", "xh", "z")
ROW = ("y", "xh", "xl")
COL = ("z", "core")
NEAR = ("y", "xl", "core")
FAR = ("xh", "z")
bf16 = jnp.bfloat16
f32 = jnp.float32
LANES = 128
TILE = 128
SCORE_TILE = 256


def exchange(pieces, axes):
    return lax.all_to_all(pieces, axes, split_axis=0, concat_axis=0, tiled=True)


def spread(value, axes):
    count = lax.axis_size(axes)
    return exchange(jnp.broadcast_to(value[None], (count, *value.shape)), axes)


def contract(left, right, dims):
    return lax.dot_general(left, right, (dims, ((), ())), preferred_element_type=f32)


def call(kernel, grid, in_specs, out_specs, out_shape, scratch=(), flops=0, room=32):
    return pl.pallas_call(
        kernel,
        grid=grid,
        in_specs=in_specs,
        out_specs=out_specs,
        out_shape=out_shape,
        scratch_shapes=scratch,
        compiler_params=pltpu.CompilerParams(vmem_limit_bytes=room * 2**20),
        cost_estimate=pl.CostEstimate(flops=flops, bytes_accessed=8 * 2**20, transcendentals=0),
    )


def whole(shape):
    return pl.BlockSpec(shape, lambda *_: (0,) * len(shape))


scalars = pl.BlockSpec(memory_space=pltpu.SMEM)


def share_kernel(share, line, at_ref, f0_ref, f1_ref, f2_ref, own_ref, *send_refs):
    n_y = 1 + len(send_refs)
    rows, feat = own_ref.shape[2], f0_ref.shape[1]
    r = lax.broadcasted_iota(jnp.int32, (rows, 1), 0)
    place = r // line
    inside = r - place * line < share
    column = lax.broadcasted_iota(jnp.int32, (rows, feat), 1)
    jobs = [(own_ref.at[x], 0, x) for x in range(2)]
    jobs += [(ref, step, at_ref[2]) for step, ref in enumerate(send_refs, 1)]
    for ref, step, x in jobs:
        start = (2 * lax.rem(at_ref[3] + step, n_y) + x) * (feat // n_y // 2)
        target = jnp.where(inside, r - place * (line - share) + start, -1)
        pick = jnp.where(column == target, 1.0, 0.0).astype(bf16)
        for m, f_ref in enumerate((f0_ref, f1_ref, f2_ref)):
            ref[m] = contract(pick, f_ref[...], ((1,), (1,))).astype(bf16)


def feature_shares(at, features, n_y, n_z, line):
    clips, feat = features[0].shape
    share = feat // n_y // n_z // 2
    shape = (3, n_z * line, clips)
    shapes = [(2, *shape)] + [shape] * (n_y - 1)
    return call(
        functools.partial(share_kernel, share, line),
        (1,),
        [scalars] + [whole(f.shape) for f in features],
        [whole(x) for x in shapes],
        [jax.ShapeDtypeStruct(x, bf16) for x in shapes],
        flops=6 * n_y * n_z * line * feat * clips,
    )(at, *features)


def unit_kernel(t_ref, emb_ref, all_ref, unit_ref, rows_ref, cols_ref, own_ref):
    parts, _, own, quarter = emb_ref.shape
    for m in range(3):
        emb = jnp.concatenate([emb_ref[e, m] for e in range(parts)], axis=1)
        values = emb.astype(f32)
        length = jnp.sqrt(jnp.sum(values * values, axis=1, keepdims=True) + epsilon)
        unit = (values / length).astype(bf16)
        all_ref[m] = emb
        unit_ref[m] = unit
        if m > 0:
            cols_ref[m - 1] = unit
        if m < 2:
            for copy in range(rows_ref.shape[0]):
                rows_ref[copy, m] = unit
    total = jnp.zeros((1, parts * quarter), f32)
    for p, (a, b) in enumerate(couples):
        product = unit_ref[a].astype(f32) * unit_ref[b].astype(f32)
        total += t_ref[p] * jnp.sum(product, axis=0, keepdims=True)
    own_ref[...] = jnp.broadcast_to(jnp.sum(total, axis=1, keepdims=True), own_ref.shape)


def units(t, emb, copies):
    parts, _, own, quarter = emb.shape
    full = (3, own, parts * quarter)
    shapes = [full, full, (copies, 2, *full[1:]), (2, *full[1:])]
    return call(
        unit_kernel,
        (1,),
        [scalars, whole(emb.shape)],
        [whole(x) for x in shapes] + [whole((8, LANES))],
        [jax.ShapeDtypeStruct(x, bf16) for x in shapes] + [jax.ShapeDtypeStruct((8, LANES), f32)],
        flops=10**6,
    )(t, emb)


def score_kernel(t_ref, rows_ref, cols_ref, own_ref, e_ref, row_ref, col_ref):
    step = pl.program_id(0)
    own, width = rows_ref.shape[2], rows_ref.shape[3]
    rows = [rows_ref[:, m].reshape(SCORE_TILE, width) for m in range(2)]
    cols = [cols_ref[:, m].reshape(cols_ref.shape[0] * own, width) for m in range(2)]

    @pl.when(step == 0)
    def _():
        col_ref[...] = jnp.zeros_like(col_ref)

    row_ref[...] = jnp.broadcast_to(own_ref[:, 0:1], row_ref.shape)
    for p, (a, b) in enumerate(((0, 0), (0, 1), (1, 1))):
        t = t_ref[p]
        e = jnp.exp(t * contract(rows[a], cols[b], ((1,), (1,))) - t)
        e_ref[p] = e
        col_ref[p : p + 1, :] += jnp.sum(e, axis=0, keepdims=True)
        total = jnp.broadcast_to(jnp.sum(e, axis=1, keepdims=True), (SCORE_TILE, LANES))
        row_ref[p : p + 1, :] = total.T[0:1]


def scores(t, rows, cols, own_scores):
    n_row, _, own, width = rows.shape
    n_col = cols.shape[0]
    block_r, block_c = n_row * own, n_col * own
    per = SCORE_TILE // own
    return call(
        score_kernel,
        (block_r // SCORE_TILE,),
        [
            scalars,
            pl.BlockSpec((per, 2, own, width), lambda i: (i, 0, 0, 0)),
            whole(cols.shape),
            whole(own_scores.shape),
        ],
        [
            pl.BlockSpec((3, SCORE_TILE, block_c), lambda i: (0, i, 0)),
            pl.BlockSpec((8, SCORE_TILE), lambda i: (0, i)),
            whole((8, block_c)),
        ],
        [
            jax.ShapeDtypeStruct((3, block_r, block_c), f32),
            jax.ShapeDtypeStruct((8, block_r), f32),
            jax.ShapeDtypeStruct((8, block_c), f32),
        ],
        flops=6 * block_r * block_c * width,
        room=60,
    )(t, rows, cols, own_scores)


def column_kernel(
    t_ref, at_ref, e_ref, rows_ref, zr_ref, zc_ref, zc_all_ref, g_ref, keep_ref, send_ref, w_ref, hr_ref
):
    step = pl.program_id(0)
    n_row, own, width = rows_ref.shape[0], rows_ref.shape[2], rows_ref.shape[3]
    block_r = n_row * own
    my_row, my_col, my_core = at_ref[0], at_ref[1], at_ref[2]

    @pl.when(step == 0)
    def _():
        for p in range(3):
            half = jnp.broadcast_to(0.5 / zr_ref[p : p + 1, :], (LANES, block_r))
            hr_ref[p] = half.T
            half = jnp.broadcast_to(0.5 / zc_all_ref[p : p + 1, :], (LANES, zc_all_ref.shape[1]))
            hr_ref[3] = half.T
            w_ref[p] = (
                hr_ref[p, pl.ds(pl.multiple_of(my_row * own, own), own), :]
                + hr_ref[3, pl.ds(pl.multiple_of(my_col * own, own), own), :]
            )

    row_id = lax.broadcasted_iota(jnp.int32, (block_r, TILE), 0) - my_row * own
    col_id = lax.broadcasted_iota(jnp.int32, (block_r, TILE), 1) + (step * TILE - my_col * own)
    own_term = (row_id == col_id) & (row_id >= 0) & (row_id < own)
    rows = [rows_ref[:, m].reshape(block_r, width) for m in range(2)]
    grads = []
    for p in range(3):
        g = e_ref[p] * (hr_ref[p] + 0.5 / zc_ref[p : p + 1, :])
        g = jnp.where(own_term, 0.0, g).astype(bf16)
        g_ref[p] = g
        grads.append(g)
    d1 = t_ref[0] * contract(grads[0], rows[0], ((0,), (0,)))
    d2 = t_ref[1] * contract(grads[1], rows[0], ((0,), (0,)))
    d2 += t_ref[2] * contract(grads[2], rows[1], ((0,), (0,)))
    for i in range(TILE // (2 * own)):
        for m, d in enumerate((d1, d2)):
            low = d[2 * i * own : (2 * i + 1) * own]
            high = d[(2 * i + 1) * own : (2 * i + 2) * own]
            keep_ref[i, m] = jnp.where(my_core == 0, low, high)
            send_ref[i, m] = jnp.where(my_core == 0, high, low).astype(bf16)


def column_gradients(t, at, e, rows, zr, zc):
    n_row, _, own, width = rows.shape
    _, block_r, block_c = e.shape
    half = block_c // own // 2
    per = TILE // (2 * own)
    tiles = lambda i: (i, 0, 0, 0)
    return call(
        column_kernel,
        (block_c // TILE,),
        [
            scalars,
            scalars,
            pl.BlockSpec((3, block_r, TILE), lambda i: (0, 0, i)),
            whole(rows.shape),
            whole(zr.shape),
            pl.BlockSpec((4, TILE), lambda i: (0, i)),
            whole(zc.shape),
        ],
        [
            pl.BlockSpec((3, block_r, TILE), lambda i: (0, 0, i)),
            pl.BlockSpec((per, 2, own, width), tiles),
            pl.BlockSpec((per, 2, own, width), tiles),
            whole((3, own, LANES)),
        ],
        [
            jax.ShapeDtypeStruct((3, block_r, block_c), bf16),
            jax.ShapeDtypeStruct((half, 2, own, width), f32),
            jax.ShapeDtypeStruct((half, 2, own, width), bf16),
            jax.ShapeDtypeStruct((3, own, LANES), f32),
        ],
        [pltpu.VMEM((4, max(block_r, block_c), LANES), f32)],
        flops=6 * block_r * block_c * width,
        room=60,
    )(t, at, e, rows, zr, zc, zc)


def row_kernel(t_ref, g_ref, cols_ref, out_ref):
    per, own, width = out_ref.shape[0], out_ref.shape[2], out_ref.shape[3]
    cols = [cols_ref[:, m].reshape(cols_ref.shape[0] * own, width) for m in range(2)]
    d0 = t_ref[0] * contract(g_ref[0], cols[0], ((1,), (0,)))
    d0 += t_ref[1] * contract(g_ref[1], cols[1], ((1,), (0,)))
    d1 = t_ref[2] * contract(g_ref[2], cols[1], ((1,), (0,)))
    out_ref[:, 0] = d0.astype(bf16).reshape(per, own, width)
    out_ref[:, 1] = d1.astype(bf16).reshape(per, own, width)


def row_gradients(t, g, cols):
    n_col, _, own, width = cols.shape
    _, block_r, block_c = g.shape
    per = TILE // own
    return call(
        row_kernel,
        (block_r // TILE,),
        [scalars, pl.BlockSpec((3, TILE, block_c), lambda i: (0, i, 0)), whole(cols.shape)],
        pl.BlockSpec((per, 2, own, width), lambda i: (i, 0, 0, 0)),
        jax.ShapeDtypeStruct((block_r // own, 2, own, width), bf16),
        flops=6 * block_r * block_c * width,
        room=60,
    )(t, g, cols)


def exact_parts(value, rows):
    line = lax.broadcasted_iota(jnp.int32, (rows, value.shape[1]), 0)
    rest = jnp.broadcast_to(value, line.shape)
    out = jnp.zeros(line.shape, f32)
    for i in range(3):
        part = rest.astype(bf16).astype(f32)
        out = jnp.where(line == i, part, out)
        rest = rest - part
    return out


def embed_kernel(
    n_row, n_col, scale, t_ref, rows_ref, cols_ref, emb_ref, unit_ref, w_ref, zr_ref, zc_ref, out_ref
):
    copies, parts = out_ref.shape[0], out_ref.shape[1]
    own, width = emb_ref.shape[1], emb_ref.shape[2]
    quarter = width // parts
    sums = [jnp.zeros((own, width), f32) for _ in range(2)]
    for i in range(rows_ref.shape[0]):
        for m in range(2):
            sums[m] += rows_ref[i, m].astype(f32)
    d_unit = [sums[0], sums[1] + cols_ref[0], cols_ref[1]]
    unit = [unit_ref[m].astype(f32) for m in range(3)]
    for p, (a, b) in enumerate(couples):
        t = t_ref[p]
        score = t * jnp.sum(unit[a] * unit[b], axis=1, keepdims=True)
        g = (jnp.exp(score - t) * w_ref[p][:, 0:1] - 1.0).astype(bf16).astype(f32)
        d_unit[a] += (t * g) * unit[b]
        d_unit[b] += (t * g) * unit[a]
    for m in range(3):
        values = emb_ref[m].astype(f32)
        length = jnp.sqrt(jnp.sum(values * values, axis=1, keepdims=True) + epsilon)
        value = values / length
        inner = jnp.sum(value * d_unit[m], axis=1, keepdims=True)
        d = ((d_unit[m] - value * inner) / length).astype(bf16)
        for c in range(copies):
            for e in range(parts):
                out_ref[c, e, m * own : (m + 1) * own, :] = d[:, e * quarter : (e + 1) * quarter]
    loss = -2.0 / n_row * zr_ref[3:4, 0:1]
    for p in range(3):
        for z_ref, count in ((zr_ref, n_row), (zc_ref, n_col)):
            lse = t_ref[p] + jnp.log(z_ref[p : p + 1, :])
            loss += jnp.sum(lse, axis=1, keepdims=True) * (1.0 / count)
    tail = exact_parts(jnp.broadcast_to(loss * scale, (1, quarter)), 16).astype(bf16)
    for c in range(copies):
        for e in range(parts):
            out_ref[c, e, 3 * own : 3 * own + 16, :] = tail


def embed_gradients(t, rows, cols, emb, unit, w, zr, zc, copies, parts, total):
    _, own, width = emb.shape
    shape = (copies, parts, 3 * own + 16, width // parts)
    kernel = functools.partial(
        embed_kernel, zr.shape[1] // own, zc.shape[1] // own, 1.0 / (2 * total)
    )
    return call(
        kernel,
        (1,),
        [scalars] + [whole(x.shape) for x in (rows, cols, emb, unit, w, zr, zc)],
        whole(shape),
        jax.ShapeDtypeStruct(shape, bf16),
        flops=10**6,
    )(t, rows, cols, emb, unit, w, zr, zc)


def head_kernel(share, line, at_ref, d_ref, own_ref, mine_ref, other_ref, out_ref):
    n_y = 1 + mine_ref.shape[0]
    my_core, my_y = at_ref[2], at_ref[3]
    n_far, height, quarter = out_ref.shape
    n_z = n_far // 2
    parts = d_ref.shape[0] // n_y
    own = (d_ref.shape[1] - 16) // 3
    clips = parts * own
    tail = jnp.sum(d_ref[:, 3 * own : 3 * own + 16, :].astype(f32), axis=0)
    loss = exact_parts(jnp.sum(tail, axis=0, keepdims=True), 8)[: height - 3 * share]
    totals = []
    for m in range(3):
        there = [
            d_ref[
                pl.ds(lax.rem(my_y + (n_y - step), n_y) * parts, parts), m * own : (m + 1) * own, :
            ].reshape(clips, quarter)
            for step in range(n_y)
        ]
        there = jnp.concatenate(there, axis=0)
        mine = [mine_ref[step, m] for step in range(n_y - 1)]
        other = [other_ref[step, m] for step in range(n_y - 1)]
        for x in range(2):
            here = [jnp.where(my_core == x, a, b) for a, b in zip(mine, other)]
            here = jnp.concatenate([own_ref[x, m]] + here, axis=1)
            totals.append(contract(here, there, ((1,), (0,))))
    for far in range(n_far):
        x, z = far // n_z, far % n_z
        piece = [totals[2 * m + x][z * line : z * line + share] for m in range(3)]
        out_ref[far] = jnp.concatenate(piece + [loss], axis=0).astype(bf16)


def head_gradients(at, d, own, mine, other, share, line):
    n_z = own.shape[2] // line
    quarter = d.shape[2]
    shape = (2 * n_z, -(-(3 * share + 3) // 16) * 16, quarter)
    return call(
        functools.partial(head_kernel, share, line),
        (1,),
        [scalars] + [whole(x.shape) for x in (d, own, mine, other)],
        whole(shape),
        jax.ShapeDtypeStruct(shape, bf16),
        flops=10**9,
    )(at, d, own, mine, other)


def summing_groups(n_y, n_x, n_z, n_l):
    ids = np.arange(n_y * n_x * n_z * n_l * 2).reshape(n_y, n_x, n_z, n_l, 2)
    over_z = ids[..., 0].reshape(n_y * n_x, n_z * n_l)
    over_plane = ids[..., 1].transpose(2, 0, 1, 3).reshape(n_z, n_y * n_x * n_l)
    return over_z.tolist() + over_plane.tolist()


def shards(f0, f1, f2, h0, h1, h2, sharpness):
    features, heads = (f0, f1, f2), (h0, h1, h2)
    clips, feat = f0.shape
    quarter = h0.shape[1]
    emb_size = lax.axis_size(EMB)
    n_y, n_x, n_z = lax.axis_size("y"), lax.axis_size("xh"), lax.axis_size("z")
    n_row, n_col = lax.axis_size(ROW), lax.axis_size(COL)
    own = clips // emb_size
    width = quarter * emb_size
    block_r, block_c = n_row * own, n_col * own
    my_y = lax.axis_index("y")
    at = jnp.stack(
        [lax.axis_index(ROW), lax.axis_index(COL), lax.axis_index("core"), my_y, lax.axis_index("xh")]
    ).astype(jnp.int32)

    share = feat // n_y // n_x // n_z
    line = -(-share // 8) * 8
    swap = [(0, 1), (1, 0)]
    wide, *sent = feature_shares(at, features, n_y, n_z, line)
    sent = [
        lax.ppermute(piece, "y", [(i, (i + step) % n_y) for i in range(n_y)])
        for step, piece in enumerate(sent, 1)
    ]
    mine = jnp.stack(sent)
    other = lax.ppermute(mine, "core", swap)

    emb = jnp.stack(
        [contract(f, h, ((1,), (0,))).astype(bf16) for f, h in zip(features, heads)]
    )
    emb = emb.reshape(3, emb_size, own, quarter).transpose(1, 0, 2, 3)
    emb, unit, rows, cols, own_scores = units(sharpness, exchange(emb, EMB), n_row)

    cols = lax.all_gather(cols, COL, axis=0)
    rows = exchange(rows, ROW)
    rows, wide, mine, other = lax.optimization_barrier((rows, wide, mine, other))

    e, row_part, col_part = scores(sharpness, rows, cols, own_scores)
    first = lax.axis_index("core") == 0
    got = lax.ppermute(jnp.where(first, row_part, col_part), "core", swap)
    both = jnp.where(
        first,
        jnp.concatenate([(col_part + got)[:4], jnp.zeros((4, block_c), f32)], axis=0),
        jnp.concatenate([got[:4], row_part[:4]], axis=0),
    )
    groups = summing_groups(n_y, n_x, n_z, 2)
    same = jnp.arange(n_row) % 2 == lax.axis_index("xl")
    weight = jnp.where(first, same.astype(f32), 1.0)
    both = jnp.broadcast_to(both[None], (n_row, *both.shape))
    both, weight = lax.optimization_barrier((both, weight))
    both = lax.all_to_all(
        both, ("y", "xh", "z", "xl", "core"), 0, 0, axis_index_groups=groups, tiled=True
    )
    both = jnp.sum(both * weight[:, None, None], axis=0)
    got = lax.ppermute(both[:4], "core", swap)
    row_sum = jnp.where(first, got, both[4:])
    col_sum = jnp.where(first, both[:4], got)

    grad, keep, send, w = column_gradients(sharpness, at, e, rows, row_sum, col_sum)
    received = lax.ppermute(send, "core", swap)
    d_rows = row_gradients(sharpness, grad, cols)
    received, d_rows = lax.optimization_barrier((received, d_rows))
    d_cols = lax.psum_scatter(keep + received.astype(f32), "z", scatter_dimension=0)
    d_rows = exchange(d_rows, ROW)

    d_emb = embed_gradients(
        sharpness, d_rows, d_cols, emb, unit, w, row_sum, col_sum, n_y, emb_size, clips * lax.axis_size(DP)
    )
    d_emb = exchange(d_emb.reshape(n_y * emb_size, 3 * own + 16, quarter), NEAR)

    out = head_gradients(at, d_emb, wide, mine, other, share, line)
    out = jnp.sum(exchange(out, FAR).astype(f32), axis=0)
    loss = out[3 * share, 0] + out[3 * share + 1, 0] + out[3 * share + 2, 0]
    return loss, out[:share], out[share : 2 * share], out[2 * share : 3 * share]


def solution(mesh):
    fine = Mesh(mesh.devices.reshape(4, 2, 8, 2, 2), ("y", "xh", "z", "xl", "core"))
    clip_rows, columns = P(DP, None), P(None, EMB)
    out = P(DP, EMB)
    return jax.shard_map(
        shards,
        mesh=fine,
        in_specs=(clip_rows,) * 3 + (columns,) * 3 + (P(),),
        out_specs=(P(), out, out, out),
        check_vma=False,
    )
```

time: 256 us -> 207 us (0.81)
  blocking collectives: 27.2 us -> 104 us
  waiting for transfers between devices: 85.4 us -> 30.4 us
  matrix products: 33.6 us -> 2.93 us
  Pallas kernels: 0 us -> 25.9 us
  starting transfers between devices: 34.9 us -> 13.8 us
  local copies, waits for them, and re-layouts: 25 us -> 6.28 us
  other arithmetic: 20 us -> 5.39 us
  between operations: 26.9 us -> 17.3 us
    all_to_all x2 -> x4, blocking collectives: 27.2 us -> 85.3 us  [exchange(): return lax.all_to_all(pieces, axes, split_axis=0, concat_axis=0, tiled=True)]
    all_to_all x5 -> x1, waiting for transfers between devices: 50.4 us -> 0.01 us  [exchange(): return lax.all_to_all(pieces, axes, split_axis=0, concat_axis=0, tiled=True)]
    dot_general x24 -> x3, matrix products: 33.6 us -> 2.93 us  [contract(): lax.dot_general(left, right, (dims, ((), ())), preferred_element_type=f32)]
    pallas_call x0 -> x7, Pallas kernels: none -> 25.9 us  [the longest x1 7 us: column_gradients(): call(column_kernel, (block_c // TILE,), [scalars, scalars, pl.BlockSpec((...]
    all_to_all x5 -> x1, starting transfers between devices: 27.8 us -> 7.03 us  [exchange(): return lax.all_to_all(pieces, axes, split_axis=0, concat_axis=0, tiled=True)]
    all_to_all x0 -> x1, blocking collectives: none -> 18.7 us  [shards(): lax.all_to_all(both, ('y', 'xh', 'z', 'xl', 'core'), 0, 0, axis_index_gro...]
    ppermute x5 -> x7, waiting for transfers between devices: 35 us -> 26.5 us  [the longest x3 23.3 us: shards(): lax.ppermute(piece, 'y', [(i, (i + step) % n_y) for i in range(n_y)])]
    reduce_sum x13 -> x2, other arithmetic: 8.28 us -> 0.16 us  [the longest x1 0.08 us: shards(): both = jnp.sum(both * weight[:, None, None], axis=0)]
  transfers between devices with their start and end apart: 12 -> 10, of which waited for: 8 -> 6; matrix products, arithmetic and copies ran while one was open for 11% -> 0% of each run, Pallas kernels for 0% -> 4%
where the time goes in v2:
time: 207 us; the launch traced here: 206 us
  blocking collectives  104 us (50%)
  waiting for transfers between devices  30.4 us (15%)
  Pallas kernels  25.9 us (13%)
  between operations  17.3 us (8%)
  starting transfers between devices  13.8 us (7%)
  local copies, waits for them, and re-layouts  6.28 us (3%)
  other arithmetic  5.39 us (3%)
  matrix products  2.93 us (1%)
    all_to_all x4, blocking collectives, exchange(): return lax.all_to_all(pieces, axes, split_axis=0, concat_axis=0, tiled=True)  85.3 us
    ppermute x3, waiting for transfers between devices, shards(): lax.ppermute(piece, 'y', [(i, (i + step) % n_y) for i in range(n_y)])  23.3 us
    all_to_all x1, blocking collectives, shards(): lax.all_to_all(both, ('y', 'xh', 'z', 'xl', 'core'), 0, 0, axis_index_gro...  18.7 us
    all_to_all x1, starting transfers between devices, exchange(): return lax.all_to_all(pieces, axes, split_axis=0, concat_axis=0, tiled=True)  7.03 us
    pallas_call x1, Pallas kernels, column_gradients(): call(column_kernel, (block_c // TILE,), [scalars, scalars, pl.BlockSpec((...  7 us
    ppermute x3, starting transfers between devices, shards(): lax.ppermute(piece, 'y', [(i, (i + step) % n_y) for i in range(n_y)])  6.08 us
    pallas_call x1, Pallas kernels, scores(): call(score_kernel, (block_r // SCORE_TILE,), [scalars, pl.BlockSpec((per,...  6.08 us
    pallas_call x1, Pallas kernels, row_gradients(): call(row_kernel, (block_r // TILE,), [scalars, pl.BlockSpec((3, TILE, blo...  5.7 us
  transfers between devices with their start and end apart: 10, of which 6 were waited for; matrix products, arithmetic and copies ran while one was open for 0% of the time, Pallas kernels for 4%

profile of v2, /device:TPU:32, one launch (start us, length us, event | category | flops | bytes accessed | tf_op | source)
XLA Modules:
  0.0 206.1 jit_solution(13373318056783218193)
XLA Ops:
  7.2 0.0 copy-start
  7.2 0.0 copy-start.1
  7.2 0.0 copy-start.20
  7.2 0.0 copy-start.10
  7.2 0.0 all-gather.3.cloned.1.call-start
  7.3 1.0 copy-done
  8.3 1.2 convolution_convert_fusion.2
  9.5 1.4 convolution_convert_fusion.1
  11.0 0.3 convolution_convert_fusion
  11.3 7.9 %all_to_all.30.emb_ref = bf16[4,3,32,256]{3,2,1,0:T(8,128)(2,1)S(1)} all-to-all(bf16[4,3,32,256]{3,2,1,0:T(8,128)(2,1)S(1)} %maximum_bitcast_fusion), channel_id=1, replica_groups=mesh['y'=4,'xh'=2,'z'=8,'xl'=2,'core'=2] {'xl','core'}, dimensions={0} | all-to-all | bytes 393216 | tf_op jit(solution)/shard_map/all_to_all | solution.py:27
  19.2 0.0 copy-done.10
  19.2 2.3 %shard_map.102 = (bf16[3,32,1024]{2,1,0:T(8,128)(2,1)S(1)}, bf16[3,32,1024]{2,1,0:T(8,128)(2,1)S(1)}, bf16[16,2,32,1024]{3,2,1,0:T(8,128)(2,1)}, bf16[2,32,1024]{2,1,0:T(8,128)(2,1)}, f32[8,128]{1,0:T(8,128)S(1)}) custom-call(f32[3]{0:T(128)S(1)} %copy-done.10, bf16[4,3,32,256]{3,2,1,0:T(8,128)(2,1)S(1)} %all_to_all.30.emb_ref), custom_call_target="tpu_custom_call" | custom-call | flops 1000000 | bytes 8388608 | tf_op jit(solution)/shard_map/pallas_call | solution.py:116
  21.5 0.7 copy-done.5
  22.2 0.6 copy-done.16
  22.7 0.0 all-gather.3.cloned.1.call-update
  22.8 0.0 copy-start.2
  22.8 0.0 copy-start.3
  22.8 7.0 %all-to-all-start.1 = ((bf16[16,2,32,1024]{3,2,1,0:T(8,128)(2,1)}), bf16[16,2,32,1024]{3,2,1,0:T(8,128)(2,1)}, u32[]{:S(2)}, u32[]{:S(2)}) async-start(bf16[16,2,32,1024]{3,2,1,0:T(8,128)(2,1)} %get-tuple-element.28), calls=%async_computation.1 | async-start | bytes 4194304 | tf_op jit(solution)/shard_map/all_to_all | solution.py:27
  29.8 0.0 reduce-scatter.2.cloned.1.call-start
  29.9 0.1 stack.47.at_ref
  30.0 0.0 copy-done.3
  30.0 2.6 %shard_map.103 = (bf16[2,3,192,128]{3,2,1,0:T(8,128)(2,1)S(1)}, bf16[3,192,128]{2,1,0:T(8,128)(2,1)S(1)}, bf16[3,192,128]{2,1,0:T(8,128)(2,1)S(1)}, bf16[3,192,128]{2,1,0:T(8,128)(2,1)S(1)}) custom-call(s32[5]{0:T(128)S(1)} %stack.47.at_ref, bf16[128,1280]{1,0:T(8,128)(2,1)S(1)} %copy-done.3, bf16[128,1280]{1,0:T(8,128)(2,1)S(1)} %copy-done.2, ...), custom_call_target="tpu_custom_call" | custom-call | flops 754974720 | bytes 8388608 | tf_op jit(solution)/shard_map/pallas_call | solution.py:81
  32.6 1.9 collective-permute-start
  34.6 2.7 %collective-permute-start.1 = (bf16[3,192,128]{2,1,0:T(8,128)(2,1)S(1)}, bf16[3,192,128]{2,1,0:T(8,128)(2,1)S(1)}, u32[]{:S(2)}, u32[]{:S(2)}) collective-permute-start(bf16[3,192,128]{2,1,0:T(8,128)(2,1)S(1)} %get-tuple-element.31), channel_id=1, source_target_pairs={{0,128},{64,192},{128,0},{192,64},{1,129},{65,193},{129,1},{193,65... | collective-permute-start | bytes 442376 | tf_op jit(solution)/shard_map/ppermute | solution.py:414
  37.3 1.5 collective-permute-start.2
  38.7 23.3 %collective-permute-done = bf16[3,192,128]{2,1,0:T(8,128)(2,1)S(1)} collective-permute-done((bf16[3,192,128]{2,1,0:T(8,128)(2,1)S(1)}, bf16[3,192,128]{2,1,0:T(8,128)(2,1)S(1)}, u32[]{:S(2)}, u32[]{:S(2)}) %collective-permute-start) | collective-permute-done | bytes 147488 | tf_op jit(solution)/shard_map/ppermute | solution.py:414
  62.1 0.0 collective-permute-done.1
  62.1 0.0 collective-permute-done.2
  62.1 0.1 pad_maximum_fusion.mine_ref
  62.1 0.1 collective-permute-start.3
  62.2 1.8 collective-permute-done.3.other_ref
  64.0 0.0 all-to-all-done.1.rows_ref
  64.0 0.5 all-gather.3.cloned.1.call-done
  64.5 6.1 %shard_map.104 = (f32[3,512,512]{2,1,0:T(8,128)}, f32[8,512]{1,0:T(8,128)}, f32[8,512]{1,0:T(8,128)}) custom-call(f32[3]{0:T(128)} %t_ref.9, bf16[16,2,32,1024]{3,2,1,0:T(8,128)(2,1)} %all-to-all-done.1.rows_ref, bf16[16,2,32,1024]{3,2,1,0:T(8,128)(2,1)} %bitcast.31, f32[8,128]{1,0:T(8,128)} %copy-done.16), custom_call_target="tpu_custom_call" | custom-call | flops 1610612736 | bytes 8388608 | tf_op jit(solution)/shard_map/pallas_call | solution.py:151
  70.6 0.7 broadcast_select_fusion
  71.3 0.2 collective-permute-start.4
  71.6 0.7 slice.34
  72.3 0.2 collective-permute-done.4
  72.5 0.8 maximum_select_fusion
  73.4 18.7 %all_to_all.31 = f32[16,8,512]{2,1,0:T(8,128)S(1)} all-to-all(f32[16,8,512]{2,1,0:T(8,128)S(1)} %broadcast_in_dim.6), channel_id=1, replica_groups={{0,2,4,6,8,10,12,14,16,18,20,22,24,26,28,30},{32,34,36,38,40,42,44,46,4..., dimensions={0} | all-to-all | bytes 524288 | tf_op jit(solution)/shard_map/all_to_all | solution.py:443
  92.1 0.1 multiply_reduce_fusion
  92.2 0.1 collective-permute-start.5
  92.3 1.2 collective-permute-done.5
  93.4 0.6 broadcast_select_fusion.1
  94.0 7.0 %shard_map.105 = (bf16[3,512,512]{2,1,0:T(8,128)(2,1)}, f32[8,2,32,1024]{3,2,1,0:T(8,128)}, bf16[8,2,32,1024]{3,2,1,0:T(8,128)(2,1)}, f32[3,32,128]{2,1,0:T(8,128)}) custom-call(f32[3]{0:T(128)} %t_ref.9, s32[5]{0:T(128)} %copy-done.12, f32[3,512,512]{2,1,0:T(8,128)} %get-tuple-element.36.e_ref, bf16[16,2,32,1024]{3,2,1,0:T(8,128)(2,1)} %all-to-all-done.1.rows_ref, ...), custom_call_target="tpu_custom_call" | custom-call | flops 1610612736 | bytes 8388608 | tf_op jit(solution)/shard_map/pallas_call | solution.py:222
  101.0 0.2 collective-permute-start.6
  101.2 5.7 %shard_map.106 = bf16[16,2,32,1024]{3,2,1,0:T(8,128)(2,1)} custom-call(f32[3]{0:T(128)} %t_ref.9, bf16[3,512,512]{2,1,0:T(8,128)(2,1)} %get-tuple-element.42.g_ref, bf16[16,2,32,1024]{3,2,1,0:T(8,128)(2,1)} %bitcast.32), custom_call_target="tpu_custom_call" | custom-call | flops 1610612736 | bytes 8388608 | tf_op jit(solution)/shard_map/pallas_call | solution.py:266
  106.9 0.0 collective-permute-done.6
  106.9 3.0 %convert_add_fusion = f32[8,2,32,1024]{3,2,1,0:T(8,128)} fusion(f32[8,2,32,1024]{3,2,1,0:T(8,128)S(1)} %copy-done.19, bf16[8,2,32,1024]{3,2,1,0:T(8,128)(2,1)} %collective-permute-done.6), kind=kLoop, calls=%fused_computation | loop fusion | flops 1048576 | bytes 5242880 | tf_op jit(solution)/shard_map/add | solution.py:455
  110.0 0.0 reduce-scatter.2.cloned.1.call-update
  110.0 0.0 copy-start.8
  110.0 0.0 copy-start.9
  110.0 0.0 copy-start.11
  110.0 33.6 %all_to_all.32.rows_ref = bf16[16,2,32,1024]{3,2,1,0:T(8,128)(2,1)S(1)} all-to-all(bf16[16,2,32,1024]{3,2,1,0:T(8,128)(2,1)} %shard_map.106), channel_id=1, replica_groups=mesh['y'=4,'xh'=2,'z'=8,'xl'=2,'core'=2] {'y','xh','xl'}, dimensions={0} | all-to-all | bytes 4194304 | tf_op jit(solution)/shard_map/all_to_all | solution.py:27
  143.6 3.4 %reduce-scatter.2.cloned.1.call-done = f32[1,2,32,1024]{3,2,1,0:T(8,128)} async-done(((f32[8,2,32,1024]{3,2,1,0:T(8,128)}), f32[1,2,32,1024]{3,2,1,0:T(8,128)}) %reduce-scatter.2.cloned.1.call-update) | async-done | bytes 262160 | tf_op jit(solution)/shard_map/reduce_scatter | solution.py:455
  147.0 0.9 copy-done.4
  147.9 0.9 copy-done.6
  148.9 1.2 shard_map.107
  150.0 20.5 %all_to_all.33.d_ref = bf16[16,112,256]{2,1,0:T(8,128)(2,1)S(1)} all-to-all(bf16[16,112,256]{2,1,0:T(8,128)(2,1)S(1)} %bitcast.23), channel_id=1, replica_groups=mesh['y'=4,'xh'=2,'z'=8,'xl'=2,'core'=2] {'y','xl','core'}, dimensions={0} | all-to-all | bytes 1835008 | tf_op jit(solution)/shard_map/all_to_all | solution.py:27
  170.5 1.0 shard_map.108
  171.6 23.4 %all_to_all.34 = bf16[16,64,256]{2,1,0:T(8,128)(2,1)S(1)} all-to-all(bf16[16,64,256]{2,1,0:T(8,128)(2,1)S(1)} %shard_map.108), channel_id=1, replica_groups=mesh['y'=4,'xh'=2,'z'=8,'xl'=2,'core'=2] {'xh','z'}, dimensions={0} | all-to-all | bytes 1048576 | tf_op jit(solution)/shard_map/all_to_all | solution.py:27
  194.9 0.1 convert_reduce_fusion
  195.0 0.6 fusion.1
  195.6 0.6 fusion
  (33 shorter events, 0.1 us)
Async XLA Ops:
  7.2 1.1 copy-start
  7.2 3.8 %copy-start.1 = (bf16[128,1280]{1,0:T(8,128)(2,1)S(1)}, bf16[128,1280]{1,0:T(8,128)(2,1)}, u32[]{:S(2)}) copy-start(bf16[128,1280]{1,0:T(8,128)(2,1)} %f2_ref.1) | copy-start | bytes 983044
  7.2 3.8 %copy-start.20 = (bf16[1280,256]{1,0:T(8,128)(2,1)S(1)}, bf16[1280,256]{1,0:T(8,128)(2,1)}, u32[]{:S(2)}) copy-start(bf16[1280,256]{1,0:T(8,128)(2,1)} %param.12) | copy-start | bytes 1966084
  7.2 12.0 %copy-start.10 = (f32[3]{0:T(128)S(1)}, f32[3]{0:T(128)}, u32[]{:S(2)}) copy-start(f32[3]{0:T(128)} %t_ref.9) | copy-start | bytes 40
  7.2 57.3 %all-gather.3.cloned.1.call-start = ((), (), s32[]{:S(2)}) async-start(), calls=%async_computation.8 | async-start | bytes 2228224 | tf_op jit(solution)/shard_map/all_gather | solution.py:426
  21.5 0.7 copy-start.5
  22.1 0.6 copy-start.16
  22.8 7.2 %copy-start.2 = (bf16[128,1280]{1,0:T(8,128)(2,1)S(1)}, bf16[128,1280]{1,0:T(8,128)(2,1)}, u32[]{:S(2)}) copy-start(bf16[128,1280]{1,0:T(8,128)(2,1)} %f1_ref.1) | copy-start | bytes 983044
  22.8 7.2 %copy-start.3 = (bf16[128,1280]{1,0:T(8,128)(2,1)S(1)}, bf16[128,1280]{1,0:T(8,128)(2,1)}, u32[]{:S(2)}) copy-start(bf16[128,1280]{1,0:T(8,128)(2,1)} %f0_ref.1) | copy-start | bytes 983044
  22.8 41.2 %all-to-all-start.1 = ((bf16[16,2,32,1024]{3,2,1,0:T(8,128)(2,1)}), bf16[16,2,32,1024]{3,2,1,0:T(8,128)(2,1)}, u32[]{:S(2)}, u32[]{:S(2)}) async-start(bf16[16,2,32,1024]{3,2,1,0:T(8,128)(2,1)} %get-tuple-element.28), calls=%async_computation.1 | async-start | bytes 4194304 | tf_op jit(solution)/shard_map/all_to_all | solution.py:27
  29.8 117.1 %reduce-scatter.2.cloned.1.call-start = ((), (), s32[]{:S(2)}) async-start(), calls=%async_computation.7 | async-start | bytes 2359296 | tf_op jit(solution)/shard_map/reduce_scatter | solution.py:455
  30.0 40.6 %copy-start.12 = (s32[5]{0:T(128)}, s32[5]{0:T(128)S(1)}, u32[]{:S(2)}) copy-start(s32[5]{0:T(128)S(1)} %stack.47.at_ref) | copy-start | bytes 64
  32.6 38.0 %copy-start.17 = (bf16[2,3,192,128]{3,2,1,0:T(8,128)(2,1)}, bf16[2,3,192,128]{3,2,1,0:T(8,128)(2,1)S(1)}, u32[]{:S(2)}) copy-start(bf16[2,3,192,128]{3,2,1,0:T(8,128)(2,1)S(1)} %get-tuple-element.49.own_ref) | copy-start | bytes 884740
  32.6 29.4 %collective-permute-start = (bf16[3,192,128]{2,1,0:T(8,128)(2,1)S(1)}, bf16[3,192,128]{2,1,0:T(8,128)(2,1)S(1)}, u32[]{:S(2)}, u32[]{:S(2)}) collective-permute-start(bf16[3,192,128]{2,1,0:T(8,128)(2,1)S(1)} %get-tuple-element.30), channel_id=1, source_target_pairs={{0,64},{64,128},{128,192},{192,0},{1,65},{65,129},{129,193},{193,1... | collective-permute-start | bytes 442376 | tf_op jit(solution)/shard_map/ppermute | solution.py:414
  34.6 27.5 %collective-permute-start.1 = (bf16[3,192,128]{2,1,0:T(8,128)(2,1)S(1)}, bf16[3,192,128]{2,1,0:T(8,128)(2,1)S(1)}, u32[]{:S(2)}, u32[]{:S(2)}) collective-permute-start(bf16[3,192,128]{2,1,0:T(8,128)(2,1)S(1)} %get-tuple-element.31), channel_id=1, source_target_pairs={{0,128},{64,192},{128,0},{192,64},{1,129},{65,193},{129,1},{193,65... | collective-permute-start | bytes 442376 | tf_op jit(solution)/shard_map/ppermute | solution.py:414
  37.3 24.8 %collective-permute-start.2 = (bf16[3,192,128]{2,1,0:T(8,128)(2,1)S(1)}, bf16[3,192,128]{2,1,0:T(8,128)(2,1)S(1)}, u32[]{:S(2)}, u32[]{:S(2)}) collective-permute-start(bf16[3,192,128]{2,1,0:T(8,128)(2,1)S(1)} %get-tuple-element.32), channel_id=1, source_target_pairs={{0,192},{64,0},{128,64},{192,128},{1,193},{65,1},{129,65},{193,129... | collective-permute-start | bytes 442376 | tf_op jit(solution)/shard_map/ppermute | solution.py:414
  62.1 1.9 collective-permute-start.3
  64.0 6.6 %copy-start.14 = (bf16[3,3,192,128]{3,2,1,0:T(8,128)(2,1)}, bf16[3,3,192,128]{3,2,1,0:T(8,128)(2,1)S(1)}, u32[]{:S(2)}) copy-start(bf16[3,3,192,128]{3,2,1,0:T(8,128)(2,1)S(1)} %collective-permute-done.3.other_ref) | copy-start | bytes 1327108
  64.5 8.0 %copy-start.21 = (pred[8]{0:T(512)(128)(4,1)S(1)}, pred[8]{0:T(512)(128)(4,1)}, u32[]{:S(2)}) copy-start(pred[8]{0:T(512)(128)(4,1)} %constant.43.clone.1) | copy-start | bytes 28
  71.3 1.2 collective-permute-start.4
  92.2 1.3 collective-permute-start.5
  101.0 5.9 %collective-permute-start.6 = (bf16[8,2,32,1024]{3,2,1,0:T(8,128)(2,1)}, bf16[8,2,32,1024]{3,2,1,0:T(8,128)(2,1)}, u32[]{:S(2)}, u32[]{:S(2)}) collective-permute-start(bf16[8,2,32,1024]{3,2,1,0:T(8,128)(2,1)} %get-tuple-element.41), channel_id=1, source_target_pairs={{0,1},{1,0},{2,3},{3,2},{4,5},{5,4},{6,7},{7,6},{8,9},{9,8},{10,11... | collective-permute-start | bytes 3145736 | tf_op jit(solution)/shard_map/ppermute | solution.py:452
  101.2 5.7 %copy-start.19 = (f32[8,2,32,1024]{3,2,1,0:T(8,128)S(1)}, f32[8,2,32,1024]{3,2,1,0:T(8,128)}, u32[]{:S(2)}) copy-start(f32[8,2,32,1024]{3,2,1,0:T(8,128)} %get-tuple-element.44) | copy-start | bytes 6291460
  110.0 37.0 %copy-start.7 = (f32[3,32,128]{2,1,0:T(8,128)S(1)}, f32[3,32,128]{2,1,0:T(8,128)}, u32[]{:S(2)}) copy-start(f32[3,32,128]{2,1,0:T(8,128)} %get-tuple-element.48.w_ref) | copy-start | bytes 147460
  110.0 37.0 %copy-start.8 = (f32[4,512]{1,0:T(4,128)S(1)}, f32[4,512]{1,0:T(4,128)}, u32[]{:S(2)}) copy-start(f32[4,512]{1,0:T(4,128)} %get-tuple-element.58.zc_ref.zc_all_ref) | copy-start | bytes 24580
  110.0 37.0 %copy-start.9 = (f32[4,512]{1,0:T(4,128)S(1)}, f32[4,512]{1,0:T(4,128)}, u32[]{:S(2)}) copy-start(f32[4,512]{1,0:T(4,128)} %get-tuple-element.59.zr_ref) | copy-start | bytes 24580
  110.0 37.0 %copy-start.11 = (f32[3]{0:T(128)S(1)}, f32[3]{0:T(128)}, u32[]{:S(2)}) copy-start(f32[3]{0:T(128)} %t_ref.9) | copy-start | bytes 40
  147.0 1.0 copy-start.4
  147.9 0.9 copy-start.6
  148.9 21.7 %copy-start.13 = (s32[5]{0:T(128)S(1)}, s32[5]{0:T(128)}, u32[]{:S(2)}) copy-start(s32[5]{0:T(128)} %copy-done.12) | copy-start | bytes 64
  148.9 21.7 %copy-start.15 = (bf16[3,3,192,128]{3,2,1,0:T(8,128)(2,1)S(1)}, bf16[3,3,192,128]{3,2,1,0:T(8,128)(2,1)}, u32[]{:S(2)}) copy-start(bf16[3,3,192,128]{3,2,1,0:T(8,128)(2,1)} %copy-done.14) | copy-start | bytes 1327108
  148.9 21.7 %copy-start.18 = (bf16[2,3,192,128]{3,2,1,0:T(8,128)(2,1)S(1)}, bf16[2,3,192,128]{3,2,1,0:T(8,128)(2,1)}, u32[]{:S(2)}) copy-start(bf16[2,3,192,128]{3,2,1,0:T(8,128)(2,1)} %copy-done.17) | copy-start | bytes 884740
Sparse Core Ops, SparseCore 0:
  22.9 41.5 all-gather.2
  110.1 36.8 reduce-scatter.1

commit v3 on v2

--- a/solution.py
+++ b/solution.py
@@ -19,8 +19,7 @@
 bf16 = jnp.bfloat16
 f32 = jnp.float32
 LANES = 128
-TILE = 128
-SCORE_TILE = 256
+TILE = 256
 
 
 def exchange(pieces, axes):
@@ -83,7 +82,7 @@
         (1,),
         [scalars] + [whole(f.shape) for f in features],
         [whole(x) for x in shapes],
-        [jax.ShapeDtypeStruct(x, bf16) for x in shapes],
+        [pltpu.HBM(x, bf16) for x in shapes],
         flops=6 * n_y * n_z * line * feat * clips,
     )(at, *features)
 
@@ -118,160 +117,184 @@
         (1,),
         [scalars, whole(emb.shape)],
         [whole(x) for x in shapes] + [whole((8, LANES))],
-        [jax.ShapeDtypeStruct(x, bf16) for x in shapes] + [jax.ShapeDtypeStruct((8, LANES), f32)],
+        [pltpu.HBM(x, bf16) for x in shapes] + [jax.ShapeDtypeStruct((8, LANES), f32)],
         flops=10**6,
     )(t, emb)
 
 
-def score_kernel(t_ref, rows_ref, cols_ref, own_ref, e_ref, row_ref, col_ref):
-    step = pl.program_id(0)
+def pair_scores(t_ref, rows_ref, cols_ref):
     own, width = rows_ref.shape[2], rows_ref.shape[3]
-    rows = [rows_ref[:, m].reshape(SCORE_TILE, width) for m in range(2)]
+    rows = [rows_ref[:, m].reshape(rows_ref.shape[0] * own, width) for m in range(2)]
     cols = [cols_ref[:, m].reshape(cols_ref.shape[0] * own, width) for m in range(2)]
-
-    @pl.when(step == 0)
-    def _():
-        col_ref[...] = jnp.zeros_like(col_ref)
-
-    row_ref[...] = jnp.broadcast_to(own_ref[:, 0:1], row_ref.shape)
+    shifted = []
     for p, (a, b) in enumerate(((0, 0), (0, 1), (1, 1))):
         t = t_ref[p]
-        e = jnp.exp(t * contract(rows[a], cols[b], ((1,), (1,))) - t)
-        e_ref[p] = e
+        shifted.append(jnp.exp(t * contract(rows[a], cols[b], ((1,), (1,))) - t))
+    return rows, cols, shifted
+
+
+def score_kernel(t_ref, at_ref, rows_ref, cols_ref, own_ref, send_ref, keep_ref, row_ref, col_ref):
+    step = pl.program_id(0)
+    _, _, shifted = pair_scores(t_ref, rows_ref, cols_ref)
+    rows = pl.ds(pl.multiple_of(step * TILE, TILE), TILE)
+
+    @pl.when(step == 0)
+    def _():
+        col_ref[...] = jnp.zeros_like(col_ref)
+        row_ref[...] = jnp.broadcast_to(own_ref[:, 0:1], row_ref.shape)
+
+    for p, e in enumerate(shifted):
         col_ref[p : p + 1, :] += jnp.sum(e, axis=0, keepdims=True)
-        total = jnp.broadcast_to(jnp.sum(e, axis=1, keepdims=True), (SCORE_TILE, LANES))
-        row_ref[p : p + 1, :] = total.T[0:1]
-
-
-def scores(t, rows, cols, own_scores):
+        total = jnp.broadcast_to(jnp.sum(e, axis=1, keepdims=True), (TILE, LANES))
+        row_ref[p : p + 1, rows] = total.T[0:1]
+
+    @pl.when(step == pl.num_programs(0) - 1)
+    def _():
+        first = at_ref[2] == 0
+        send_ref[...] = jnp.where(first, row_ref[...], col_ref[...])
+        keep_ref[...] = jnp.where(first, col_ref[...], row_ref[...])
+
+
+def scores(t, at, rows, cols, own_scores):
     n_row, _, own, width = rows.shape
-    n_col = cols.shape[0]
-    block_r, block_c = n_row * own, n_col * own
-    per = SCORE_TILE // own
+    block = n_row * own
     return call(
         score_kernel,
-        (block_r // SCORE_TILE,),
+        (block // TILE,),
         [
             scalars,
-            pl.BlockSpec((per, 2, own, width), lambda i: (i, 0, 0, 0)),
+            scalars,
+            pl.BlockSpec((TILE // own, 2, own, width), lambda i: (i, 0, 0, 0)),
             whole(cols.shape),
             whole(own_scores.shape),
         ],
-        [
-            pl.BlockSpec((3, SCORE_TILE, block_c), lambda i: (0, i, 0)),
-            pl.BlockSpec((8, SCORE_TILE), lambda i: (0, i)),
-            whole((8, block_c)),
-        ],
-        [
-            jax.ShapeDtypeStruct((3, block_r, block_c), f32),
-            jax.ShapeDtypeStruct((8, block_r), f32),
-            jax.ShapeDtypeStruct((8, block_c), f32),
-        ],
-        flops=6 * block_r * block_c * width,
-        room=60,
-    )(t, rows, cols, own_scores)
-
-
-def column_kernel(
-    t_ref, at_ref, e_ref, rows_ref, zr_ref, zc_ref, zc_all_ref, g_ref, keep_ref, send_ref, w_ref, hr_ref
+        [whole((8, block))] * 2,
+        [jax.ShapeDtypeStruct((8, block), f32)] * 2,
+        [pltpu.VMEM((8, block), f32)] * 2,
+        flops=6 * block * block * width,
+    )(t, at, rows, cols, own_scores)
+
+
+def gather_kernel(at_ref, keep_ref, got_ref, out_ref):
+    first = at_ref[2] == 0
+    keep, got = keep_ref[...], got_ref[...]
+    top = jnp.where(first, keep + got, got)[0:4]
+    both = jnp.concatenate([top, keep[0:4]], axis=0)
+    for copy in range(out_ref.shape[0]):
+        out_ref[copy] = both
+
+
+def sum_kernel(at_ref, both_ref, out_ref):
+    first = at_ref[2] == 0
+    out = jnp.zeros(out_ref.shape, f32)
+    for i in range(both_ref.shape[0]):
+        out += jnp.where(jnp.logical_and(first, at_ref[5] != i % 2), 0.0, both_ref[i])
+    out_ref[...] = out
+
+
+def small(kernel, at, arrays, shape):
+    return call(
+        kernel,
+        (1,),
+        [scalars] + [whole(x.shape) for x in arrays],
+        whole(shape),
+        jax.ShapeDtypeStruct(shape, f32),
+        flops=10**5,
+    )(at, *arrays)
+
+
+def softmax_sums(at_ref, tot_ref, got_ref):
+    first = at_ref[2] == 0
+    row = jnp.where(first, got_ref[0:4], tot_ref[4:8])
+    col = jnp.where(first, tot_ref[0:4], got_ref[0:4])
+    return row, col
+
+
+def product_kernel(
+    t_ref, at_ref, rows_ref, cols_ref, tot_ref, got_ref, out_ref, keep_ref, send_ref, w_ref, hr_ref, hc_ref, acc_ref
 ):
     step = pl.program_id(0)
-    n_row, own, width = rows_ref.shape[0], rows_ref.shape[2], rows_ref.shape[3]
-    block_r = n_row * own
+    per, _, own, width = rows_ref.shape
+    block = cols_ref.shape[0] * own
     my_row, my_col, my_core = at_ref[0], at_ref[1], at_ref[2]
 
     @pl.when(step == 0)
     def _():
+        row, col = softmax_sums(at_ref, tot_ref, got_ref)
+        hc_ref[0:4, :] = 0.5 / col
+        row = 0.5 / row
         for p in range(3):
-            half = jnp.broadcast_to(0.5 / zr_ref[p : p + 1, :], (LANES, block_r))
-            hr_ref[p] = half.T
-            half = jnp.broadcast_to(0.5 / zc_all_ref[p : p + 1, :], (LANES, zc_all_ref.shape[1]))
-            hr_ref[3] = half.T
+            hr_ref[p] = jnp.broadcast_to(row[p : p + 1], (LANES, block)).T
+            hr_ref[3] = jnp.broadcast_to(hc_ref[p : p + 1, :], (LANES, block)).T
             w_ref[p] = (
                 hr_ref[p, pl.ds(pl.multiple_of(my_row * own, own), own), :]
                 + hr_ref[3, pl.ds(pl.multiple_of(my_col * own, own), own), :]
             )
 
-    row_id = lax.broadcasted_iota(jnp.int32, (block_r, TILE), 0) - my_row * own
-    col_id = lax.broadcasted_iota(jnp.int32, (block_r, TILE), 1) + (step * TILE - my_col * own)
+    rows, cols, shifted = pair_scores(t_ref, rows_ref, cols_ref)
+    row_id = lax.broadcasted_iota(jnp.int32, (TILE, block), 0) + (step * TILE - my_row * own)
+    col_id = lax.broadcasted_iota(jnp.int32, (TILE, block), 1) - my_col * own
     own_term = (row_id == col_id) & (row_id >= 0) & (row_id < own)
-    rows = [rows_ref[:, m].reshape(block_r, width) for m in range(2)]
     grads = []
     for p in range(3):
-        g = e_ref[p] * (hr_ref[p] + 0.5 / zc_ref[p : p + 1, :])
-        g = jnp.where(own_term, 0.0, g).astype(bf16)
-        g_ref[p] = g
-        grads.append(g)
+        half = hr_ref[p, pl.ds(pl.multiple_of(step * TILE, TILE), TILE), :]
+        half = jnp.concatenate([half] * (block // LANES), axis=1)
+        g = shifted[p] * (half + hc_ref[p : p + 1, :])
+        grads.append(jnp.where(own_term, 0.0, g).astype(bf16))
+    d0 = t_ref[0] * contract(grads[0], cols[0], ((1,), (0,)))
+    d0 += t_ref[1] * contract(grads[1], cols[1], ((1,), (0,)))
+    d1 = t_ref[2] * contract(grads[2], cols[1], ((1,), (0,)))
+    out_ref[:, 0] = d0.astype(bf16).reshape(per, own, width)
+    out_ref[:, 1] = d1.astype(bf16).reshape(per, own, width)
     d1 = t_ref[0] * contract(grads[0], rows[0], ((0,), (0,)))
     d2 = t_ref[1] * contract(grads[1], rows[0], ((0,), (0,)))
     d2 += t_ref[2] * contract(grads[2], rows[1], ((0,), (0,)))
-    for i in range(TILE // (2 * own)):
+    last = pl.num_programs(0) - 1
+
+    @pl.when(step == 0)
+    def _():
+        acc_ref[0] = d1
+        acc_ref[1] = d2
+
+    @pl.when((step > 0) & (step < last))
+    def _():
+        acc_ref[0] += d1
+        acc_ref[1] += d2
+
+    @pl.when(step == last)
+    def _():
         for m, d in enumerate((d1, d2)):
-            low = d[2 * i * own : (2 * i + 1) * own]
-            high = d[(2 * i + 1) * own : (2 * i + 2) * own]
-            keep_ref[i, m] = jnp.where(my_core == 0, low, high)
-            send_ref[i, m] = jnp.where(my_core == 0, high, low).astype(bf16)
-
-
-def column_gradients(t, at, e, rows, zr, zc):
+            d = d + acc_ref[m]
+            for i in range(block // (2 * own)):
+                low = d[2 * i * own : (2 * i + 1) * own]
+                high = d[(2 * i + 1) * own : (2 * i + 2) * own]
+                keep_ref[i, m] = jnp.where(my_core == 0, low, high)
+                send_ref[i, m] = jnp.where(my_core == 0, high, low).astype(bf16)
+
+
+def products(t, at, rows, cols, tot, got):
     n_row, _, own, width = rows.shape
-    _, block_r, block_c = e.shape
-    half = block_c // own // 2
-    per = TILE // (2 * own)
-    tiles = lambda i: (i, 0, 0, 0)
-    return call(
-        column_kernel,
-        (block_c // TILE,),
+    block = n_row * own
+    half = (block // own // 2, 2, own, width)
+    tile = pl.BlockSpec((TILE // own, 2, own, width), lambda i: (i, 0, 0, 0))
+    return call(
+        product_kernel,
+        (block // TILE,),
+        [scalars, scalars, tile] + [whole(x.shape) for x in (cols, tot, got)],
+        [tile, whole(half), whole(half), whole((3, own, LANES))],
         [
-            scalars,
-            scalars,
-            pl.BlockSpec((3, block_r, TILE), lambda i: (0, 0, i)),
-            whole(rows.shape),
-            whole(zr.shape),
-            pl.BlockSpec((4, TILE), lambda i: (0, i)),
-            whole(zc.shape),
+            pltpu.HBM(rows.shape, bf16),
+            jax.ShapeDtypeStruct(half, f32),
+            jax.ShapeDtypeStruct(half, bf16),
+            jax.ShapeDtypeStruct((3, own, LANES), f32),
         ],
         [
-            pl.BlockSpec((3, block_r, TILE), lambda i: (0, 0, i)),
-            pl.BlockSpec((per, 2, own, width), tiles),
-            pl.BlockSpec((per, 2, own, width), tiles),
-            whole((3, own, LANES)),
+            pltpu.VMEM((4, block, LANES), f32),
+            pltpu.VMEM((8, block), f32),
+            pltpu.VMEM((2, block, width), f32),
         ],
-        [
-            jax.ShapeDtypeStruct((3, block_r, block_c), bf16),
-            jax.ShapeDtypeStruct((half, 2, own, width), f32),
-            jax.ShapeDtypeStruct((half, 2, own, width), bf16),
-            jax.ShapeDtypeStruct((3, own, LANES), f32),
-        ],
-        [pltpu.VMEM((4, max(block_r, block_c), LANES), f32)],
-        flops=6 * block_r * block_c * width,
-        room=60,
-    )(t, at, e, rows, zr, zc, zc)
-
-
-def row_kernel(t_ref, g_ref, cols_ref, out_ref):
-    per, own, width = out_ref.shape[0], out_ref.shape[2], out_ref.shape[3]
-    cols = [cols_ref[:, m].reshape(cols_ref.shape[0] * own, width) for m in range(2)]
-    d0 = t_ref[0] * contract(g_ref[0], cols[0], ((1,), (0,)))
-    d0 += t_ref[1] * contract(g_ref[1], cols[1], ((1,), (0,)))
-    d1 = t_ref[2] * contract(g_ref[2], cols[1], ((1,), (0,)))
-    out_ref[:, 0] = d0.astype(bf16).reshape(per, own, width)
-    out_ref[:, 1] = d1.astype(bf16).reshape(per, own, width)
-
-
-def row_gradients(t, g, cols):
-    n_col, _, own, width = cols.shape
-    _, block_r, block_c = g.shape
-    per = TILE // own
-    return call(
-        row_kernel,
-        (block_r // TILE,),
-        [scalars, pl.BlockSpec((3, TILE, block_c), lambda i: (0, i, 0)), whole(cols.shape)],
-        pl.BlockSpec((per, 2, own, width), lambda i: (i, 0, 0, 0)),
-        jax.ShapeDtypeStruct((block_r // own, 2, own, width), bf16),
-        flops=6 * block_r * block_c * width,
-        room=60,
-    )(t, g, cols)
+        flops=18 * block * block * width,
+    )(t, at, rows, cols, tot, got)
 
 
 def exact_parts(value, rows):
@@ -286,7 +309,7 @@
 
 
 def embed_kernel(
-    n_row, n_col, scale, t_ref, rows_ref, cols_ref, emb_ref, unit_ref, w_ref, zr_ref, zc_ref, out_ref
+    n_row, n_col, scale, t_ref, at_ref, rows_ref, cols_ref, emb_ref, unit_ref, w_ref, tot_ref, got_ref, out_ref
 ):
     copies, parts = out_ref.shape[0], out_ref.shape[1]
     own, width = emb_ref.shape[1], emb_ref.shape[2]
@@ -295,7 +318,7 @@
     for i in range(rows_ref.shape[0]):
         for m in range(2):
             sums[m] += rows_ref[i, m].astype(f32)
-    d_unit = [sums[0], sums[1] + cols_ref[0], cols_ref[1]]
+    d_unit = [sums[0], sums[1] + cols_ref[0].astype(f32), cols_ref[1].astype(f32)]
     unit = [unit_ref[m].astype(f32) for m in range(3)]
     for p, (a, b) in enumerate(couples):
         t = t_ref[p]
@@ -312,10 +335,11 @@
         for c in range(copies):
             for e in range(parts):
                 out_ref[c, e, m * own : (m + 1) * own, :] = d[:, e * quarter : (e + 1) * quarter]
-    loss = -2.0 / n_row * zr_ref[3:4, 0:1]
+    row, col = softmax_sums(at_ref, tot_ref, got_ref)
+    loss = -2.0 / n_row * row[3:4, 0:1]
     for p in range(3):
-        for z_ref, count in ((zr_ref, n_row), (zc_ref, n_col)):
-            lse = t_ref[p] + jnp.log(z_ref[p : p + 1, :])
+        for sums_of, count in ((row, n_row), (col, n_col)):
+            lse = t_ref[p] + jnp.log(sums_of[p : p + 1])
             loss += jnp.sum(lse, axis=1, keepdims=True) * (1.0 / count)
     tail = exact_parts(jnp.broadcast_to(loss * scale, (1, quarter)), 16).astype(bf16)
     for c in range(copies):
@@ -323,20 +347,21 @@
             out_ref[c, e, 3 * own : 3 * own + 16, :] = tail
 
 
-def embed_gradients(t, rows, cols, emb, unit, w, zr, zc, copies, parts, total):
+def embed_gradients(t, at, rows, cols, emb, unit, w, tot, got, copies, parts, total):
     _, own, width = emb.shape
     shape = (copies, parts, 3 * own + 16, width // parts)
     kernel = functools.partial(
-        embed_kernel, zr.shape[1] // own, zc.shape[1] // own, 1.0 / (2 * total)
-    )
+        embed_kernel, tot.shape[1] // own, tot.shape[1] // own, 1.0 / (2 * total)
+    )
+    arrays = (rows, cols, emb, unit, w, tot, got)
     return call(
         kernel,
         (1,),
-        [scalars] + [whole(x.shape) for x in (rows, cols, emb, unit, w, zr, zc)],
+        [scalars, scalars] + [whole(x.shape) for x in arrays],
         whole(shape),
         jax.ShapeDtypeStruct(shape, bf16),
         flops=10**6,
-    )(t, rows, cols, emb, unit, w, zr, zc)
+    )(t, at, *arrays)
 
 
 def head_kernel(share, line, at_ref, d_ref, own_ref, mine_ref, other_ref, out_ref):
@@ -397,13 +422,11 @@
     quarter = h0.shape[1]
     emb_size = lax.axis_size(EMB)
     n_y, n_x, n_z = lax.axis_size("y"), lax.axis_size("xh"), lax.axis_size("z")
-    n_row, n_col = lax.axis_size(ROW), lax.axis_size(COL)
+    n_row = lax.axis_size(ROW)
     own = clips // emb_size
-    width = quarter * emb_size
-    block_r, block_c = n_row * own, n_col * own
-    my_y = lax.axis_index("y")
+    block_r = n_row * own
     at = jnp.stack(
-        [lax.axis_index(ROW), lax.axis_index(COL), lax.axis_index("core"), my_y, lax.axis_index("xh")]
+        [lax.axis_index(axes) for axes in (ROW, COL, "core", "y", "xh", "xl")]
     ).astype(jnp.int32)
 
     share = feat // n_y // n_x // n_z
@@ -427,36 +450,23 @@
     rows = exchange(rows, ROW)
     rows, wide, mine, other = lax.optimization_barrier((rows, wide, mine, other))
 
-    e, row_part, col_part = scores(sharpness, rows, cols, own_scores)
-    first = lax.axis_index("core") == 0
-    got = lax.ppermute(jnp.where(first, row_part, col_part), "core", swap)
-    both = jnp.where(
-        first,
-        jnp.concatenate([(col_part + got)[:4], jnp.zeros((4, block_c), f32)], axis=0),
-        jnp.concatenate([got[:4], row_part[:4]], axis=0),
-    )
+    send, keep = scores(sharpness, at, rows, cols, own_scores)
+    both = small(gather_kernel, at, (keep, lax.ppermute(send, "core", swap)), (n_row, 8, block_r))
     groups = summing_groups(n_y, n_x, n_z, 2)
-    same = jnp.arange(n_row) % 2 == lax.axis_index("xl")
-    weight = jnp.where(first, same.astype(f32), 1.0)
-    both = jnp.broadcast_to(both[None], (n_row, *both.shape))
-    both, weight = lax.optimization_barrier((both, weight))
     both = lax.all_to_all(
         both, ("y", "xh", "z", "xl", "core"), 0, 0, axis_index_groups=groups, tiled=True
     )
-    both = jnp.sum(both * weight[:, None, None], axis=0)
-    got = lax.ppermute(both[:4], "core", swap)
-    row_sum = jnp.where(first, got, both[4:])
-    col_sum = jnp.where(first, both[:4], got)
-
-    grad, keep, send, w = column_gradients(sharpness, at, e, rows, row_sum, col_sum)
+    tot = small(sum_kernel, at, (both,), (8, block_r))
+    got = lax.ppermute(tot, "core", swap)
+
+    d_rows, keep, send, w = products(sharpness, at, rows, cols, tot, got)
     received = lax.ppermute(send, "core", swap)
-    d_rows = row_gradients(sharpness, grad, cols)
-    received, d_rows = lax.optimization_barrier((received, d_rows))
-    d_cols = lax.psum_scatter(keep + received.astype(f32), "z", scatter_dimension=0)
+    d_cols = (keep + received.astype(f32)).astype(bf16)
+    d_cols = lax.psum_scatter(d_cols, "z", scatter_dimension=0)
     d_rows = exchange(d_rows, ROW)
 
     d_emb = embed_gradients(
-        sharpness, d_rows, d_cols, emb, unit, w, row_sum, col_sum, n_y, emb_size, clips * lax.axis_size(DP)
+        sharpness, at, d_rows, d_cols, emb, unit, w, tot, got, n_y, emb_size, clips * lax.axis_size(DP)
     )
     d_emb = exchange(d_emb.reshape(n_y * emb_size, 3 * own + 16, quarter), NEAR)
 

time: 207 us -> 197 us (0.952)
  Pallas kernels: 25.9 us -> 21 us
  other arithmetic: 5.39 us -> 1.54 us
    pallas_call x4 -> x5, Pallas kernels: 19.9 us -> 14.3 us  [the longest x1 8.73 us: products(): call(product_kernel, (block // TILE,), [scalars, scalars, tile] + [whole(...]
    reduce_scatter x1, waiting for transfers between devices: 3.36 us -> 0.07 us  [shards(): d_cols = lax.psum_scatter(d_cols, 'z', scatter_dimension=0)]
    add x1 -> x0, other arithmetic: 3.02 us -> none  [shards(): keep + received.astype(f32)]
    ppermute x1, waiting for transfers between devices: 0.01 us -> 2.5 us  [shards(): received = lax.ppermute(send, 'core', swap)]
    select_n x4 -> x0, other arithmetic: 2.14 us -> none  [the longest x1 0.79 us: shards(): jnp.where(first, jnp.concatenate([(col_part + got)[:4], jnp.zeros((4, blo...]
    unnamed x44 -> x28, local copies, waits for them, and re-layouts: 4.24 us -> 6.21 us
  transfers between devices with their start and end apart: 10 -> 10, of which waited for: 6 -> 6; matrix products, arithmetic and copies ran while one was open for 0% -> 0% of each run, Pallas kernels for 4% -> 2%
where the time goes in v3:
time: 197 us
  blocking collectives  104 us (53%)
  waiting for transfers between devices  28.4 us (14%)
  Pallas kernels  21 us (11%)
  between operations  17.2 us (9%)
  starting transfers between devices  13.9 us (7%)
  local copies, waits for them, and re-layouts  7.48 us (4%)
  matrix products  2.93 us (1%)
    all_to_all x4, blocking collectives, exchange(): return lax.all_to_all(pieces, axes, split_axis=0, concat_axis=0, tiled=True)  85 us
    ppermute x3, waiting for transfers between devices, shards(): lax.ppermute(piece, 'y', [(i, (i + step) % n_y) for i in range(n_y)])  21.8 us
    all_to_all x1, blocking collectives, shards(): lax.all_to_all(both, ('y', 'xh', 'z', 'xl', 'core'), 0, 0, axis_index_gro...  19.1 us
    pallas_call x1, Pallas kernels, products(): call(product_kernel, (block // TILE,), [scalars, scalars, tile] + [whole(...  8.73 us
    all_to_all x1, starting transfers between devices, exchange(): return lax.all_to_all(pieces, axes, split_axis=0, concat_axis=0, tiled=True)  6.98 us
    unnamed x28, local copies, waits for them, and re-layouts  6.21 us
    ppermute x3, starting transfers between devices, shards(): lax.ppermute(piece, 'y', [(i, (i + step) % n_y) for i in range(n_y)])  6.06 us
  transfers between devices with their start and end apart: 10, of which 6 were waited for; matrix products, arithmetic and copies ran while one was open for 0% of the time, Pallas kernels for 2%

profile of v3, /device:TPU:32, one launch (start us, length us, event | category | flops | bytes accessed | tf_op | source)
XLA Modules:
  0.0 196.6 jit_solution(17854308120654272054)
XLA Ops:
  7.2 0.0 copy-start
  7.2 0.0 copy-start.1
  7.2 0.0 copy-start.13
  7.2 0.0 copy-start.7
  7.2 0.0 all-gather.3.cloned.1.call-start
  7.3 1.0 copy-done
  8.3 1.2 convolution_convert_fusion.2
  9.5 1.4 convolution_convert_fusion.1
  10.9 0.0 copy-done.1
  11.0 0.0 copy-done.13
  11.0 0.3 convolution_convert_fusion
  11.3 7.9 %all_to_all.30.emb_ref = bf16[4,3,32,256]{3,2,1,0:T(8,128)(2,1)S(1)} all-to-all(bf16[4,3,32,256]{3,2,1,0:T(8,128)(2,1)S(1)} %maximum_bitcast_fusion), channel_id=1, replica_groups=mesh['y'=4,'xh'=2,'z'=8,'xl'=2,'core'=2] {'xl','core'}, dimensions={0} | all-to-all | bytes 393216 | tf_op jit(solution)/shard_map/all_to_all | solution.py:26
  19.2 0.0 copy-done.7
  19.2 2.4 %shard_map.102 = (bf16[3,32,1024]{2,1,0:T(8,128)(2,1)}, bf16[3,32,1024]{2,1,0:T(8,128)(2,1)}, bf16[16,2,32,1024]{3,2,1,0:T(8,128)(2,1)}, bf16[2,32,1024]{2,1,0:T(8,128)(2,1)}, f32[8,128]{1,0:T(8,128)S(1)}) custom-call(f32[3]{0:T(128)S(1)} %copy-done.7, bf16[4,3,32,256]{3,2,1,0:T(8,128)(2,1)S(1)} %all_to_all.30.emb_ref), custom_call_target="tpu_custom_call" | custom-call | flops 1000000 | bytes 8388608 | tf_op jit(solution)/shard_map/pallas_call | solution.py:115
  21.6 0.0 all-gather.3.cloned.1.call-update
  21.6 0.0 copy-start.2
  21.6 7.0 %all-to-all-start.1 = ((bf16[16,2,32,1024]{3,2,1,0:T(8,128)(2,1)}), bf16[16,2,32,1024]{3,2,1,0:T(8,128)(2,1)S(1)}, u32[]{:S(2)}, u32[]{:S(2)}) async-start(bf16[16,2,32,1024]{3,2,1,0:T(8,128)(2,1)} %get-tuple-element.23), calls=%async_computation.1 | async-start | bytes 4194304 | tf_op jit(solution)/shard_map/all_to_all | solution.py:26
  28.6 0.0 reduce-scatter.2.cloned.1.call-start
  28.6 0.1 stack.51.at_ref
  28.7 0.0 copy-done.2
  28.7 0.0 copy-start.3
  28.7 1.0 copy-done.3
  29.7 3.3 %shard_map.103 = (bf16[2,3,192,128]{3,2,1,0:T(8,128)(2,1)}, bf16[3,192,128]{2,1,0:T(8,128)(2,1)}, bf16[3,192,128]{2,1,0:T(8,128)(2,1)}, bf16[3,192,128]{2,1,0:T(8,128)(2,1)}) custom-call(s32[6]{0:T(128)S(1)} %stack.51.at_ref, bf16[128,1280]{1,0:T(8,128)(2,1)S(1)} %copy-done.3, bf16[128,1280]{1,0:T(8,128)(2,1)S(1)} %copy-done.2, bf16[128,1280]{1,0:T(8,128)(2,1)S(1)} %copy-done.1), custom_call_target="tpu_custom_call" | custom-call | flops 754974720 | bytes 8388608 | tf_op jit(solution)/shard_map/pallas_call | solution.py:80
  33.0 1.9 collective-permute-start
  34.9 2.7 %collective-permute-start.1 = (bf16[3,192,128]{2,1,0:T(8,128)(2,1)}, bf16[3,192,128]{2,1,0:T(8,128)(2,1)S(1)}, u32[]{:S(2)}, u32[]{:S(2)}) collective-permute-start(bf16[3,192,128]{2,1,0:T(8,128)(2,1)} %get-tuple-element.26), channel_id=1, source_target_pairs={{0,128},{64,192},{128,0},{192,64},{1,129},{65,193},{129,1},{193,65... | collective-permute-start | bytes 442376 | tf_op jit(solution)/shard_map/ppermute | solution.py:437
  37.6 1.5 collective-permute-start.2
  39.1 21.8 %collective-permute-done = bf16[3,192,128]{2,1,0:T(8,128)(2,1)S(1)} collective-permute-done((bf16[3,192,128]{2,1,0:T(8,128)(2,1)}, bf16[3,192,128]{2,1,0:T(8,128)(2,1)S(1)}, u32[]{:S(2)}, u32[]{:S(2)}) %collective-permute-start) | collective-permute-done | bytes 147488 | tf_op jit(solution)/shard_map/ppermute | solution.py:437
  60.9 0.0 collective-permute-done.1
  60.9 0.0 collective-permute-done.2
  60.9 0.1 pad_maximum_fusion.mine_ref
  60.9 0.1 collective-permute-start.3
  61.0 1.8 collective-permute-done.3.other_ref
  62.8 0.8 copy-done.10
  63.6 0.0 all-to-all-done.1.rows_ref
  63.6 1.6 copy-done.8
  65.2 3.3 %shard_map.104 = (f32[8,512]{1,0:T(8,128)S(1)}, f32[8,512]{1,0:T(8,128)S(1)}) custom-call(f32[3]{0:T(128)S(1)} %copy-done.7, s32[6]{0:T(128)S(1)} %stack.51.at_ref, bf16[16,2,32,1024]{3,2,1,0:T(8,128)(2,1)S(1)} %all-to-all-done.1.rows_ref, bf16[16,2,32,1024]{3,2,1,0:T(8,128)(2,1)S(1)} %bitcast.26, f32[8,128]{1,0:T(8,128)S(1)} %get-tuple-element.30.own_ref), custom_call_target="tpu_custom_call" | custom-call | flops 1610612736 | bytes 8388608 | tf_op jit(solution)/shard_map/pallas_call | solution.py:161
  68.4 0.2 collective-permute-start.4
  68.7 1.0 collective-permute-done.4.got_ref
  69.7 0.6 shard_map.105
  70.3 19.1 %all_to_all.31.both_ref = f32[16,8,512]{2,1,0:T(8,128)S(1)} all-to-all(f32[16,8,512]{2,1,0:T(8,128)S(1)} %shard_map.105), channel_id=1, replica_groups={{0,2,4,6,8,10,12,14,16,18,20,22,24,26,28,30},{32,34,36,38,40,42,44,46,4..., dimensions={0} | all-to-all | bytes 524288 | tf_op jit(solution)/shard_map/all_to_all | solution.py:456
  89.3 0.6 shard_map.106.tot_ref
  89.9 0.3 collective-permute-start.5
  90.2 1.2 collective-permute-done.5.got_ref
  91.4 0.0 copy-done.9
  91.4 8.7 %shard_map.107 = (bf16[16,2,32,1024]{3,2,1,0:T(8,128)(2,1)}, f32[8,2,32,1024]{3,2,1,0:T(8,128)S(1)}, bf16[8,2,32,1024]{3,2,1,0:T(8,128)(2,1)S(1)}, f32[3,32,128]{2,1,0:T(8,128)S(1)}) custom-call(f32[3]{0:T(128)S(1)} %copy-done.7, s32[6]{0:T(128)S(1)} %stack.51.at_ref, bf16[16,2,32,1024]{3,2,1,0:T(8,128)(2,1)S(1)} %all-to-all-done.1.rows_ref, ...), custom_call_target="tpu_custom_call" | custom-call | flops 4831838208 | bytes 8388608 | tf_op jit(solution)/shard_map/pallas_call | solution.py:280
  100.1 0.2 collective-permute-start.6
  100.3 2.5 %collective-permute-done.6 = bf16[8,2,32,1024]{3,2,1,0:T(8,128)(2,1)S(1)} collective-permute-done((bf16[8,2,32,1024]{3,2,1,0:T(8,128)(2,1)S(1)}, bf16[8,2,32,1024]{3,2,1,0:T(8,128)(2,1)S(1)}, u32[]{:S(2)}, u32[]{:S(2)}) %collective-permute-start.6) | collective-permute-done | bytes 1048608 | tf_op jit(solution)/shard_map/ppermute | solution.py:463
  102.8 1.4 add_convert_fusion
  104.2 0.0 reduce-scatter.2.cloned.1.call-update
  104.2 0.0 copy-start.4
  104.2 33.4 %all_to_all.32.rows_ref = bf16[16,2,32,1024]{3,2,1,0:T(8,128)(2,1)S(1)} all-to-all(bf16[16,2,32,1024]{3,2,1,0:T(8,128)(2,1)} %get-tuple-element.33), channel_id=1, replica_groups=mesh['y'=4,'xh'=2,'z'=8,'xl'=2,'core'=2] {'y','xh','xl'}, dimensions={0} | all-to-all | bytes 4194304 | tf_op jit(solution)/shard_map/all_to_all | solution.py:26
  137.6 0.1 reduce-scatter.2.cloned.1.call-done
  137.7 0.0 copy-done.4
  137.7 0.9 copy-done.5
  138.6 0.9 copy-done.6
  139.5 1.2 shard_map.108
  140.7 20.3 %all_to_all.33.d_ref = bf16[16,112,256]{2,1,0:T(8,128)(2,1)S(1)} all-to-all(bf16[16,112,256]{2,1,0:T(8,128)(2,1)S(1)} %bitcast.24), channel_id=1, replica_groups=mesh['y'=4,'xh'=2,'z'=8,'xl'=2,'core'=2] {'y','xl','core'}, dimensions={0} | all-to-all | bytes 1835008 | tf_op jit(solution)/shard_map/all_to_all | solution.py:26
  161.0 0.0 copy-done.11
  161.0 0.0 copy-done.12
  161.0 1.0 shard_map.109
  162.0 23.4 %all_to_all.34 = bf16[16,64,256]{2,1,0:T(8,128)(2,1)S(1)} all-to-all(bf16[16,64,256]{2,1,0:T(8,128)(2,1)S(1)} %shard_map.109), channel_id=1, replica_groups=mesh['y'=4,'xh'=2,'z'=8,'xl'=2,'core'=2] {'xh','z'}, dimensions={0} | all-to-all | bytes 1048576 | tf_op jit(solution)/shard_map/all_to_all | solution.py:26
  185.4 0.1 convert_reduce_fusion
  185.5 0.6 fusion.1
  186.1 0.6 fusion
  (9 shorter events, 0.0 us)
Async XLA Ops:
  7.2 1.1 copy-start
  7.2 3.8 %copy-start.1 = (bf16[128,1280]{1,0:T(8,128)(2,1)S(1)}, bf16[128,1280]{1,0:T(8,128)(2,1)}, u32[]{:S(2)}) copy-start(bf16[128,1280]{1,0:T(8,128)(2,1)} %f2_ref.1) | copy-start | bytes 983044
  7.2 3.8 %copy-start.13 = (bf16[1280,256]{1,0:T(8,128)(2,1)S(1)}, bf16[1280,256]{1,0:T(8,128)(2,1)}, u32[]{:S(2)}) copy-start(bf16[1280,256]{1,0:T(8,128)(2,1)} %param.12) | copy-start | bytes 1966084
  7.2 12.0 %copy-start.7 = (f32[3]{0:T(128)S(1)}, f32[3]{0:T(128)}, u32[]{:S(2)}) copy-start(f32[3]{0:T(128)} %t_ref.7) | copy-start | bytes 40
  7.2 56.4 %all-gather.3.cloned.1.call-start = ((), (), s32[]{:S(2)}) async-start(), calls=%async_computation.8 | async-start | bytes 2228224 | tf_op jit(solution)/shard_map/all_gather | solution.py:449
  21.6 7.2 %copy-start.2 = (bf16[128,1280]{1,0:T(8,128)(2,1)S(1)}, bf16[128,1280]{1,0:T(8,128)(2,1)}, u32[]{:S(2)}) copy-start(bf16[128,1280]{1,0:T(8,128)(2,1)} %f1_ref.1) | copy-start | bytes 983044
  21.6 42.0 %all-to-all-start.1 = ((bf16[16,2,32,1024]{3,2,1,0:T(8,128)(2,1)}), bf16[16,2,32,1024]{3,2,1,0:T(8,128)(2,1)S(1)}, u32[]{:S(2)}, u32[]{:S(2)}) async-start(bf16[16,2,32,1024]{3,2,1,0:T(8,128)(2,1)} %get-tuple-element.23), calls=%async_computation.1 | async-start | bytes 4194304 | tf_op jit(solution)/shard_map/all_to_all | solution.py:26
  28.6 109.1 %reduce-scatter.2.cloned.1.call-start = ((), (), s32[]{:S(2)}) async-start(), calls=%async_computation.7 | async-start | bytes 1179648 | tf_op jit(solution)/shard_map/reduce_scatter | solution.py:465
  28.7 1.0 copy-start.3
  33.0 27.9 %collective-permute-start = (bf16[3,192,128]{2,1,0:T(8,128)(2,1)}, bf16[3,192,128]{2,1,0:T(8,128)(2,1)S(1)}, u32[]{:S(2)}, u32[]{:S(2)}) collective-permute-start(bf16[3,192,128]{2,1,0:T(8,128)(2,1)} %get-tuple-element.25), channel_id=1, source_target_pairs={{0,64},{64,128},{128,192},{192,0},{1,65},{65,129},{129,193},{193,1... | collective-permute-start | bytes 442376 | tf_op jit(solution)/shard_map/ppermute | solution.py:437
  34.9 25.9 %collective-permute-start.1 = (bf16[3,192,128]{2,1,0:T(8,128)(2,1)}, bf16[3,192,128]{2,1,0:T(8,128)(2,1)S(1)}, u32[]{:S(2)}, u32[]{:S(2)}) collective-permute-start(bf16[3,192,128]{2,1,0:T(8,128)(2,1)} %get-tuple-element.26), channel_id=1, source_target_pairs={{0,128},{64,192},{128,0},{192,64},{1,129},{65,193},{129,1},{193,65... | collective-permute-start | bytes 442376 | tf_op jit(solution)/shard_map/ppermute | solution.py:437
  37.6 23.3 %collective-permute-start.2 = (bf16[3,192,128]{2,1,0:T(8,128)(2,1)}, bf16[3,192,128]{2,1,0:T(8,128)(2,1)S(1)}, u32[]{:S(2)}, u32[]{:S(2)}) collective-permute-start(bf16[3,192,128]{2,1,0:T(8,128)(2,1)} %get-tuple-element.27), channel_id=1, source_target_pairs={{0,192},{64,0},{128,64},{192,128},{1,193},{65,1},{129,65},{193,129... | collective-permute-start | bytes 442376 | tf_op jit(solution)/shard_map/ppermute | solution.py:437
  60.9 1.9 collective-permute-start.3
  62.8 0.8 copy-start.10
  63.6 1.6 copy-start.8
  65.2 26.2 %copy-start.9 = (bf16[32,32,1024]{2,1,0:T(8,128)(2,1)S(1)}, bf16[32,32,1024]{2,1,0:T(8,128)(2,1)}, u32[]{:S(2)}) copy-start(bf16[32,32,1024]{2,1,0:T(8,128)(2,1)} %all-gather.3.cloned.1.call-done) | copy-start | bytes 6291460
  68.4 1.3 collective-permute-start.4
  89.9 1.5 collective-permute-start.5
  100.1 2.7 %collective-permute-start.6 = (bf16[8,2,32,1024]{3,2,1,0:T(8,128)(2,1)S(1)}, bf16[8,2,32,1024]{3,2,1,0:T(8,128)(2,1)S(1)}, u32[]{:S(2)}, u32[]{:S(2)}) collective-permute-start(bf16[8,2,32,1024]{3,2,1,0:T(8,128)(2,1)S(1)} %get-tuple-element.35), channel_id=1, source_target_pairs={{0,1},{1,0},{2,3},{3,2},{4,5},{5,4},{6,7},{7,6},{8,9},{9,8},{10,11... | collective-permute-start | bytes 3145736 | tf_op jit(solution)/shard_map/ppermute | solution.py:463
  104.2 33.5 %copy-start.4 = (bf16[3,32,1024]{2,1,0:T(8,128)(2,1)S(1)}, bf16[3,32,1024]{2,1,0:T(8,128)(2,1)}, u32[]{:S(2)}) copy-start(bf16[3,32,1024]{2,1,0:T(8,128)(2,1)} %get-tuple-element.36.emb_ref) | copy-start | bytes 589828
  137.7 0.9 copy-start.5
  138.6 0.9 copy-start.6
  139.5 21.5 %copy-start.11 = (bf16[3,3,192,128]{3,2,1,0:T(8,128)(2,1)S(1)}, bf16[3,3,192,128]{3,2,1,0:T(8,128)(2,1)}, u32[]{:S(2)}) copy-start(bf16[3,3,192,128]{3,2,1,0:T(8,128)(2,1)} %copy-done.10) | copy-start | bytes 1327108
  139.5 21.5 %copy-start.12 = (bf16[2,3,192,128]{3,2,1,0:T(8,128)(2,1)S(1)}, bf16[2,3,192,128]{3,2,1,0:T(8,128)(2,1)}, u32[]{:S(2)}) copy-start(bf16[2,3,192,128]{3,2,1,0:T(8,128)(2,1)} %get-tuple-element.39.own_ref) | copy-start | bytes 884740
Sparse Core Ops, SparseCore 0:
  21.7 41.5 all-gather.2
  104.3 33.3 reduce-scatter.1

commit v4 on v3

--- a/solution.py
+++ b/solution.py
@@ -19,7 +19,6 @@
 bf16 = jnp.bfloat16
 f32 = jnp.float32
 LANES = 128
-TILE = 256
 
 
 def exchange(pieces, axes):
@@ -53,6 +52,7 @@
 
 
 scalars = pl.BlockSpec(memory_space=pltpu.SMEM)
+remote = pl.BlockSpec(memory_space=pltpu.HBM)
 
 
 def share_kernel(share, line, at_ref, f0_ref, f1_ref, f2_ref, own_ref, *send_refs):
@@ -122,37 +122,35 @@
     )(t, emb)
 
 
-def pair_scores(t_ref, rows_ref, cols_ref):
-    own, width = rows_ref.shape[2], rows_ref.shape[3]
-    rows = [rows_ref[:, m].reshape(rows_ref.shape[0] * own, width) for m in range(2)]
-    cols = [cols_ref[:, m].reshape(cols_ref.shape[0] * own, width) for m in range(2)]
-    shifted = []
+def far_memory(value):
+    return pltpu.with_memory_space_constraint(value, pltpu.HBM)
+
+
+def shifted_scores(t, rows, cols):
+    return jnp.exp(t * contract(rows, cols, ((1,), (1,))) - t)
+
+
+def score_kernel(t_ref, at_ref, rows_ref, cols_hbm, own_ref, send_ref, keep_ref, cols_ref, sems):
+    n_row, _, own, width = rows_ref.shape
+    block = n_row * own
+    copies = [pltpu.make_async_copy(cols_hbm.at[:, m], cols_ref.at[m], sems.at[m]) for m in range(2)]
+    for copy in copies:
+        copy.start()
+    rows = [rows_ref[:, m].reshape(block, width) for m in range(2)]
+    row_sums, col_sums = [], []
     for p, (a, b) in enumerate(((0, 0), (0, 1), (1, 1))):
-        t = t_ref[p]
-        shifted.append(jnp.exp(t * contract(rows[a], cols[b], ((1,), (1,))) - t))
-    return rows, cols, shifted
-
-
-def score_kernel(t_ref, at_ref, rows_ref, cols_ref, own_ref, send_ref, keep_ref, row_ref, col_ref):
-    step = pl.program_id(0)
-    _, _, shifted = pair_scores(t_ref, rows_ref, cols_ref)
-    rows = pl.ds(pl.multiple_of(step * TILE, TILE), TILE)
-
-    @pl.when(step == 0)
-    def _():
-        col_ref[...] = jnp.zeros_like(col_ref)
-        row_ref[...] = jnp.broadcast_to(own_ref[:, 0:1], row_ref.shape)
-
-    for p, e in enumerate(shifted):
-        col_ref[p : p + 1, :] += jnp.sum(e, axis=0, keepdims=True)
-        total = jnp.broadcast_to(jnp.sum(e, axis=1, keepdims=True), (TILE, LANES))
-        row_ref[p : p + 1, rows] = total.T[0:1]
-
-    @pl.when(step == pl.num_programs(0) - 1)
-    def _():
-        first = at_ref[2] == 0
-        send_ref[...] = jnp.where(first, row_ref[...], col_ref[...])
-        keep_ref[...] = jnp.where(first, col_ref[...], row_ref[...])
+        if p < 2:
+            copies[p].wait()
+        e = shifted_scores(t_ref[p], rows[a], cols_ref[b].reshape(block, width))
+        col_sums.append(jnp.sum(e, axis=0, keepdims=True))
+        total = jnp.broadcast_to(jnp.sum(e, axis=1, keepdims=True), (block, LANES))
+        row_sums.append(total.T[0:1])
+    own_sum = jnp.broadcast_to(own_ref[:, 0:1], (8, block))
+    row = jnp.concatenate(row_sums + [own_sum[0:5]], axis=0)
+    col = jnp.concatenate(col_sums + [own_sum[0:5]], axis=0)
+    first = at_ref[2] == 0
+    send_ref[...] = jnp.where(first, row, col)
+    keep_ref[...] = jnp.where(first, col, row)
 
 
 def scores(t, at, rows, cols, own_scores):
@@ -160,19 +158,13 @@
     block = n_row * own
     return call(
         score_kernel,
-        (block // TILE,),
-        [
-            scalars,
-            scalars,
-            pl.BlockSpec((TILE // own, 2, own, width), lambda i: (i, 0, 0, 0)),
-            whole(cols.shape),
-            whole(own_scores.shape),
-        ],
+        (1,),
+        [scalars, scalars, whole(rows.shape), remote, whole(own_scores.shape)],
         [whole((8, block))] * 2,
         [jax.ShapeDtypeStruct((8, block), f32)] * 2,
-        [pltpu.VMEM((8, block), f32)] * 2,
+        [pltpu.VMEM((2, n_row, own, width), bf16), pltpu.SemaphoreType.DMA((2,))],
         flops=6 * block * block * width,
-    )(t, at, rows, cols, own_scores)
+    )(t, at, rows, far_memory(cols), own_scores)
 
 
 def gather_kernel(at_ref, keep_ref, got_ref, out_ref):
@@ -211,87 +203,71 @@
 
 
 def product_kernel(
-    t_ref, at_ref, rows_ref, cols_ref, tot_ref, got_ref, out_ref, keep_ref, send_ref, w_ref, hr_ref, hc_ref, acc_ref
+    t_ref, at_ref, rows_ref, cols_ref, tot_ref, got_ref, out_hbm, keep_ref, send_ref, w_ref, hr_ref, out_ref, sems
 ):
-    step = pl.program_id(0)
-    per, _, own, width = rows_ref.shape
-    block = cols_ref.shape[0] * own
+    n_row, _, own, width = rows_ref.shape
+    block = n_row * own
     my_row, my_col, my_core = at_ref[0], at_ref[1], at_ref[2]
-
-    @pl.when(step == 0)
-    def _():
-        row, col = softmax_sums(at_ref, tot_ref, got_ref)
-        hc_ref[0:4, :] = 0.5 / col
-        row = 0.5 / row
-        for p in range(3):
-            hr_ref[p] = jnp.broadcast_to(row[p : p + 1], (LANES, block)).T
-            hr_ref[3] = jnp.broadcast_to(hc_ref[p : p + 1, :], (LANES, block)).T
-            w_ref[p] = (
-                hr_ref[p, pl.ds(pl.multiple_of(my_row * own, own), own), :]
-                + hr_ref[3, pl.ds(pl.multiple_of(my_col * own, own), own), :]
-            )
-
-    rows, cols, shifted = pair_scores(t_ref, rows_ref, cols_ref)
-    row_id = lax.broadcasted_iota(jnp.int32, (TILE, block), 0) + (step * TILE - my_row * own)
-    col_id = lax.broadcasted_iota(jnp.int32, (TILE, block), 1) - my_col * own
+    row, col = softmax_sums(at_ref, tot_ref, got_ref)
+    row, col = 0.5 / row, 0.5 / col
+    for p in range(3):
+        hr_ref[p] = jnp.broadcast_to(row[p : p + 1], (LANES, block)).T
+        hr_ref[3] = jnp.broadcast_to(col[p : p + 1], (LANES, block)).T
+        w_ref[p] = (
+            hr_ref[p, pl.ds(pl.multiple_of(my_row * own, own), own), :]
+            + hr_ref[3, pl.ds(pl.multiple_of(my_col * own, own), own), :]
+        )
+
+    rows = [rows_ref[:, m].reshape(block, width) for m in range(2)]
+    cols = [cols_ref[:, m].reshape(block, width) for m in range(2)]
+    row_id = lax.broadcasted_iota(jnp.int32, (block, block), 0) - my_row * own
+    col_id = lax.broadcasted_iota(jnp.int32, (block, block), 1) - my_col * own
     own_term = (row_id == col_id) & (row_id >= 0) & (row_id < own)
     grads = []
-    for p in range(3):
-        half = hr_ref[p, pl.ds(pl.multiple_of(step * TILE, TILE), TILE), :]
-        half = jnp.concatenate([half] * (block // LANES), axis=1)
-        g = shifted[p] * (half + hc_ref[p : p + 1, :])
+    for p, (a, b) in enumerate(((0, 0), (0, 1), (1, 1))):
+        half = jnp.concatenate([hr_ref[p]] * (block // LANES), axis=1)
+        g = shifted_scores(t_ref[p], rows[a], cols[b]) * (half + col[p : p + 1])
         grads.append(jnp.where(own_term, 0.0, g).astype(bf16))
     d0 = t_ref[0] * contract(grads[0], cols[0], ((1,), (0,)))
     d0 += t_ref[1] * contract(grads[1], cols[1], ((1,), (0,)))
     d1 = t_ref[2] * contract(grads[2], cols[1], ((1,), (0,)))
-    out_ref[:, 0] = d0.astype(bf16).reshape(per, own, width)
-    out_ref[:, 1] = d1.astype(bf16).reshape(per, own, width)
+    copies = []
+    for m, d in enumerate((d0, d1)):
+        out_ref[m] = d.astype(bf16).reshape(n_row, own, width)
+        copies.append(pltpu.make_async_copy(out_ref.at[m], out_hbm.at[:, m], sems.at[m]))
+        copies[m].start()
     d1 = t_ref[0] * contract(grads[0], rows[0], ((0,), (0,)))
     d2 = t_ref[1] * contract(grads[1], rows[0], ((0,), (0,)))
     d2 += t_ref[2] * contract(grads[2], rows[1], ((0,), (0,)))
-    last = pl.num_programs(0) - 1
-
-    @pl.when(step == 0)
-    def _():
-        acc_ref[0] = d1
-        acc_ref[1] = d2
-
-    @pl.when((step > 0) & (step < last))
-    def _():
-        acc_ref[0] += d1
-        acc_ref[1] += d2
-
-    @pl.when(step == last)
-    def _():
-        for m, d in enumerate((d1, d2)):
-            d = d + acc_ref[m]
-            for i in range(block // (2 * own)):
-                low = d[2 * i * own : (2 * i + 1) * own]
-                high = d[(2 * i + 1) * own : (2 * i + 2) * own]
-                keep_ref[i, m] = jnp.where(my_core == 0, low, high)
-                send_ref[i, m] = jnp.where(my_core == 0, high, low).astype(bf16)
+    for m, d in enumerate((d1, d2)):
+        for i in range(block // (2 * own)):
+            low = d[2 * i * own : (2 * i + 1) * own]
+            high = d[(2 * i + 1) * own : (2 * i + 2) * own]
+            keep_ref[i, m] = jnp.where(my_core == 0, low, high).astype(bf16)
+            send_ref[i, m] = jnp.where(my_core == 0, high, low).astype(bf16)
+    for copy in copies:
+        copy.wait()
 
 
 def products(t, at, rows, cols, tot, got):
     n_row, _, own, width = rows.shape
     block = n_row * own
-    half = (block // own // 2, 2, own, width)
-    tile = pl.BlockSpec((TILE // own, 2, own, width), lambda i: (i, 0, 0, 0))
+    half = (n_row // 2, 2, own, width)
     return call(
         product_kernel,
-        (block // TILE,),
-        [scalars, scalars, tile] + [whole(x.shape) for x in (cols, tot, got)],
-        [tile, whole(half), whole(half), whole((3, own, LANES))],
+        (1,),
+        [scalars, scalars] + [whole(x.shape) for x in (rows, cols, tot, got)],
+        [remote, whole(half), whole(half), whole((3, own, LANES))],
         [
             pltpu.HBM(rows.shape, bf16),
-            jax.ShapeDtypeStruct(half, f32),
+            jax.ShapeDtypeStruct(half, bf16),
             jax.ShapeDtypeStruct(half, bf16),
             jax.ShapeDtypeStruct((3, own, LANES), f32),
         ],
         [
             pltpu.VMEM((4, block, LANES), f32),
-            pltpu.VMEM((8, block), f32),
-            pltpu.VMEM((2, block, width), f32),
+            pltpu.VMEM((2, n_row, own, width), bf16),
+            pltpu.SemaphoreType.DMA((2,)),
         ],
         flops=18 * block * block * width,
     )(t, at, rows, cols, tot, got)
@@ -309,8 +285,12 @@
 
 
 def embed_kernel(
-    n_row, n_col, scale, t_ref, at_ref, rows_ref, cols_ref, emb_ref, unit_ref, w_ref, tot_ref, got_ref, out_ref
+    n_row, n_col, scale, t_ref, at_ref, rows_ref, cols_hbm, emb_hbm, unit_hbm, w_ref, tot_ref, got_ref, out_ref, cols_ref, emb_ref, unit_ref, sems
 ):
+    pairs = ((cols_hbm, cols_ref), (emb_hbm, emb_ref), (unit_hbm, unit_ref))
+    loads = [pltpu.make_async_copy(*pair, sems.at[i]) for i, pair in enumerate(pairs)]
+    for load in loads:
+        load.start()
     copies, parts = out_ref.shape[0], out_ref.shape[1]
     own, width = emb_ref.shape[1], emb_ref.shape[2]
     quarter = width // parts
@@ -318,6 +298,8 @@
     for i in range(rows_ref.shape[0]):
         for m in range(2):
             sums[m] += rows_ref[i, m].astype(f32)
+    for load in loads:
+        load.wait()
     d_unit = [sums[0], sums[1] + cols_ref[0].astype(f32), cols_ref[1].astype(f32)]
     unit = [unit_ref[m].astype(f32) for m in range(3)]
     for p, (a, b) in enumerate(couples):
@@ -353,13 +335,14 @@
     kernel = functools.partial(
         embed_kernel, tot.shape[1] // own, tot.shape[1] // own, 1.0 / (2 * total)
     )
-    arrays = (rows, cols, emb, unit, w, tot, got)
+    arrays = (rows, far_memory(cols), far_memory(emb), far_memory(unit), w, tot, got)
     return call(
         kernel,
         (1,),
-        [scalars, scalars] + [whole(x.shape) for x in arrays],
+        [scalars, scalars, whole(rows.shape)] + [remote] * 3 + [whole(x.shape) for x in (w, tot, got)],
         whole(shape),
         jax.ShapeDtypeStruct(shape, bf16),
+        [pltpu.VMEM(x.shape, bf16) for x in (cols, emb, unit)] + [pltpu.SemaphoreType.DMA((3,))],
         flops=10**6,
     )(t, at, *arrays)
 
@@ -406,7 +389,7 @@
         whole(shape),
         jax.ShapeDtypeStruct(shape, bf16),
         flops=10**9,
-    )(at, d, own, mine, other)
+    )(at, d, own, mine, far_memory(other))
 
 
 def summing_groups(n_y, n_x, n_z, n_l):
@@ -438,7 +421,6 @@
         for step, piece in enumerate(sent, 1)
     ]
     mine = jnp.stack(sent)
-    other = lax.ppermute(mine, "core", swap)
 
     emb = jnp.stack(
         [contract(f, h, ((1,), (0,))).astype(bf16) for f, h in zip(features, heads)]
@@ -448,6 +430,7 @@
 
     cols = lax.all_gather(cols, COL, axis=0)
     rows = exchange(rows, ROW)
+    other = lax.ppermute(mine, "core", swap)
     rows, wide, mine, other = lax.optimization_barrier((rows, wide, mine, other))
 
     send, keep = scores(sharpness, at, rows, cols, own_scores)
@@ -461,7 +444,7 @@
 
     d_rows, keep, send, w = products(sharpness, at, rows, cols, tot, got)
     received = lax.ppermute(send, "core", swap)
-    d_cols = (keep + received.astype(f32)).astype(bf16)
+    d_cols = (keep.astype(f32) + received.astype(f32)).astype(bf16)
     d_cols = lax.psum_scatter(d_cols, "z", scatter_dimension=0)
     d_rows = exchange(d_rows, ROW)
 

time: 197 us -> 193 us (0.980)
  local copies, waits for them, and re-layouts: 7.48 us -> 3.3 us
    unnamed x28 -> x16, local copies, waits for them, and re-layouts: 6.21 us -> 2.01 us
  transfers between devices with their start and end apart: 10 -> 10, of which waited for: 6 -> 7; matrix products, arithmetic and copies ran while one was open for 0% -> 0% of each run, Pallas kernels for 2% -> 2%
where the time goes in v4:
time: 193 us
  blocking collectives  103 us (53%)
  waiting for transfers between devices  29 us (15%)
  Pallas kernels  21.1 us (11%)
  between operations  17.3 us (9%)
  starting transfers between devices  14.1 us (7%)
  local copies, waits for them, and re-layouts  3.3 us (2%)
  matrix products  2.93 us (2%)
    all_to_all x4, blocking collectives, exchange(): return lax.all_to_all(pieces, axes, split_axis=0, concat_axis=0, tiled=True)  84.8 us
    ppermute x3, waiting for transfers between devices, shards(): lax.ppermute(piece, 'y', [(i, (i + step) % n_y) for i in range(n_y)])  21.8 us
    all_to_all x1, blocking collectives, shards(): lax.all_to_all(both, ('y', 'xh', 'z', 'xl', 'core'), 0, 0, axis_index_gro...  18.7 us
    all_to_all x1, starting transfers between devices, exchange(): return lax.all_to_all(pieces, axes, split_axis=0, concat_axis=0, tiled=True)  6.98 us
    pallas_call x1, Pallas kernels, products(): call(product_kernel, (1,), [scalars, scalars] + [whole(x.shape) for x in...  6.24 us
    ppermute x3, starting transfers between devices, shards(): lax.ppermute(piece, 'y', [(i, (i + step) % n_y) for i in range(n_y)])  6.06 us
    pallas_call x1, Pallas kernels, scores(): call(score_kernel, (1,), [scalars, scalars, whole(rows.shape), remote, wh...  4.49 us
  transfers between devices with their start and end apart: 10, of which 7 were waited for; matrix products, arithmetic and copies ran while one was open for 0% of the time, Pallas kernels for 2%

profile of v4, /device:TPU:32, one launch (start us, length us, event | category | flops | bytes accessed | tf_op | source)
XLA Modules:
  0.0 192.6 jit_solution(997854092783025304)
XLA Ops:
  7.2 0.0 copy-start
  7.2 0.0 copy-start.1
  7.2 0.0 copy-start.7
  7.2 0.0 copy-start.4
  7.2 0.0 all-gather.3.cloned.1.call-start
  7.3 1.0 copy-done
  8.3 1.2 convolution_convert_fusion.2
  9.5 1.4 convolution_convert_fusion.1
  10.9 0.0 copy-done.1
  11.0 0.0 copy-done.7
  11.0 0.3 convolution_convert_fusion
  11.3 7.9 %all_to_all.30.emb_ref = bf16[4,3,32,256]{3,2,1,0:T(8,128)(2,1)S(1)} all-to-all(bf16[4,3,32,256]{3,2,1,0:T(8,128)(2,1)S(1)} %maximum_bitcast_fusion), channel_id=1, replica_groups=mesh['y'=4,'xh'=2,'z'=8,'xl'=2,'core'=2] {'xl','core'}, dimensions={0} | all-to-all | bytes 393216 | tf_op jit(solution)/shard_map/all_to_all | solution.py:25
  19.2 0.0 copy-done.4
  19.2 2.4 %shard_map.102 = (bf16[3,32,1024]{2,1,0:T(8,128)(2,1)}, bf16[3,32,1024]{2,1,0:T(8,128)(2,1)}, bf16[16,2,32,1024]{3,2,1,0:T(8,128)(2,1)}, bf16[2,32,1024]{2,1,0:T(8,128)(2,1)}, f32[8,128]{1,0:T(8,128)S(1)}) custom-call(f32[3]{0:T(128)S(1)} %copy-done.4, bf16[4,3,32,256]{3,2,1,0:T(8,128)(2,1)S(1)} %all_to_all.30.emb_ref), custom_call_target="tpu_custom_call" | custom-call | flops 1000000 | bytes 8388608 | tf_op jit(solution)/shard_map/pallas_call | solution.py:115
  21.5 0.0 all-gather.3.cloned.1.call-update
  21.6 0.0 copy-start.2
  21.6 7.0 %all-to-all-start.1 = ((bf16[16,2,32,1024]{3,2,1,0:T(8,128)(2,1)}), bf16[16,2,32,1024]{3,2,1,0:T(8,128)(2,1)S(1)}, u32[]{:S(2)}, u32[]{:S(2)}) async-start(bf16[16,2,32,1024]{3,2,1,0:T(8,128)(2,1)} %get-tuple-element.23), calls=%async_computation.1 | async-start | bytes 4194304 | tf_op jit(solution)/shard_map/all_to_all | solution.py:25
  28.6 0.0 reduce-scatter.2.cloned.1.call-start
  28.6 0.1 stack.51.at_ref
  28.7 0.0 copy-done.2
  28.7 0.0 copy-start.3
  28.7 1.0 copy-done.3
  29.7 3.3 %shard_map.103 = (bf16[2,3,192,128]{3,2,1,0:T(8,128)(2,1)}, bf16[3,192,128]{2,1,0:T(8,128)(2,1)}, bf16[3,192,128]{2,1,0:T(8,128)(2,1)}, bf16[3,192,128]{2,1,0:T(8,128)(2,1)}) custom-call(s32[6]{0:T(128)S(1)} %stack.51.at_ref, bf16[128,1280]{1,0:T(8,128)(2,1)S(1)} %copy-done.3, bf16[128,1280]{1,0:T(8,128)(2,1)S(1)} %copy-done.2, bf16[128,1280]{1,0:T(8,128)(2,1)S(1)} %copy-done.1), custom_call_target="tpu_custom_call" | custom-call | flops 754974720 | bytes 8388608 | tf_op jit(solution)/shard_map/pallas_call | solution.py:80
  33.0 1.9 collective-permute-start
  34.9 2.7 %collective-permute-start.1 = (bf16[3,192,128]{2,1,0:T(8,128)(2,1)}, bf16[3,192,128]{2,1,0:T(8,128)(2,1)S(1)}, u32[]{:S(2)}, u32[]{:S(2)}) collective-permute-start(bf16[3,192,128]{2,1,0:T(8,128)(2,1)} %get-tuple-element.26), channel_id=1, source_target_pairs={{0,128},{64,192},{128,0},{192,64},{1,129},{65,193},{129,1},{193,65... | collective-permute-start | bytes 442376 | tf_op jit(solution)/shard_map/ppermute | solution.py:420
  37.6 1.5 collective-permute-start.2
  39.0 21.8 %collective-permute-done = bf16[3,192,128]{2,1,0:T(8,128)(2,1)S(1)} collective-permute-done((bf16[3,192,128]{2,1,0:T(8,128)(2,1)}, bf16[3,192,128]{2,1,0:T(8,128)(2,1)S(1)}, u32[]{:S(2)}, u32[]{:S(2)}) %collective-permute-start) | collective-permute-done | bytes 147488 | tf_op jit(solution)/shard_map/ppermute | solution.py:420
  60.8 0.0 collective-permute-done.1
  60.8 0.0 collective-permute-done.2
  60.8 0.1 pad_maximum_fusion.mine_ref
  60.9 0.1 collective-permute-start.3
  61.0 1.9 collective-permute-done.3.other_ref
  62.9 0.0 all-to-all-done.1.rows_ref
  62.9 0.4 all-gather.3.cloned.1.call-done
  63.3 0.0 copy-start.5
  63.3 4.5 %shard_map.104 = (f32[8,512]{1,0:T(8,128)S(1)}, f32[8,512]{1,0:T(8,128)S(1)}) custom-call(f32[3]{0:T(128)S(1)} %copy-done.4, s32[6]{0:T(128)S(1)} %stack.51.at_ref, bf16[16,2,32,1024]{3,2,1,0:T(8,128)(2,1)S(1)} %all-to-all-done.1.rows_ref, bf16[16,2,32,1024]{3,2,1,0:T(8,128)(2,1)} %bitcast.25, f32[8,128]{1,0:T(8,128)S(1)} %get-tuple-element.30.own_ref), custom_call_target="tpu_custom_call" | custom-call | flops 1610612736 | bytes 8388608 | tf_op jit(solution)/shard_map/pallas_call | solution.py:159
  67.8 0.3 collective-permute-start.4
  68.1 1.0 collective-permute-done.4.got_ref
  69.1 0.6 shard_map.105
  69.6 18.7 %all_to_all.31.both_ref = f32[16,8,512]{2,1,0:T(8,128)S(1)} all-to-all(f32[16,8,512]{2,1,0:T(8,128)S(1)} %shard_map.105), channel_id=1, replica_groups={{0,2,4,6,8,10,12,14,16,18,20,22,24,26,28,30},{32,34,36,38,40,42,44,46,4..., dimensions={0} | all-to-all | bytes 524288 | tf_op jit(solution)/shard_map/all_to_all | solution.py:439
  88.3 0.6 shard_map.106.tot_ref
  88.9 0.3 collective-permute-start.5
  89.2 1.2 collective-permute-done.5.got_ref
  90.4 0.0 copy-done.5
  90.4 6.2 %shard_map.107 = (bf16[16,2,32,1024]{3,2,1,0:T(8,128)(2,1)}, bf16[8,2,32,1024]{3,2,1,0:T(8,128)(2,1)S(1)}, bf16[8,2,32,1024]{3,2,1,0:T(8,128)(2,1)S(1)}, f32[3,32,128]{2,1,0:T(8,128)S(1)}) custom-call(f32[3]{0:T(128)S(1)} %copy-done.4, s32[6]{0:T(128)S(1)} %stack.51.at_ref, bf16[16,2,32,1024]{3,2,1,0:T(8,128)(2,1)S(1)} %all-to-all-done.1.rows_ref, ...), custom_call_target="tpu_custom_call" | custom-call | flops 4831838208 | bytes 8388608 | tf_op jit(solution)/shard_map/pallas_call | solution.py:256
  96.6 0.3 collective-permute-start.6
  96.9 2.5 %collective-permute-done.6 = bf16[8,2,32,1024]{3,2,1,0:T(8,128)(2,1)S(1)} collective-permute-done((bf16[8,2,32,1024]{3,2,1,0:T(8,128)(2,1)S(1)}, bf16[8,2,32,1024]{3,2,1,0:T(8,128)(2,1)S(1)}, u32[]{:S(2)}, u32[]{:S(2)}) %collective-permute-start.6) | collective-permute-done | bytes 1048608 | tf_op jit(solution)/shard_map/ppermute | solution.py:446
  99.4 1.4 add_convert_fusion
  100.8 0.0 reduce-scatter.2.cloned.1.call-update
  100.8 33.2 %all_to_all.32.rows_ref = bf16[16,2,32,1024]{3,2,1,0:T(8,128)(2,1)S(1)} all-to-all(bf16[16,2,32,1024]{3,2,1,0:T(8,128)(2,1)} %get-tuple-element.33), channel_id=1, replica_groups=mesh['y'=4,'xh'=2,'z'=8,'xl'=2,'core'=2] {'y','xh','xl'}, dimensions={0} | all-to-all | bytes 4194304 | tf_op jit(solution)/shard_map/all_to_all | solution.py:25
  134.0 0.3 reduce-scatter.2.cloned.1.call-done
  134.3 0.0 copy-start.6
  134.3 2.0 %shard_map.108 = bf16[4,4,112,256]{3,2,1,0:T(8,128)(2,1)S(1)} custom-call(f32[3]{0:T(128)S(1)} %copy-done.4, s32[6]{0:T(128)S(1)} %stack.51.at_ref, bf16[16,2,32,1024]{3,2,1,0:T(8,128)(2,1)S(1)} %all_to_all.32.rows_ref, bf16[2,32,1024]{2,1,0:T(8,128)(2,1)} %bitcast.33, bf16[3,32,1024]{2,1,0:T(8,128)(2,1)} %get-tuple-element.36.emb_hbm, ...), custom_call_target="tpu_custom_call" | custom-call | flops 1000000 | bytes 8388608 | tf_op jit(solution)/shard_map/pallas_call | solution.py:339
  136.3 20.2 %all_to_all.33.d_ref = bf16[16,112,256]{2,1,0:T(8,128)(2,1)S(1)} all-to-all(bf16[16,112,256]{2,1,0:T(8,128)(2,1)S(1)} %bitcast.24), channel_id=1, replica_groups=mesh['y'=4,'xh'=2,'z'=8,'xl'=2,'core'=2] {'y','xl','core'}, dimensions={0} | all-to-all | bytes 1835008 | tf_op jit(solution)/shard_map/all_to_all | solution.py:25
  156.5 0.0 copy-done.6
  156.5 1.5 shard_map.109
  158.0 23.5 %all_to_all.34 = bf16[16,64,256]{2,1,0:T(8,128)(2,1)S(1)} all-to-all(bf16[16,64,256]{2,1,0:T(8,128)(2,1)S(1)} %shard_map.109), channel_id=1, replica_groups=mesh['y'=4,'xh'=2,'z'=8,'xl'=2,'core'=2] {'xh','z'}, dimensions={0} | all-to-all | bytes 1048576 | tf_op jit(solution)/shard_map/all_to_all | solution.py:25
  181.5 0.1 convert_reduce_fusion
  181.6 0.6 fusion.1
  182.2 0.6 fusion
  (1 shorter events, 0.0 us)
Async XLA Ops:
  7.2 1.1 copy-start
  7.2 3.8 %copy-start.1 = (bf16[128,1280]{1,0:T(8,128)(2,1)S(1)}, bf16[128,1280]{1,0:T(8,128)(2,1)}, u32[]{:S(2)}) copy-start(bf16[128,1280]{1,0:T(8,128)(2,1)} %f2_ref.1) | copy-start | bytes 983044
  7.2 3.8 %copy-start.7 = (bf16[1280,256]{1,0:T(8,128)(2,1)S(1)}, bf16[1280,256]{1,0:T(8,128)(2,1)}, u32[]{:S(2)}) copy-start(bf16[1280,256]{1,0:T(8,128)(2,1)} %param.12) | copy-start | bytes 1966084
  7.2 12.0 %copy-start.4 = (f32[3]{0:T(128)S(1)}, f32[3]{0:T(128)}, u32[]{:S(2)}) copy-start(f32[3]{0:T(128)} %t_ref.7) | copy-start | bytes 40
  7.2 56.1 %all-gather.3.cloned.1.call-start = ((), (), s32[]{:S(2)}) async-start(), calls=%async_computation.8 | async-start | bytes 2228224 | tf_op jit(solution)/shard_map/all_gather | solution.py:431
  21.6 7.2 %copy-start.2 = (bf16[128,1280]{1,0:T(8,128)(2,1)S(1)}, bf16[128,1280]{1,0:T(8,128)(2,1)}, u32[]{:S(2)}) copy-start(bf16[128,1280]{1,0:T(8,128)(2,1)} %f1_ref.1) | copy-start | bytes 983044
  21.6 41.3 %all-to-all-start.1 = ((bf16[16,2,32,1024]{3,2,1,0:T(8,128)(2,1)}), bf16[16,2,32,1024]{3,2,1,0:T(8,128)(2,1)S(1)}, u32[]{:S(2)}, u32[]{:S(2)}) async-start(bf16[16,2,32,1024]{3,2,1,0:T(8,128)(2,1)} %get-tuple-element.23), calls=%async_computation.1 | async-start | bytes 4194304 | tf_op jit(solution)/shard_map/all_to_all | solution.py:25
  28.6 105.7 %reduce-scatter.2.cloned.1.call-start = ((), (), s32[]{:S(2)}) async-start(), calls=%async_computation.7 | async-start | bytes 1179648 | tf_op jit(solution)/shard_map/reduce_scatter | solution.py:448
  28.7 1.0 copy-start.3
  33.0 27.9 %collective-permute-start = (bf16[3,192,128]{2,1,0:T(8,128)(2,1)}, bf16[3,192,128]{2,1,0:T(8,128)(2,1)S(1)}, u32[]{:S(2)}, u32[]{:S(2)}) collective-permute-start(bf16[3,192,128]{2,1,0:T(8,128)(2,1)} %get-tuple-element.25), channel_id=1, source_target_pairs={{0,64},{64,128},{128,192},{192,0},{1,65},{65,129},{129,193},{193,1... | collective-permute-start | bytes 442376 | tf_op jit(solution)/shard_map/ppermute | solution.py:420
  34.9 25.9 %collective-permute-start.1 = (bf16[3,192,128]{2,1,0:T(8,128)(2,1)}, bf16[3,192,128]{2,1,0:T(8,128)(2,1)S(1)}, u32[]{:S(2)}, u32[]{:S(2)}) collective-permute-start(bf16[3,192,128]{2,1,0:T(8,128)(2,1)} %get-tuple-element.26), channel_id=1, source_target_pairs={{0,128},{64,192},{128,0},{192,64},{1,129},{65,193},{129,1},{193,65... | collective-permute-start | bytes 442376 | tf_op jit(solution)/shard_map/ppermute | solution.py:420
  37.6 23.3 %collective-permute-start.2 = (bf16[3,192,128]{2,1,0:T(8,128)(2,1)}, bf16[3,192,128]{2,1,0:T(8,128)(2,1)S(1)}, u32[]{:S(2)}, u32[]{:S(2)}) collective-permute-start(bf16[3,192,128]{2,1,0:T(8,128)(2,1)} %get-tuple-element.27), channel_id=1, source_target_pairs={{0,192},{64,0},{128,64},{192,128},{1,193},{65,1},{129,65},{193,129... | collective-permute-start | bytes 442376 | tf_op jit(solution)/shard_map/ppermute | solution.py:420
  60.9 2.0 %collective-permute-start.3 = (bf16[3,3,192,128]{3,2,1,0:T(8,128)(2,1)S(1)}, bf16[3,3,192,128]{3,2,1,0:T(8,128)(2,1)}, u32[]{:S(2)}, u32[]{:S(2)}) collective-permute-start(bf16[3,3,192,128]{3,2,1,0:T(8,128)(2,1)S(1)} %pad_maximum_fusion.mine_ref), channel_id=1, source_target_pairs={{0,1},{1,0},{2,3},{3,2},{4,5},{5,4},{6,7},{7,6},{8,9},{9,8},{10,11... | collective-permute-start | bytes 1327112 | tf_op jit(solution)/shard_map/ppermute | solution.py:433
  63.3 27.1 %copy-start.5 = (bf16[32,32,1024]{2,1,0:T(8,128)(2,1)S(1)}, bf16[32,32,1024]{2,1,0:T(8,128)(2,1)}, u32[]{:S(2)}) copy-start(bf16[32,32,1024]{2,1,0:T(8,128)(2,1)} %all-gather.3.cloned.1.call-done) | copy-start | bytes 6291460
  67.8 1.3 collective-permute-start.4
  88.9 1.5 collective-permute-start.5
  96.6 2.7 %collective-permute-start.6 = (bf16[8,2,32,1024]{3,2,1,0:T(8,128)(2,1)S(1)}, bf16[8,2,32,1024]{3,2,1,0:T(8,128)(2,1)S(1)}, u32[]{:S(2)}, u32[]{:S(2)}) collective-permute-start(bf16[8,2,32,1024]{3,2,1,0:T(8,128)(2,1)S(1)} %get-tuple-element.35), channel_id=1, source_target_pairs={{0,1},{1,0},{2,3},{3,2},{4,5},{5,4},{6,7},{7,6},{8,9},{9,8},{10,11... | collective-permute-start | bytes 3145736 | tf_op jit(solution)/shard_map/ppermute | solution.py:446
  134.3 22.2 %copy-start.6 = (bf16[2,3,192,128]{3,2,1,0:T(8,128)(2,1)S(1)}, bf16[2,3,192,128]{3,2,1,0:T(8,128)(2,1)}, u32[]{:S(2)}) copy-start(bf16[2,3,192,128]{3,2,1,0:T(8,128)(2,1)} %get-tuple-element.39.own_ref) | copy-start | bytes 884740
Sparse Core Ops, SparseCore 0:
  21.7 41.5 all-gather.2
  100.9 33.3 reduce-scatter.1

commit v5 on v4

--- a/solution.py
+++ b/solution.py
@@ -23,11 +23,6 @@
 
 def exchange(pieces, axes):
     return lax.all_to_all(pieces, axes, split_axis=0, concat_axis=0, tiled=True)
-
-
-def spread(value, axes):
-    count = lax.axis_size(axes)
-    return exchange(jnp.broadcast_to(value[None], (count, *value.shape)), axes)
 
 
 def contract(left, right, dims):
@@ -85,6 +80,27 @@
         [pltpu.HBM(x, bf16) for x in shapes],
         flops=6 * n_y * n_z * line * feat * clips,
     )(at, *features)
+
+
+def project_kernel(*refs):
+    out_ref = refs[6]
+    parts, _, own, quarter = out_ref.shape
+    for m in range(3):
+        emb = contract(refs[m][...], refs[3 + m][...], ((1,), (0,))).astype(bf16)
+        out_ref[:, m] = emb.reshape(parts, own, quarter)
+
+
+def project(features, heads, parts):
+    clips, quarter = features[0].shape[0], heads[0].shape[1]
+    shape = (parts, 3, clips // parts, quarter)
+    return call(
+        project_kernel,
+        (1,),
+        [whole(x.shape) for x in features + heads],
+        whole(shape),
+        jax.ShapeDtypeStruct(shape, bf16),
+        flops=10**8,
+    )(*[far_memory(x) for x in features + heads])
 
 
 def unit_kernel(t_ref, emb_ref, all_ref, unit_ref, rows_ref, cols_ref, own_ref):
@@ -392,6 +408,28 @@
     )(at, d, own, mine, far_memory(other))
 
 
+def total_kernel(share, in_ref, loss_ref, *out_refs):
+    total = jnp.zeros(in_ref.shape[1:], f32)
+    for i in range(in_ref.shape[0]):
+        total += in_ref[i].astype(f32)
+    for m, ref in enumerate(out_refs):
+        ref[...] = total[m * share : (m + 1) * share]
+    loss = jnp.sum(total[3 * share : 3 * share + 3], axis=0, keepdims=True)
+    loss_ref[...] = loss[:, 0:1]
+
+
+def totals(pieces, share):
+    shapes = [(1, 1)] + [(share, pieces.shape[2])] * 3
+    return call(
+        functools.partial(total_kernel, share),
+        (1,),
+        [whole(pieces.shape)],
+        [whole(x) for x in shapes],
+        [jax.ShapeDtypeStruct(x, f32) for x in shapes],
+        flops=10**6,
+    )(pieces)
+
+
 def summing_groups(n_y, n_x, n_z, n_l):
     ids = np.arange(n_y * n_x * n_z * n_l * 2).reshape(n_y, n_x, n_z, n_l, 2)
     over_z = ids[..., 0].reshape(n_y * n_x, n_z * n_l)
@@ -422,10 +460,7 @@
     ]
     mine = jnp.stack(sent)
 
-    emb = jnp.stack(
-        [contract(f, h, ((1,), (0,))).astype(bf16) for f, h in zip(features, heads)]
-    )
-    emb = emb.reshape(3, emb_size, own, quarter).transpose(1, 0, 2, 3)
+    emb = project(features, heads, emb_size)
     emb, unit, rows, cols, own_scores = units(sharpness, exchange(emb, EMB), n_row)
 
     cols = lax.all_gather(cols, COL, axis=0)
@@ -454,9 +489,8 @@
     d_emb = exchange(d_emb.reshape(n_y * emb_size, 3 * own + 16, quarter), NEAR)
 
     out = head_gradients(at, d_emb, wide, mine, other, share, line)
-    out = jnp.sum(exchange(out, FAR).astype(f32), axis=0)
-    loss = out[3 * share, 0] + out[3 * share + 1, 0] + out[3 * share + 2, 0]
-    return loss, out[:share], out[share : 2 * share], out[2 * share : 3 * share]
+    loss, *out = totals(exchange(out, FAR), share)
+    return loss.reshape(()), *out
 
 
 def solution(mesh):

time: 193 us -> 188 us (0.974)
  local copies, waits for them, and re-layouts: 3.3 us -> 0.12 us
  between operations: 17.3 us -> 14.2 us
  matrix products: 2.93 us -> 0 us
  Pallas kernels: 21.1 us -> 24 us
    dot_general x3 -> x0, matrix products: 2.93 us -> none  [contract(): lax.dot_general(left, right, (dims, ((), ())), preferred_element_type=f32)]
    pallas_call x0 -> x2, Pallas kernels: none -> 2.9 us  [the longest x1 2.22 us: project(): call(project_kernel, (1,), [whole(x.shape) for x in features + heads], wh...]
    unnamed x16 -> x14, local copies, waits for them, and re-layouts: 2.01 us -> 0.03 us
where the time goes in v5:
time: 188 us; the launch traced here: 187 us
  blocking collectives  104 us (55%)
  waiting for transfers between devices  29.9 us (16%)
  Pallas kernels  24 us (13%)
  between operations  14.2 us (8%)
  starting transfers between devices  14 us (7%)
    all_to_all x4, blocking collectives, exchange(): return lax.all_to_all(pieces, axes, split_axis=0, concat_axis=0, tiled=True)  84.8 us
    ppermute x3, waiting for transfers between devices, shards(): lax.ppermute(piece, 'y', [(i, (i + step) % n_y) for i in range(n_y)])  22.7 us
    all_to_all x1, blocking collectives, shards(): lax.all_to_all(both, ('y', 'xh', 'z', 'xl', 'core'), 0, 0, axis_index_gro...  18.7 us
    all_to_all x1, starting transfers between devices, exchange(): return lax.all_to_all(pieces, axes, split_axis=0, concat_axis=0, tiled=True)  6.98 us
    pallas_call x1, Pallas kernels, products(): call(product_kernel, (1,), [scalars, scalars] + [whole(x.shape) for x in...  6.24 us
    ppermute x3, starting transfers between devices, shards(): lax.ppermute(piece, 'y', [(i, (i + step) % n_y) for i in range(n_y)])  6.06 us
    pallas_call x1, Pallas kernels, scores(): call(score_kernel, (1,), [scalars, scalars, whole(rows.shape), remote, wh...  4.5 us
  transfers between devices with their start and end apart: 10, of which 7 were waited for; matrix products, arithmetic and copies ran while one was open for 0% of the time, Pallas kernels for 2%

profile of v5, /device:TPU:32, one launch (start us, length us, event | category | flops | bytes accessed | tf_op | source)
XLA Modules:
  0.0 187.3 jit_solution(18309073224112843716)
XLA Ops:
  7.2 0.0 copy-start.3
  7.2 0.0 all-gather.3.cloned.1.call-start
  7.2 2.2 %shard_map.102 = bf16[4,3,32,256]{3,2,1,0:T(8,128)(2,1)S(1)} custom-call(bf16[128,1280]{1,0:T(8,128)(2,1)} %f0_ref.1, bf16[128,1280]{1,0:T(8,128)(2,1)} %f1_ref.1, bf16[128,1280]{1,0:T(8,128)(2,1)} %f2_ref.1, bf16[1280,256]{1,0:T(8,128)(2,1)} %refs_3_.1, bf16[1280,256]{1,0:T(8,128)(2,1)} %refs_4_.1, bf16[1280,256]{1,0:T(8,128)(2,1)} %refs_5_.1), custom_call_target="tpu_custom_call" | custom-call | flops 100000000 | bytes 8388608 | tf_op jit(solution)/shard_map/pallas_call | solution.py:96
  9.4 7.9 %all_to_all.30.emb_ref = bf16[4,3,32,256]{3,2,1,0:T(8,128)(2,1)S(1)} all-to-all(bf16[4,3,32,256]{3,2,1,0:T(8,128)(2,1)S(1)} %shard_map.102), channel_id=1, replica_groups=mesh['y'=4,'xh'=2,'z'=8,'xl'=2,'core'=2] {'xl','core'}, dimensions={0} | all-to-all | bytes 393216 | tf_op jit(solution)/shard_map/all_to_all | solution.py:25
  17.3 0.0 copy-done.3
  17.3 2.4 %shard_map.103 = (bf16[3,32,1024]{2,1,0:T(8,128)(2,1)}, bf16[3,32,1024]{2,1,0:T(8,128)(2,1)}, bf16[16,2,32,1024]{3,2,1,0:T(8,128)(2,1)}, bf16[2,32,1024]{2,1,0:T(8,128)(2,1)}, f32[8,128]{1,0:T(8,128)S(1)}) custom-call(f32[3]{0:T(128)S(1)} %copy-done.3, bf16[4,3,32,256]{3,2,1,0:T(8,128)(2,1)S(1)} %all_to_all.30.emb_ref), custom_call_target="tpu_custom_call" | custom-call | flops 1000000 | bytes 8388608 | tf_op jit(solution)/shard_map/pallas_call | solution.py:131
  19.7 0.0 all-gather.3.cloned.1.call-update
  19.7 0.0 copy-start
  19.8 0.0 copy-start.1
  19.8 0.0 copy-start.2
  19.8 7.0 %all-to-all-start.1 = ((bf16[16,2,32,1024]{3,2,1,0:T(8,128)(2,1)}), bf16[16,2,32,1024]{3,2,1,0:T(8,128)(2,1)S(1)}, u32[]{:S(2)}, u32[]{:S(2)}) async-start(bf16[16,2,32,1024]{3,2,1,0:T(8,128)(2,1)} %get-tuple-element.27), calls=%async_computation.1 | async-start | bytes 4194304 | tf_op jit(solution)/shard_map/all_to_all | solution.py:25
  26.8 0.0 reduce-scatter.2.cloned.1.call-start
  26.8 0.1 stack.39.at_ref
  26.9 0.0 copy-done
  26.9 0.0 copy-done.1
  26.9 0.0 copy-done.2
  26.9 3.3 %shard_map.104 = (bf16[2,3,192,128]{3,2,1,0:T(8,128)(2,1)}, bf16[3,192,128]{2,1,0:T(8,128)(2,1)}, bf16[3,192,128]{2,1,0:T(8,128)(2,1)}, bf16[3,192,128]{2,1,0:T(8,128)(2,1)}) custom-call(s32[6]{0:T(128)S(1)} %stack.39.at_ref, bf16[128,1280]{1,0:T(8,128)(2,1)S(1)} %copy-done, bf16[128,1280]{1,0:T(8,128)(2,1)S(1)} %copy-done.1, bf16[128,1280]{1,0:T(8,128)(2,1)S(1)} %copy-done.2), custom_call_target="tpu_custom_call" | custom-call | flops 754974720 | bytes 8388608 | tf_op jit(solution)/shard_map/pallas_call | solution.py:75
  30.2 1.9 %collective-permute-start = (bf16[3,192,128]{2,1,0:T(8,128)(2,1)}, bf16[3,192,128]{2,1,0:T(8,128)(2,1)S(1)}, u32[]{:S(2)}, u32[]{:S(2)}) collective-permute-start(bf16[3,192,128]{2,1,0:T(8,128)(2,1)} %get-tuple-element.29), channel_id=1, source_target_pairs={{0,64},{64,128},{128,192},{192,0},{1,65},{65,129},{129,193},{193,1... | collective-permute-start | bytes 442376 | tf_op jit(solution)/shard_map/ppermute | solution.py:458
  32.2 2.7 %collective-permute-start.1 = (bf16[3,192,128]{2,1,0:T(8,128)(2,1)}, bf16[3,192,128]{2,1,0:T(8,128)(2,1)S(1)}, u32[]{:S(2)}, u32[]{:S(2)}) collective-permute-start(bf16[3,192,128]{2,1,0:T(8,128)(2,1)} %get-tuple-element.30), channel_id=1, source_target_pairs={{0,128},{64,192},{128,0},{192,64},{1,129},{65,193},{129,1},{193,65... | collective-permute-start | bytes 442376 | tf_op jit(solution)/shard_map/ppermute | solution.py:458
  34.8 1.5 collective-permute-start.2
  36.3 22.7 %collective-permute-done = bf16[3,192,128]{2,1,0:T(8,128)(2,1)S(1)} collective-permute-done((bf16[3,192,128]{2,1,0:T(8,128)(2,1)}, bf16[3,192,128]{2,1,0:T(8,128)(2,1)S(1)}, u32[]{:S(2)}, u32[]{:S(2)}) %collective-permute-start) | collective-permute-done | bytes 147488 | tf_op jit(solution)/shard_map/ppermute | solution.py:458
  59.0 0.0 collective-permute-done.1
  59.0 0.0 collective-permute-done.2
  59.0 0.1 pad_maximum_fusion.mine_ref
  59.1 0.1 collective-permute-start.3
  59.2 1.8 collective-permute-done.3.other_ref
  61.0 0.0 copy-start.6
  61.0 0.0 all-to-all-done.1.rows_ref
  61.0 0.5 all-gather.3.cloned.1.call-done
  61.5 0.0 copy-start.4
  61.5 4.5 %shard_map.105 = (f32[8,512]{1,0:T(8,128)S(1)}, f32[8,512]{1,0:T(8,128)S(1)}) custom-call(f32[3]{0:T(128)S(1)} %copy-done.3, s32[6]{0:T(128)S(1)} %stack.39.at_ref, bf16[16,2,32,1024]{3,2,1,0:T(8,128)(2,1)S(1)} %all-to-all-done.1.rows_ref, bf16[16,2,32,1024]{3,2,1,0:T(8,128)(2,1)} %bitcast.14, f32[8,128]{1,0:T(8,128)S(1)} %get-tuple-element.34.own_ref), custom_call_target="tpu_custom_call" | custom-call | flops 1610612736 | bytes 8388608 | tf_op jit(solution)/shard_map/pallas_call | solution.py:175
  66.0 0.0 copy-done.6
  66.0 0.3 collective-permute-start.4
  66.3 1.0 collective-permute-done.4.got_ref
  67.3 0.6 shard_map.106
  67.8 18.7 %all_to_all.31.both_ref = f32[16,8,512]{2,1,0:T(8,128)S(1)} all-to-all(f32[16,8,512]{2,1,0:T(8,128)S(1)} %shard_map.106), channel_id=1, replica_groups={{0,2,4,6,8,10,12,14,16,18,20,22,24,26,28,30},{32,34,36,38,40,42,44,46,4..., dimensions={0} | all-to-all | bytes 524288 | tf_op jit(solution)/shard_map/all_to_all | solution.py:474
  86.6 0.6 shard_map.107.tot_ref
  87.2 0.3 collective-permute-start.5
  87.4 1.2 collective-permute-done.5.got_ref
  88.6 0.0 copy-done.4
  88.6 6.2 %shard_map.108 = (bf16[16,2,32,1024]{3,2,1,0:T(8,128)(2,1)}, bf16[8,2,32,1024]{3,2,1,0:T(8,128)(2,1)S(1)}, bf16[8,2,32,1024]{3,2,1,0:T(8,128)(2,1)S(1)}, f32[3,32,128]{2,1,0:T(8,128)S(1)}) custom-call(f32[3]{0:T(128)S(1)} %copy-done.3, s32[6]{0:T(128)S(1)} %stack.39.at_ref, bf16[16,2,32,1024]{3,2,1,0:T(8,128)(2,1)S(1)} %all-to-all-done.1.rows_ref, ...), custom_call_target="tpu_custom_call" | custom-call | flops 4831838208 | bytes 8388608 | tf_op jit(solution)/shard_map/pallas_call | solution.py:272
  94.9 0.3 collective-permute-start.6
  95.1 2.5 %collective-permute-done.6 = bf16[8,2,32,1024]{3,2,1,0:T(8,128)(2,1)S(1)} collective-permute-done((bf16[8,2,32,1024]{3,2,1,0:T(8,128)(2,1)S(1)}, bf16[8,2,32,1024]{3,2,1,0:T(8,128)(2,1)S(1)}, u32[]{:S(2)}, u32[]{:S(2)}) %collective-permute-start.6) | collective-permute-done | bytes 1048608 | tf_op jit(solution)/shard_map/ppermute | solution.py:481
  97.6 1.4 add_convert_fusion
  99.0 0.0 reduce-scatter.2.cloned.1.call-update
  99.0 33.3 %all_to_all.32.rows_ref = bf16[16,2,32,1024]{3,2,1,0:T(8,128)(2,1)S(1)} all-to-all(bf16[16,2,32,1024]{3,2,1,0:T(8,128)(2,1)} %get-tuple-element.37), channel_id=1, replica_groups=mesh['y'=4,'xh'=2,'z'=8,'xl'=2,'core'=2] {'y','xh','xl'}, dimensions={0} | all-to-all | bytes 4194304 | tf_op jit(solution)/shard_map/all_to_all | solution.py:25
  132.3 0.3 reduce-scatter.2.cloned.1.call-done
  132.6 0.0 copy-start.5
  132.6 2.0 %shard_map.109 = bf16[4,4,112,256]{3,2,1,0:T(8,128)(2,1)S(1)} custom-call(f32[3]{0:T(128)S(1)} %copy-done.3, s32[6]{0:T(128)S(1)} %stack.39.at_ref, bf16[16,2,32,1024]{3,2,1,0:T(8,128)(2,1)S(1)} %all_to_all.32.rows_ref, bf16[2,32,1024]{2,1,0:T(8,128)(2,1)} %bitcast.19, bf16[3,32,1024]{2,1,0:T(8,128)(2,1)} %get-tuple-element.40.emb_hbm, ...), custom_call_target="tpu_custom_call" | custom-call | flops 1000000 | bytes 8388608 | tf_op jit(solution)/shard_map/pallas_call | solution.py:355
  134.6 20.2 %all_to_all.33.d_ref = bf16[16,112,256]{2,1,0:T(8,128)(2,1)S(1)} all-to-all(bf16[16,112,256]{2,1,0:T(8,128)(2,1)S(1)} %bitcast.13), channel_id=1, replica_groups=mesh['y'=4,'xh'=2,'z'=8,'xl'=2,'core'=2] {'y','xl','core'}, dimensions={0} | all-to-all | bytes 1835008 | tf_op jit(solution)/shard_map/all_to_all | solution.py:25
  154.8 0.0 copy-done.5
  154.8 1.5 shard_map.110
  156.3 23.5 %all_to_all.34.in_ref = bf16[16,64,256]{2,1,0:T(8,128)(2,1)S(1)} all-to-all(bf16[16,64,256]{2,1,0:T(8,128)(2,1)S(1)} %shard_map.110), channel_id=1, replica_groups=mesh['y'=4,'xh'=2,'z'=8,'xl'=2,'core'=2] {'xh','z'}, dimensions={0} | all-to-all | bytes 1048576 | tf_op jit(solution)/shard_map/all_to_all | solution.py:25
  179.8 0.7 shard_map.111
Async XLA Ops:
  7.2 10.2 %copy-start.3 = (f32[3]{0:T(128)S(1)}, f32[3]{0:T(128)}, u32[]{:S(2)}) copy-start(f32[3]{0:T(128)} %t_ref.7) | copy-start | bytes 40
  7.2 54.3 %all-gather.3.cloned.1.call-start = ((), (), s32[]{:S(2)}) async-start(), calls=%async_computation.8 | async-start | bytes 2228224 | tf_op jit(solution)/shard_map/all_gather | solution.py:466
  19.7 7.2 %copy-start = (bf16[128,1280]{1,0:T(8,128)(2,1)S(1)}, bf16[128,1280]{1,0:T(8,128)(2,1)}, u32[]{:S(2)}) copy-start(bf16[128,1280]{1,0:T(8,128)(2,1)} %f0_ref.1) | copy-start | bytes 983044
  19.8 7.2 %copy-start.1 = (bf16[128,1280]{1,0:T(8,128)(2,1)S(1)}, bf16[128,1280]{1,0:T(8,128)(2,1)}, u32[]{:S(2)}) copy-start(bf16[128,1280]{1,0:T(8,128)(2,1)} %f1_ref.1) | copy-start | bytes 983044
  19.8 7.2 %copy-start.2 = (bf16[128,1280]{1,0:T(8,128)(2,1)S(1)}, bf16[128,1280]{1,0:T(8,128)(2,1)}, u32[]{:S(2)}) copy-start(bf16[128,1280]{1,0:T(8,128)(2,1)} %f2_ref.1) | copy-start | bytes 983044
  19.8 41.2 %all-to-all-start.1 = ((bf16[16,2,32,1024]{3,2,1,0:T(8,128)(2,1)}), bf16[16,2,32,1024]{3,2,1,0:T(8,128)(2,1)S(1)}, u32[]{:S(2)}, u32[]{:S(2)}) async-start(bf16[16,2,32,1024]{3,2,1,0:T(8,128)(2,1)} %get-tuple-element.27), calls=%async_computation.1 | async-start | bytes 4194304 | tf_op jit(solution)/shard_map/all_to_all | solution.py:25
  26.8 105.8 %reduce-scatter.2.cloned.1.call-start = ((), (), s32[]{:S(2)}) async-start(), calls=%async_computation.7 | async-start | bytes 1179648 | tf_op jit(solution)/shard_map/reduce_scatter | solution.py:483
  30.2 28.8 %collective-permute-start = (bf16[3,192,128]{2,1,0:T(8,128)(2,1)}, bf16[3,192,128]{2,1,0:T(8,128)(2,1)S(1)}, u32[]{:S(2)}, u32[]{:S(2)}) collective-permute-start(bf16[3,192,128]{2,1,0:T(8,128)(2,1)} %get-tuple-element.29), channel_id=1, source_target_pairs={{0,64},{64,128},{128,192},{192,0},{1,65},{65,129},{129,193},{193,1... | collective-permute-start | bytes 442376 | tf_op jit(solution)/shard_map/ppermute | solution.py:458
  32.2 26.9 %collective-permute-start.1 = (bf16[3,192,128]{2,1,0:T(8,128)(2,1)}, bf16[3,192,128]{2,1,0:T(8,128)(2,1)S(1)}, u32[]{:S(2)}, u32[]{:S(2)}) collective-permute-start(bf16[3,192,128]{2,1,0:T(8,128)(2,1)} %get-tuple-element.30), channel_id=1, source_target_pairs={{0,128},{64,192},{128,0},{192,64},{1,129},{65,193},{129,1},{193,65... | collective-permute-start | bytes 442376 | tf_op jit(solution)/shard_map/ppermute | solution.py:458
  34.8 24.2 %collective-permute-start.2 = (bf16[3,192,128]{2,1,0:T(8,128)(2,1)}, bf16[3,192,128]{2,1,0:T(8,128)(2,1)S(1)}, u32[]{:S(2)}, u32[]{:S(2)}) collective-permute-start(bf16[3,192,128]{2,1,0:T(8,128)(2,1)} %get-tuple-element.31), channel_id=1, source_target_pairs={{0,192},{64,0},{128,64},{192,128},{1,193},{65,1},{129,65},{193,129... | collective-permute-start | bytes 442376 | tf_op jit(solution)/shard_map/ppermute | solution.py:458
  59.1 1.9 %collective-permute-start.3 = (bf16[3,3,192,128]{3,2,1,0:T(8,128)(2,1)S(1)}, bf16[3,3,192,128]{3,2,1,0:T(8,128)(2,1)S(1)}, u32[]{:S(2)}, u32[]{:S(2)}) collective-permute-start(bf16[3,3,192,128]{3,2,1,0:T(8,128)(2,1)S(1)} %pad_maximum_fusion.mine_ref), channel_id=1, source_target_pairs={{0,1},{1,0},{2,3},{3,2},{4,5},{5,4},{6,7},{7,6},{8,9},{9,8},{10,11... | collective-permute-start | bytes 1327112 | tf_op jit(solution)/shard_map/ppermute | solution.py:468
  61.0 5.0 %copy-start.6 = (bf16[3,3,192,128]{3,2,1,0:T(8,128)(2,1)}, bf16[3,3,192,128]{3,2,1,0:T(8,128)(2,1)S(1)}, u32[]{:S(2)}) copy-start(bf16[3,3,192,128]{3,2,1,0:T(8,128)(2,1)S(1)} %collective-permute-done.3.other_ref) | copy-start | bytes 1327108
  61.5 27.1 %copy-start.4 = (bf16[32,32,1024]{2,1,0:T(8,128)(2,1)S(1)}, bf16[32,32,1024]{2,1,0:T(8,128)(2,1)}, u32[]{:S(2)}) copy-start(bf16[32,32,1024]{2,1,0:T(8,128)(2,1)} %all-gather.3.cloned.1.call-done) | copy-start | bytes 6291460
  66.0 1.3 collective-permute-start.4
  87.2 1.5 collective-permute-start.5
  94.9 2.7 %collective-permute-start.6 = (bf16[8,2,32,1024]{3,2,1,0:T(8,128)(2,1)S(1)}, bf16[8,2,32,1024]{3,2,1,0:T(8,128)(2,1)S(1)}, u32[]{:S(2)}, u32[]{:S(2)}) collective-permute-start(bf16[8,2,32,1024]{3,2,1,0:T(8,128)(2,1)S(1)} %get-tuple-element.39), channel_id=1, source_target_pairs={{0,1},{1,0},{2,3},{3,2},{4,5},{5,4},{6,7},{7,6},{8,9},{9,8},{10,11... | collective-permute-start | bytes 3145736 | tf_op jit(solution)/shard_map/ppermute | solution.py:481
  132.6 22.2 %copy-start.5 = (bf16[2,3,192,128]{3,2,1,0:T(8,128)(2,1)S(1)}, bf16[2,3,192,128]{3,2,1,0:T(8,128)(2,1)}, u32[]{:S(2)}) copy-start(bf16[2,3,192,128]{3,2,1,0:T(8,128)(2,1)} %get-tuple-element.43.own_ref) | copy-start | bytes 884740
Sparse Core Ops, SparseCore 0:
  19.9 41.5 all-gather.2
  99.2 33.3 reduce-scatter.1

commit v6 on v5

--- a/solution.py
+++ b/solution.py
@@ -83,28 +83,37 @@
 
 
 def project_kernel(*refs):
-    out_ref = refs[6]
+    arrays, out_ref, buffers, sems = refs[:6], refs[6], refs[7:13], refs[13]
     parts, _, own, quarter = out_ref.shape
+    copies = [pltpu.make_async_copy(arrays[i], buffers[i], sems.at[i]) for i in range(6)]
     for m in range(3):
-        emb = contract(refs[m][...], refs[3 + m][...], ((1,), (0,))).astype(bf16)
+        copies[m].start()
+        copies[3 + m].start()
+    for m in range(3):
+        copies[m].wait()
+        copies[3 + m].wait()
+        emb = contract(buffers[m][...], buffers[3 + m][...], ((1,), (0,))).astype(bf16)
         out_ref[:, m] = emb.reshape(parts, own, quarter)
 
 
 def project(features, heads, parts):
     clips, quarter = features[0].shape[0], heads[0].shape[1]
     shape = (parts, 3, clips // parts, quarter)
+    arrays = features + heads
     return call(
         project_kernel,
         (1,),
-        [whole(x.shape) for x in features + heads],
+        [remote] * 6,
         whole(shape),
         jax.ShapeDtypeStruct(shape, bf16),
+        [pltpu.VMEM(x.shape, bf16) for x in arrays] + [pltpu.SemaphoreType.DMA((6,))],
         flops=10**8,
-    )(*[far_memory(x) for x in features + heads])
-
-
-def unit_kernel(t_ref, emb_ref, all_ref, unit_ref, rows_ref, cols_ref, own_ref):
+    )(*[far_memory(x) for x in arrays])
+
+
+def unit_kernel(t_ref, emb_ref, all_ref, unit_ref, cols_ref, rows_ref, own_ref):
     parts, _, own, quarter = emb_ref.shape
+    units = []
     for m in range(3):
         emb = jnp.concatenate([emb_ref[e, m] for e in range(parts)], axis=1)
         values = emb.astype(f32)
@@ -112,30 +121,47 @@
         unit = (values / length).astype(bf16)
         all_ref[m] = emb
         unit_ref[m] = unit
+        units.append(unit.astype(f32))
         if m > 0:
             cols_ref[m - 1] = unit
         if m < 2:
-            for copy in range(rows_ref.shape[0]):
-                rows_ref[copy, m] = unit
+            rows_ref[m] = unit
     total = jnp.zeros((1, parts * quarter), f32)
     for p, (a, b) in enumerate(couples):
-        product = unit_ref[a].astype(f32) * unit_ref[b].astype(f32)
-        total += t_ref[p] * jnp.sum(product, axis=0, keepdims=True)
+        total += t_ref[p] * jnp.sum(units[a] * units[b], axis=0, keepdims=True)
     own_ref[...] = jnp.broadcast_to(jnp.sum(total, axis=1, keepdims=True), own_ref.shape)
 
 
-def units(t, emb, copies):
+def units(t, emb):
     parts, _, own, quarter = emb.shape
     full = (3, own, parts * quarter)
-    shapes = [full, full, (copies, 2, *full[1:]), (2, *full[1:])]
+    two = (2, *full[1:])
     return call(
         unit_kernel,
         (1,),
         [scalars, whole(emb.shape)],
-        [whole(x) for x in shapes] + [whole((8, LANES))],
-        [pltpu.HBM(x, bf16) for x in shapes] + [jax.ShapeDtypeStruct((8, LANES), f32)],
+        [whole(x) for x in (full, full, two, two, (8, LANES))],
+        [pltpu.HBM(x, bf16) for x in (full, full, two)]
+        + [jax.ShapeDtypeStruct(two, bf16), jax.ShapeDtypeStruct((8, LANES), f32)],
         flops=10**6,
     )(t, emb)
+
+
+def copies_kernel(in_ref, out_ref):
+    for i in range(out_ref.shape[0]):
+        out_ref[i] = in_ref[...]
+
+
+def copies_of(value, count):
+    zeros = (0,) * value.ndim
+    return call(
+        copies_kernel,
+        (2,),
+        [whole(value.shape)],
+        pl.BlockSpec((count // 2, *value.shape), lambda i: (i, *zeros)),
+        pltpu.HBM((count, *value.shape), value.dtype),
+        flops=10**6,
+    )(value)
 
 
 def far_memory(value):
@@ -219,7 +245,7 @@
 
 
 def product_kernel(
-    t_ref, at_ref, rows_ref, cols_ref, tot_ref, got_ref, out_hbm, keep_ref, send_ref, w_ref, hr_ref, out_ref, sems
+    t_ref, at_ref, rows_ref, cols_ref, tot_ref, got_ref, g_ref, keep_ref, send_ref, w_ref, hr_ref
 ):
     n_row, _, own, width = rows_ref.shape
     block = n_row * own
@@ -244,14 +270,7 @@
         half = jnp.concatenate([hr_ref[p]] * (block // LANES), axis=1)
         g = shifted_scores(t_ref[p], rows[a], cols[b]) * (half + col[p : p + 1])
         grads.append(jnp.where(own_term, 0.0, g).astype(bf16))
-    d0 = t_ref[0] * contract(grads[0], cols[0], ((1,), (0,)))
-    d0 += t_ref[1] * contract(grads[1], cols[1], ((1,), (0,)))
-    d1 = t_ref[2] * contract(grads[2], cols[1], ((1,), (0,)))
-    copies = []
-    for m, d in enumerate((d0, d1)):
-        out_ref[m] = d.astype(bf16).reshape(n_row, own, width)
-        copies.append(pltpu.make_async_copy(out_ref.at[m], out_hbm.at[:, m], sems.at[m]))
-        copies[m].start()
+        g_ref[p] = grads[p]
     d1 = t_ref[0] * contract(grads[0], rows[0], ((0,), (0,)))
     d2 = t_ref[1] * contract(grads[1], rows[0], ((0,), (0,)))
     d2 += t_ref[2] * contract(grads[2], rows[1], ((0,), (0,)))
@@ -261,8 +280,34 @@
             high = d[(2 * i + 1) * own : (2 * i + 2) * own]
             keep_ref[i, m] = jnp.where(my_core == 0, low, high).astype(bf16)
             send_ref[i, m] = jnp.where(my_core == 0, high, low).astype(bf16)
+
+
+def row_kernel(t_ref, g_ref, cols_ref, out_hbm, out_ref, sems):
+    n_row, own, width = out_ref.shape[1:]
+    cols = [cols_ref[:, m].reshape(cols_ref.shape[0] * own, width) for m in range(2)]
+    d0 = t_ref[0] * contract(g_ref[0], cols[0], ((1,), (0,)))
+    d0 += t_ref[1] * contract(g_ref[1], cols[1], ((1,), (0,)))
+    copies = []
+    for m in range(2):
+        d = d0 if m == 0 else t_ref[2] * contract(g_ref[2], cols[1], ((1,), (0,)))
+        out_ref[m] = d.astype(bf16).reshape(n_row, own, width)
+        copies.append(pltpu.make_async_copy(out_ref.at[m], out_hbm.at[:, m], sems.at[m]))
+        copies[m].start()
     for copy in copies:
         copy.wait()
+
+
+def row_products(t, g, cols):
+    n_row, _, own, width = cols.shape
+    return call(
+        row_kernel,
+        (1,),
+        [scalars, whole(g.shape), whole(cols.shape)],
+        remote,
+        pltpu.HBM(cols.shape, bf16),
+        [pltpu.VMEM((2, n_row, own, width), bf16), pltpu.SemaphoreType.DMA((2,))],
+        flops=6 * (n_row * own) ** 2 * width,
+    )(t, g, cols)
 
 
 def products(t, at, rows, cols, tot, got):
@@ -273,19 +318,15 @@
         product_kernel,
         (1,),
         [scalars, scalars] + [whole(x.shape) for x in (rows, cols, tot, got)],
-        [remote, whole(half), whole(half), whole((3, own, LANES))],
+        [whole((3, block, block)), whole(half), whole(half), whole((3, own, LANES))],
         [
-            pltpu.HBM(rows.shape, bf16),
+            jax.ShapeDtypeStruct((3, block, block), bf16),
             jax.ShapeDtypeStruct(half, bf16),
             jax.ShapeDtypeStruct(half, bf16),
             jax.ShapeDtypeStruct((3, own, LANES), f32),
         ],
-        [
-            pltpu.VMEM((4, block, LANES), f32),
-            pltpu.VMEM((2, n_row, own, width), bf16),
-            pltpu.SemaphoreType.DMA((2,)),
-        ],
-        flops=18 * block * block * width,
+        [pltpu.VMEM((4, block, LANES), f32)],
+        flops=12 * block * block * width,
     )(t, at, rows, cols, tot, got)
 
 
@@ -461,14 +502,15 @@
     mine = jnp.stack(sent)
 
     emb = project(features, heads, emb_size)
-    emb, unit, rows, cols, own_scores = units(sharpness, exchange(emb, EMB), n_row)
+    emb, unit, cols, rows, own_scores = units(sharpness, exchange(emb, EMB))
 
     cols = lax.all_gather(cols, COL, axis=0)
-    rows = exchange(rows, ROW)
+    rows = exchange(copies_of(rows, n_row), ROW)
+    rows, wide, mine = lax.optimization_barrier((rows, wide, mine))
     other = lax.ppermute(mine, "core", swap)
-    rows, wide, mine, other = lax.optimization_barrier((rows, wide, mine, other))
 
     send, keep = scores(sharpness, at, rows, cols, own_scores)
+    send, keep, other = lax.optimization_barrier((send, keep, other))
     both = small(gather_kernel, at, (keep, lax.ppermute(send, "core", swap)), (n_row, 8, block_r))
     groups = summing_groups(n_y, n_x, n_z, 2)
     both = lax.all_to_all(
@@ -477,8 +519,10 @@
     tot = small(sum_kernel, at, (both,), (8, block_r))
     got = lax.ppermute(tot, "core", swap)
 
-    d_rows, keep, send, w = products(sharpness, at, rows, cols, tot, got)
+    grad, keep, send, w = products(sharpness, at, rows, cols, tot, got)
     received = lax.ppermute(send, "core", swap)
+    d_rows = row_products(sharpness, grad, cols)
+    received, d_rows = lax.optimization_barrier((received, d_rows))
     d_cols = (keep.astype(f32) + received.astype(f32)).astype(bf16)
     d_cols = lax.psum_scatter(d_cols, "z", scatter_dimension=0)
     d_rows = exchange(d_rows, ROW)

time: 188 us -> 186 us (0.989)
  waiting for transfers between devices: 29.9 us -> 25.8 us
  Pallas kernels: 24 us -> 26.1 us
    pallas_call x2 -> x4, Pallas kernels: 4.59 us -> 8.4 us  [the longest x1 3.4 us: row_products(): call(row_kernel, (1,), [scalars, whole(g.shape), whole(cols.shape)], remo...]
    ppermute x1, waiting for transfers between devices: 2.5 us -> 0.01 us  [shards(): received = lax.ppermute(send, 'core', swap)]
  transfers between devices with their start and end apart: 10 -> 10, of which waited for: 7 -> 4; matrix products, arithmetic and copies ran while one was open for 0% -> 0% of each run, Pallas kernels for 2% -> 7%
where the time goes in v6:
time: 186 us; the launch traced here: 185 us
  blocking collectives  103 us (55%)
  Pallas kernels  26.1 us (14%)
  waiting for transfers between devices  25.8 us (14%)
  between operations  14.2 us (8%)
  starting transfers between devices  14 us (8%)
    all_to_all x4, blocking collectives, exchange(): return lax.all_to_all(pieces, axes, split_axis=0, concat_axis=0, tiled=True)  85.1 us
    ppermute x3, waiting for transfers between devices, shards(): lax.ppermute(piece, 'y', [(i, (i + step) % n_y) for i in range(n_y)])  22.7 us
    all_to_all x1, blocking collectives, shards(): lax.all_to_all(both, ('y', 'xh', 'z', 'xl', 'core'), 0, 0, axis_index_gro...  18.3 us
    all_to_all x1, starting transfers between devices, exchange(): return lax.all_to_all(pieces, axes, split_axis=0, concat_axis=0, tiled=True)  6.97 us
    ppermute x3, starting transfers between devices, shards(): lax.ppermute(piece, 'y', [(i, (i + step) % n_y) for i in range(n_y)])  6.06 us
    pallas_call x1, Pallas kernels, scores(): call(score_kernel, (1,), [scalars, scalars, whole(rows.shape), remote, wh...  4.51 us
    pallas_call x1, Pallas kernels, products(): call(product_kernel, (1,), [scalars, scalars] + [whole(x.shape) for x in...  4.46 us
  transfers between devices with their start and end apart: 10, of which 4 were waited for; matrix products, arithmetic and copies ran while one was open for 0% of the time, Pallas kernels for 7%

profile of v6, /device:TPU:32, one launch (start us, length us, event | category | flops | bytes accessed | tf_op | source)
XLA Modules:
  0.0 185.1 jit_solution(16978219865537610549)
XLA Ops:
  7.2 0.0 copy-start.3
  7.2 0.0 all-gather.3.cloned.1.call-start
  7.2 2.2 %shard_map.102 = bf16[4,3,32,256]{3,2,1,0:T(8,128)(2,1)S(1)} custom-call(bf16[128,1280]{1,0:T(8,128)(2,1)} %f0_ref.1, bf16[128,1280]{1,0:T(8,128)(2,1)} %f1_ref.1, bf16[128,1280]{1,0:T(8,128)(2,1)} %f2_ref.1, bf16[1280,256]{1,0:T(8,128)(2,1)} %refs_3_.1, bf16[1280,256]{1,0:T(8,128)(2,1)} %refs_4_.1, bf16[1280,256]{1,0:T(8,128)(2,1)} %refs_5_.1), custom_call_target="tpu_custom_call" | custom-call | flops 100000000 | bytes 8388608 | tf_op jit(solution)/shard_map/pallas_call | solution.py:103
  9.4 7.9 %all_to_all.30.emb_ref = bf16[4,3,32,256]{3,2,1,0:T(8,128)(2,1)S(1)} all-to-all(bf16[4,3,32,256]{3,2,1,0:T(8,128)(2,1)S(1)} %shard_map.102), channel_id=1, replica_groups=mesh['y'=4,'xh'=2,'z'=8,'xl'=2,'core'=2] {'xl','core'}, dimensions={0} | all-to-all | bytes 393216 | tf_op jit(solution)/shard_map/all_to_all | solution.py:25
  17.3 0.0 copy-done.3
  17.3 1.4 shard_map.103
  18.7 0.0 all-gather.3.cloned.1.call-update
  18.8 1.4 shard_map.104
  20.2 0.0 copy-start
  20.2 0.0 copy-start.1
  20.2 0.0 copy-start.2
  20.2 7.0 %all-to-all-start.1 = ((bf16[16,2,32,1024]{3,2,1,0:T(8,128)(2,1)}), bf16[16,2,32,1024]{3,2,1,0:T(8,128)(2,1)S(1)}, u32[]{:S(2)}, u32[]{:S(2)}) async-start(bf16[16,2,32,1024]{3,2,1,0:T(8,128)(2,1)} %shard_map.104), calls=%async_computation.1 | async-start | bytes 4194304 | tf_op jit(solution)/shard_map/all_to_all | solution.py:25
  27.1 0.0 reduce-scatter.2.cloned.1.call-start
  27.2 0.1 stack.39.at_ref
  27.3 0.0 copy-done
  27.3 0.0 copy-done.1
  27.3 0.0 copy-done.2
  27.3 3.3 %shard_map.105 = (bf16[2,3,192,128]{3,2,1,0:T(8,128)(2,1)}, bf16[3,192,128]{2,1,0:T(8,128)(2,1)}, bf16[3,192,128]{2,1,0:T(8,128)(2,1)}, bf16[3,192,128]{2,1,0:T(8,128)(2,1)}) custom-call(s32[6]{0:T(128)S(1)} %stack.39.at_ref, bf16[128,1280]{1,0:T(8,128)(2,1)S(1)} %copy-done, bf16[128,1280]{1,0:T(8,128)(2,1)S(1)} %copy-done.1, bf16[128,1280]{1,0:T(8,128)(2,1)S(1)} %copy-done.2), custom_call_target="tpu_custom_call" | custom-call | flops 754974720 | bytes 8388608 | tf_op jit(solution)/shard_map/pallas_call | solution.py:75
  30.6 1.9 %collective-permute-start = (bf16[3,192,128]{2,1,0:T(8,128)(2,1)}, bf16[3,192,128]{2,1,0:T(8,128)(2,1)S(1)}, u32[]{:S(2)}, u32[]{:S(2)}) collective-permute-start(bf16[3,192,128]{2,1,0:T(8,128)(2,1)} %get-tuple-element.33), channel_id=1, source_target_pairs={{0,64},{64,128},{128,192},{192,0},{1,65},{65,129},{129,193},{193,1... | collective-permute-start | bytes 442376 | tf_op jit(solution)/shard_map/ppermute | solution.py:499
  32.5 2.7 %collective-permute-start.1 = (bf16[3,192,128]{2,1,0:T(8,128)(2,1)}, bf16[3,192,128]{2,1,0:T(8,128)(2,1)S(1)}, u32[]{:S(2)}, u32[]{:S(2)}) collective-permute-start(bf16[3,192,128]{2,1,0:T(8,128)(2,1)} %get-tuple-element.34), channel_id=1, source_target_pairs={{0,128},{64,192},{128,0},{192,64},{1,129},{65,193},{129,1},{193,65... | collective-permute-start | bytes 442376 | tf_op jit(solution)/shard_map/ppermute | solution.py:499
  35.2 1.5 collective-permute-start.2
  36.7 22.7 %collective-permute-done = bf16[3,192,128]{2,1,0:T(8,128)(2,1)S(1)} collective-permute-done((bf16[3,192,128]{2,1,0:T(8,128)(2,1)}, bf16[3,192,128]{2,1,0:T(8,128)(2,1)S(1)}, u32[]{:S(2)}, u32[]{:S(2)}) %collective-permute-start) | collective-permute-done | bytes 147488 | tf_op jit(solution)/shard_map/ppermute | solution.py:499
  59.4 0.0 collective-permute-done.1
  59.4 0.0 collective-permute-done.2
  59.4 0.1 pad_maximum_fusion.mine_ref
  59.5 0.0 all-to-all-done.1.rows_ref
  59.5 0.1 collective-permute-start.3
  59.6 0.9 all-gather.3.cloned.1.call-done
  60.5 0.0 copy-start.4
  60.5 4.5 %shard_map.106 = (f32[8,512]{1,0:T(8,128)S(1)}, f32[8,512]{1,0:T(8,128)S(1)}) custom-call(f32[3]{0:T(128)S(1)} %copy-done.3, s32[6]{0:T(128)S(1)} %stack.39.at_ref, bf16[16,2,32,1024]{3,2,1,0:T(8,128)(2,1)S(1)} %all-to-all-done.1.rows_ref, bf16[16,2,32,1024]{3,2,1,0:T(8,128)(2,1)} %bitcast.14, f32[8,128]{1,0:T(8,128)S(1)} %get-tuple-element.38.own_ref), custom_call_target="tpu_custom_call" | custom-call | flops 1610612736 | bytes 8388608 | tf_op jit(solution)/shard_map/pallas_call | solution.py:201
  65.0 0.0 collective-permute-done.3.other_ref
  65.0 0.0 copy-start.6
  65.0 0.3 collective-permute-start.4
  65.3 1.0 collective-permute-done.4.got_ref
  66.3 0.6 shard_map.107
  66.9 18.3 %all_to_all.31.both_ref = f32[16,8,512]{2,1,0:T(8,128)S(1)} all-to-all(f32[16,8,512]{2,1,0:T(8,128)S(1)} %shard_map.107), channel_id=1, replica_groups={{0,2,4,6,8,10,12,14,16,18,20,22,24,26,28,30},{32,34,36,38,40,42,44,46,4..., dimensions={0} | all-to-all | bytes 524288 | tf_op jit(solution)/shard_map/all_to_all | solution.py:516
  85.2 0.6 shard_map.108.tot_ref
  85.8 0.3 collective-permute-start.5
  86.0 1.2 collective-permute-done.5.got_ref
  87.2 0.0 copy-done.4
  87.2 4.5 %shard_map.109 = (bf16[3,512,512]{2,1,0:T(8,128)(2,1)S(1)}, bf16[8,2,32,1024]{3,2,1,0:T(8,128)(2,1)S(1)}, bf16[8,2,32,1024]{3,2,1,0:T(8,128)(2,1)S(1)}, f32[3,32,128]{2,1,0:T(8,128)S(1)}) custom-call(f32[3]{0:T(128)S(1)} %copy-done.3, s32[6]{0:T(128)S(1)} %stack.39.at_ref, bf16[16,2,32,1024]{3,2,1,0:T(8,128)(2,1)S(1)} %all-to-all-done.1.rows_ref, ...), custom_call_target="tpu_custom_call" | custom-call | flops 3221225472 | bytes 8388608 | tf_op jit(solution)/shard_map/pallas_call | solution.py:317
  91.7 0.0 copy-done.6
  91.7 0.3 collective-permute-start.6
  91.9 3.4 %shard_map.110 = bf16[16,2,32,1024]{3,2,1,0:T(8,128)(2,1)} custom-call(f32[3]{0:T(128)S(1)} %copy-done.3, bf16[3,512,512]{2,1,0:T(8,128)(2,1)S(1)} %get-tuple-element.45.g_ref, bf16[16,2,32,1024]{3,2,1,0:T(8,128)(2,1)S(1)} %bitcast.16), custom_call_target="tpu_custom_call" | custom-call | flops 1610612736 | bytes 8388608 | tf_op jit(solution)/shard_map/pallas_call | solution.py:302
  95.3 0.0 collective-permute-done.6
  95.4 1.4 add_convert_fusion
  96.8 0.0 reduce-scatter.2.cloned.1.call-update
  96.8 33.5 %all_to_all.32.rows_ref = bf16[16,2,32,1024]{3,2,1,0:T(8,128)(2,1)S(1)} all-to-all(bf16[16,2,32,1024]{3,2,1,0:T(8,128)(2,1)} %shard_map.110), channel_id=1, replica_groups=mesh['y'=4,'xh'=2,'z'=8,'xl'=2,'core'=2] {'y','xh','xl'}, dimensions={0} | all-to-all | bytes 4194304 | tf_op jit(solution)/shard_map/all_to_all | solution.py:25
  130.3 0.0 reduce-scatter.2.cloned.1.call-done
  130.3 0.0 copy-start.5
  130.3 2.0 %shard_map.111 = bf16[4,4,112,256]{3,2,1,0:T(8,128)(2,1)S(1)} custom-call(f32[3]{0:T(128)S(1)} %copy-done.3, s32[6]{0:T(128)S(1)} %stack.39.at_ref, bf16[16,2,32,1024]{3,2,1,0:T(8,128)(2,1)S(1)} %all_to_all.32.rows_ref, bf16[2,32,1024]{2,1,0:T(8,128)(2,1)} %bitcast.20, bf16[3,32,1024]{2,1,0:T(8,128)(2,1)} %get-tuple-element.49.emb_hbm, ...), custom_call_target="tpu_custom_call" | custom-call | flops 1000000 | bytes 8388608 | tf_op jit(solution)/shard_map/pallas_call | solution.py:396
  132.3 20.3 %all_to_all.33.d_ref = bf16[16,112,256]{2,1,0:T(8,128)(2,1)S(1)} all-to-all(bf16[16,112,256]{2,1,0:T(8,128)(2,1)S(1)} %bitcast.13), channel_id=1, replica_groups=mesh['y'=4,'xh'=2,'z'=8,'xl'=2,'core'=2] {'y','xl','core'}, dimensions={0} | all-to-all | bytes 1835008 | tf_op jit(solution)/shard_map/all_to_all | solution.py:25
  152.6 0.0 copy-done.5
  152.6 1.5 shard_map.112
  154.1 23.5 %all_to_all.34.in_ref = bf16[16,64,256]{2,1,0:T(8,128)(2,1)S(1)} all-to-all(bf16[16,64,256]{2,1,0:T(8,128)(2,1)S(1)} %shard_map.112), channel_id=1, replica_groups=mesh['y'=4,'xh'=2,'z'=8,'xl'=2,'core'=2] {'xh','z'}, dimensions={0} | all-to-all | bytes 1048576 | tf_op jit(solution)/shard_map/all_to_all | solution.py:25
  177.6 0.7 shard_map.113
Async XLA Ops:
  7.2 10.1 %copy-start.3 = (f32[3]{0:T(128)S(1)}, f32[3]{0:T(128)}, u32[]{:S(2)}) copy-start(f32[3]{0:T(128)} %t_ref.9) | copy-start | bytes 40
  7.2 53.3 %all-gather.3.cloned.1.call-start = ((), (), s32[]{:S(2)}) async-start(), calls=%async_computation.8 | async-start | bytes 2228224 | tf_op jit(solution)/shard_map/all_gather | solution.py:507
  20.2 7.1 %copy-start = (bf16[128,1280]{1,0:T(8,128)(2,1)S(1)}, bf16[128,1280]{1,0:T(8,128)(2,1)}, u32[]{:S(2)}) copy-start(bf16[128,1280]{1,0:T(8,128)(2,1)} %f0_ref.1) | copy-start | bytes 983044
  20.2 7.1 %copy-start.1 = (bf16[128,1280]{1,0:T(8,128)(2,1)S(1)}, bf16[128,1280]{1,0:T(8,128)(2,1)}, u32[]{:S(2)}) copy-start(bf16[128,1280]{1,0:T(8,128)(2,1)} %f1_ref.1) | copy-start | bytes 983044
  20.2 7.1 %copy-start.2 = (bf16[128,1280]{1,0:T(8,128)(2,1)S(1)}, bf16[128,1280]{1,0:T(8,128)(2,1)}, u32[]{:S(2)}) copy-start(bf16[128,1280]{1,0:T(8,128)(2,1)} %f2_ref.1) | copy-start | bytes 983044
  20.2 39.3 %all-to-all-start.1 = ((bf16[16,2,32,1024]{3,2,1,0:T(8,128)(2,1)}), bf16[16,2,32,1024]{3,2,1,0:T(8,128)(2,1)S(1)}, u32[]{:S(2)}, u32[]{:S(2)}) async-start(bf16[16,2,32,1024]{3,2,1,0:T(8,128)(2,1)} %shard_map.104), calls=%async_computation.1 | async-start | bytes 4194304 | tf_op jit(solution)/shard_map/all_to_all | solution.py:25
  27.1 103.1 %reduce-scatter.2.cloned.1.call-start = ((), (), s32[]{:S(2)}) async-start(), calls=%async_computation.7 | async-start | bytes 1179648 | tf_op jit(solution)/shard_map/reduce_scatter | solution.py:527
  30.6 28.8 %collective-permute-start = (bf16[3,192,128]{2,1,0:T(8,128)(2,1)}, bf16[3,192,128]{2,1,0:T(8,128)(2,1)S(1)}, u32[]{:S(2)}, u32[]{:S(2)}) collective-permute-start(bf16[3,192,128]{2,1,0:T(8,128)(2,1)} %get-tuple-element.33), channel_id=1, source_target_pairs={{0,64},{64,128},{128,192},{192,0},{1,65},{65,129},{129,193},{193,1... | collective-permute-start | bytes 442376 | tf_op jit(solution)/shard_map/ppermute | solution.py:499
  32.5 26.9 %collective-permute-start.1 = (bf16[3,192,128]{2,1,0:T(8,128)(2,1)}, bf16[3,192,128]{2,1,0:T(8,128)(2,1)S(1)}, u32[]{:S(2)}, u32[]{:S(2)}) collective-permute-start(bf16[3,192,128]{2,1,0:T(8,128)(2,1)} %get-tuple-element.34), channel_id=1, source_target_pairs={{0,128},{64,192},{128,0},{192,64},{1,129},{65,193},{129,1},{193,65... | collective-permute-start | bytes 442376 | tf_op jit(solution)/shard_map/ppermute | solution.py:499
  35.2 24.2 %collective-permute-start.2 = (bf16[3,192,128]{2,1,0:T(8,128)(2,1)}, bf16[3,192,128]{2,1,0:T(8,128)(2,1)S(1)}, u32[]{:S(2)}, u32[]{:S(2)}) collective-permute-start(bf16[3,192,128]{2,1,0:T(8,128)(2,1)} %get-tuple-element.35), channel_id=1, source_target_pairs={{0,192},{64,0},{128,64},{192,128},{1,193},{65,1},{129,65},{193,129... | collective-permute-start | bytes 442376 | tf_op jit(solution)/shard_map/ppermute | solution.py:499
  59.5 5.5 %collective-permute-start.3 = (bf16[3,3,192,128]{3,2,1,0:T(8,128)(2,1)S(1)}, bf16[3,3,192,128]{3,2,1,0:T(8,128)(2,1)S(1)}, u32[]{:S(2)}, u32[]{:S(2)}) collective-permute-start(bf16[3,3,192,128]{3,2,1,0:T(8,128)(2,1)S(1)} %pad_maximum_fusion.mine_ref), channel_id=1, source_target_pairs={{0,1},{1,0},{2,3},{3,2},{4,5},{5,4},{6,7},{7,6},{8,9},{9,8},{10,11... | collective-permute-start | bytes 1327112 | tf_op jit(solution)/shard_map/ppermute | solution.py:510
  60.5 26.7 %copy-start.4 = (bf16[32,32,1024]{2,1,0:T(8,128)(2,1)S(1)}, bf16[32,32,1024]{2,1,0:T(8,128)(2,1)}, u32[]{:S(2)}) copy-start(bf16[32,32,1024]{2,1,0:T(8,128)(2,1)} %all-gather.3.cloned.1.call-done) | copy-start | bytes 6291460
  65.0 26.7 %copy-start.6 = (bf16[3,3,192,128]{3,2,1,0:T(8,128)(2,1)}, bf16[3,3,192,128]{3,2,1,0:T(8,128)(2,1)S(1)}, u32[]{:S(2)}) copy-start(bf16[3,3,192,128]{3,2,1,0:T(8,128)(2,1)S(1)} %collective-permute-done.3.other_ref) | copy-start | bytes 1327108
  65.0 1.3 collective-permute-start.4
  85.8 1.5 collective-permute-start.5
  91.7 3.7 %collective-permute-start.6 = (bf16[8,2,32,1024]{3,2,1,0:T(8,128)(2,1)S(1)}, bf16[8,2,32,1024]{3,2,1,0:T(8,128)(2,1)S(1)}, u32[]{:S(2)}, u32[]{:S(2)}) collective-permute-start(bf16[8,2,32,1024]{3,2,1,0:T(8,128)(2,1)S(1)} %get-tuple-element.44), channel_id=1, source_target_pairs={{0,1},{1,0},{2,3},{3,2},{4,5},{5,4},{6,7},{7,6},{8,9},{9,8},{10,11... | collective-permute-start | bytes 3145736 | tf_op jit(solution)/shard_map/ppermute | solution.py:523
  130.3 22.3 %copy-start.5 = (bf16[2,3,192,128]{3,2,1,0:T(8,128)(2,1)S(1)}, bf16[2,3,192,128]{3,2,1,0:T(8,128)(2,1)}, u32[]{:S(2)}) copy-start(bf16[2,3,192,128]{3,2,1,0:T(8,128)(2,1)} %get-tuple-element.52.own_ref) | copy-start | bytes 884740
Sparse Core Ops, SparseCore 0:
  18.9 41.5 all-gather.2
  96.9 33.3 reduce-scatter.1

commit v7 on v6

--- a/solution.py
+++ b/solution.py
@@ -446,7 +446,7 @@
         whole(shape),
         jax.ShapeDtypeStruct(shape, bf16),
         flops=10**9,
-    )(at, d, own, mine, far_memory(other))
+    )(at, d, own, mine, other)
 
 
 def total_kernel(share, in_ref, loss_ref, *out_refs):

time: 186 us -> 185 us (level)
  transfers between devices with their start and end apart: 10 -> 10, of which waited for: 4 -> 5; matrix products, arithmetic and copies ran while one was open for 0% -> 0% of each run, Pallas kernels for 7% -> 7%
where the time goes in v7:
time: 185 us
  blocking collectives  103 us (56%)
  waiting for transfers between devices  26 us (14%)
  Pallas kernels  25.6 us (14%)
  between operations  14.2 us (8%)
  starting transfers between devices  14 us (8%)
    all_to_all x4, blocking collectives, exchange(): return lax.all_to_all(pieces, axes, split_axis=0, concat_axis=0, tiled=True)  84.9 us
    ppermute x3, waiting for transfers between devices, shards(): lax.ppermute(piece, 'y', [(i, (i + step) % n_y) for i in range(n_y)])  22.7 us
    all_to_all x1, blocking collectives, shards(): lax.all_to_all(both, ('y', 'xh', 'z', 'xl', 'core'), 0, 0, axis_index_gro...  18.3 us
    all_to_all x1, starting transfers between devices, exchange(): return lax.all_to_all(pieces, axes, split_axis=0, concat_axis=0, tiled=True)  6.97 us
    ppermute x3, starting transfers between devices, shards(): lax.ppermute(piece, 'y', [(i, (i + step) % n_y) for i in range(n_y)])  6.06 us
    pallas_call x1, Pallas kernels, scores(): call(score_kernel, (1,), [scalars, scalars, whole(rows.shape), remote, wh...  4.5 us
    pallas_call x1, Pallas kernels, products(): call(product_kernel, (1,), [scalars, scalars] + [whole(x.shape) for x in...  4.47 us
  transfers between devices with their start and end apart: 10, of which 5 were waited for; matrix products, arithmetic and copies ran while one was open for 0% of the time, Pallas kernels for 7%

profile of v7, /device:TPU:32, one launch (start us, length us, event | category | flops | bytes accessed | tf_op | source)
XLA Modules:
  0.0 184.5 jit_solution(17532292052142757161)
XLA Ops:
  7.2 0.0 copy-start.3
  7.2 0.0 all-gather.3.cloned.1.call-start
  7.2 2.2 %shard_map.102 = bf16[4,3,32,256]{3,2,1,0:T(8,128)(2,1)S(1)} custom-call(bf16[128,1280]{1,0:T(8,128)(2,1)} %f0_ref.1, bf16[128,1280]{1,0:T(8,128)(2,1)} %f1_ref.1, bf16[128,1280]{1,0:T(8,128)(2,1)} %f2_ref.1, bf16[1280,256]{1,0:T(8,128)(2,1)} %refs_3_.1, bf16[1280,256]{1,0:T(8,128)(2,1)} %refs_4_.1, bf16[1280,256]{1,0:T(8,128)(2,1)} %refs_5_.1), custom_call_target="tpu_custom_call" | custom-call | flops 100000000 | bytes 8388608 | tf_op jit(solution)/shard_map/pallas_call | solution.py:103
  9.4 7.9 %all_to_all.30.emb_ref = bf16[4,3,32,256]{3,2,1,0:T(8,128)(2,1)S(1)} all-to-all(bf16[4,3,32,256]{3,2,1,0:T(8,128)(2,1)S(1)} %shard_map.102), channel_id=1, replica_groups=mesh['y'=4,'xh'=2,'z'=8,'xl'=2,'core'=2] {'xl','core'}, dimensions={0} | all-to-all | bytes 393216 | tf_op jit(solution)/shard_map/all_to_all | solution.py:25
  17.3 0.0 copy-done.3
  17.3 1.4 shard_map.103
  18.7 0.0 all-gather.3.cloned.1.call-update
  18.7 1.4 shard_map.104
  20.1 0.0 copy-start
  20.1 0.0 copy-start.1
  20.1 0.0 copy-start.2
  20.1 7.0 %all-to-all-start.1 = ((bf16[16,2,32,1024]{3,2,1,0:T(8,128)(2,1)}), bf16[16,2,32,1024]{3,2,1,0:T(8,128)(2,1)S(1)}, u32[]{:S(2)}, u32[]{:S(2)}) async-start(bf16[16,2,32,1024]{3,2,1,0:T(8,128)(2,1)} %shard_map.104), calls=%async_computation.1 | async-start | bytes 4194304 | tf_op jit(solution)/shard_map/all_to_all | solution.py:25
  27.1 0.0 reduce-scatter.2.cloned.1.call-start
  27.2 0.1 stack.39.at_ref
  27.3 0.0 copy-done
  27.3 0.0 copy-done.1
  27.3 0.0 copy-done.2
  27.3 3.3 %shard_map.105 = (bf16[2,3,192,128]{3,2,1,0:T(8,128)(2,1)}, bf16[3,192,128]{2,1,0:T(8,128)(2,1)}, bf16[3,192,128]{2,1,0:T(8,128)(2,1)}, bf16[3,192,128]{2,1,0:T(8,128)(2,1)}) custom-call(s32[6]{0:T(128)S(1)} %stack.39.at_ref, bf16[128,1280]{1,0:T(8,128)(2,1)S(1)} %copy-done, bf16[128,1280]{1,0:T(8,128)(2,1)S(1)} %copy-done.1, bf16[128,1280]{1,0:T(8,128)(2,1)S(1)} %copy-done.2), custom_call_target="tpu_custom_call" | custom-call | flops 754974720 | bytes 8388608 | tf_op jit(solution)/shard_map/pallas_call | solution.py:75
  30.6 1.9 %collective-permute-start = (bf16[3,192,128]{2,1,0:T(8,128)(2,1)}, bf16[3,192,128]{2,1,0:T(8,128)(2,1)S(1)}, u32[]{:S(2)}, u32[]{:S(2)}) collective-permute-start(bf16[3,192,128]{2,1,0:T(8,128)(2,1)} %get-tuple-element.33), channel_id=1, source_target_pairs={{0,64},{64,128},{128,192},{192,0},{1,65},{65,129},{129,193},{193,1... | collective-permute-start | bytes 442376 | tf_op jit(solution)/shard_map/ppermute | solution.py:499
  32.5 2.7 %collective-permute-start.1 = (bf16[3,192,128]{2,1,0:T(8,128)(2,1)}, bf16[3,192,128]{2,1,0:T(8,128)(2,1)S(1)}, u32[]{:S(2)}, u32[]{:S(2)}) collective-permute-start(bf16[3,192,128]{2,1,0:T(8,128)(2,1)} %get-tuple-element.34), channel_id=1, source_target_pairs={{0,128},{64,192},{128,0},{192,64},{1,129},{65,193},{129,1},{193,65... | collective-permute-start | bytes 442376 | tf_op jit(solution)/shard_map/ppermute | solution.py:499
  35.2 1.5 collective-permute-start.2
  36.7 22.7 %collective-permute-done = bf16[3,192,128]{2,1,0:T(8,128)(2,1)S(1)} collective-permute-done((bf16[3,192,128]{2,1,0:T(8,128)(2,1)}, bf16[3,192,128]{2,1,0:T(8,128)(2,1)S(1)}, u32[]{:S(2)}, u32[]{:S(2)}) %collective-permute-start) | collective-permute-done | bytes 147488 | tf_op jit(solution)/shard_map/ppermute | solution.py:499
  59.4 0.0 collective-permute-done.1
  59.4 0.0 collective-permute-done.2
  59.4 0.1 pad_maximum_fusion.mine_ref
  59.5 0.0 all-to-all-done.1.rows_ref
  59.5 0.1 collective-permute-start.3
  59.6 0.9 all-gather.3.cloned.1.call-done
  60.5 0.0 copy-start.4
  60.5 4.5 %shard_map.106 = (f32[8,512]{1,0:T(8,128)S(1)}, f32[8,512]{1,0:T(8,128)S(1)}) custom-call(f32[3]{0:T(128)S(1)} %copy-done.3, s32[6]{0:T(128)S(1)} %stack.39.at_ref, bf16[16,2,32,1024]{3,2,1,0:T(8,128)(2,1)S(1)} %all-to-all-done.1.rows_ref, bf16[16,2,32,1024]{3,2,1,0:T(8,128)(2,1)} %bitcast.14, f32[8,128]{1,0:T(8,128)S(1)} %get-tuple-element.38.own_ref), custom_call_target="tpu_custom_call" | custom-call | flops 1610612736 | bytes 8388608 | tf_op jit(solution)/shard_map/pallas_call | solution.py:201
  65.0 0.0 collective-permute-done.3.other_ref
  65.0 0.3 collective-permute-start.4
  65.3 0.9 collective-permute-done.4.got_ref
  66.3 0.6 shard_map.107
  66.8 18.3 %all_to_all.31.both_ref = f32[16,8,512]{2,1,0:T(8,128)S(1)} all-to-all(f32[16,8,512]{2,1,0:T(8,128)S(1)} %shard_map.107), channel_id=1, replica_groups={{0,2,4,6,8,10,12,14,16,18,20,22,24,26,28,30},{32,34,36,38,40,42,44,46,4..., dimensions={0} | all-to-all | bytes 524288 | tf_op jit(solution)/shard_map/all_to_all | solution.py:516
  85.1 0.6 shard_map.108.tot_ref
  85.7 0.3 collective-permute-start.5
  86.0 1.2 collective-permute-done.5.got_ref
  87.2 0.0 copy-done.4
  87.2 4.5 %shard_map.109 = (bf16[3,512,512]{2,1,0:T(8,128)(2,1)S(1)}, bf16[8,2,32,1024]{3,2,1,0:T(8,128)(2,1)S(1)}, bf16[8,2,32,1024]{3,2,1,0:T(8,128)(2,1)S(1)}, f32[3,32,128]{2,1,0:T(8,128)S(1)}) custom-call(f32[3]{0:T(128)S(1)} %copy-done.3, s32[6]{0:T(128)S(1)} %stack.39.at_ref, bf16[16,2,32,1024]{3,2,1,0:T(8,128)(2,1)S(1)} %all-to-all-done.1.rows_ref, ...), custom_call_target="tpu_custom_call" | custom-call | flops 3221225472 | bytes 8388608 | tf_op jit(solution)/shard_map/pallas_call | solution.py:317
  91.7 0.3 collective-permute-start.6
  91.9 3.4 %shard_map.110 = bf16[16,2,32,1024]{3,2,1,0:T(8,128)(2,1)} custom-call(f32[3]{0:T(128)S(1)} %copy-done.3, bf16[3,512,512]{2,1,0:T(8,128)(2,1)S(1)} %get-tuple-element.45.g_ref, bf16[16,2,32,1024]{3,2,1,0:T(8,128)(2,1)S(1)} %bitcast.16), custom_call_target="tpu_custom_call" | custom-call | flops 1610612736 | bytes 8388608 | tf_op jit(solution)/shard_map/pallas_call | solution.py:302
  95.3 0.0 collective-permute-done.6
  95.3 1.4 add_convert_fusion
  96.7 0.0 reduce-scatter.2.cloned.1.call-update
  96.8 33.4 %all_to_all.32.rows_ref = bf16[16,2,32,1024]{3,2,1,0:T(8,128)(2,1)S(1)} all-to-all(bf16[16,2,32,1024]{3,2,1,0:T(8,128)(2,1)} %shard_map.110), channel_id=1, replica_groups=mesh['y'=4,'xh'=2,'z'=8,'xl'=2,'core'=2] {'y','xh','xl'}, dimensions={0} | all-to-all | bytes 4194304 | tf_op jit(solution)/shard_map/all_to_all | solution.py:25
  130.2 0.1 reduce-scatter.2.cloned.1.call-done
  130.3 0.0 copy-start.5
  130.3 2.0 %shard_map.111 = bf16[4,4,112,256]{3,2,1,0:T(8,128)(2,1)S(1)} custom-call(f32[3]{0:T(128)S(1)} %copy-done.3, s32[6]{0:T(128)S(1)} %stack.39.at_ref, bf16[16,2,32,1024]{3,2,1,0:T(8,128)(2,1)S(1)} %all_to_all.32.rows_ref, bf16[2,32,1024]{2,1,0:T(8,128)(2,1)} %bitcast.20, bf16[3,32,1024]{2,1,0:T(8,128)(2,1)} %get-tuple-element.49.emb_hbm, ...), custom_call_target="tpu_custom_call" | custom-call | flops 1000000 | bytes 8388608 | tf_op jit(solution)/shard_map/pallas_call | solution.py:396
  132.4 20.1 %all_to_all.33.d_ref = bf16[16,112,256]{2,1,0:T(8,128)(2,1)S(1)} all-to-all(bf16[16,112,256]{2,1,0:T(8,128)(2,1)S(1)} %bitcast.13), channel_id=1, replica_groups=mesh['y'=4,'xh'=2,'z'=8,'xl'=2,'core'=2] {'y','xl','core'}, dimensions={0} | all-to-all | bytes 1835008 | tf_op jit(solution)/shard_map/all_to_all | solution.py:25
  152.5 0.0 copy-done.5
  152.5 1.1 shard_map.112
  153.6 23.4 %all_to_all.34.in_ref = bf16[16,64,256]{2,1,0:T(8,128)(2,1)S(1)} all-to-all(bf16[16,64,256]{2,1,0:T(8,128)(2,1)S(1)} %shard_map.112), channel_id=1, replica_groups=mesh['y'=4,'xh'=2,'z'=8,'xl'=2,'core'=2] {'xh','z'}, dimensions={0} | all-to-all | bytes 1048576 | tf_op jit(solution)/shard_map/all_to_all | solution.py:25
  177.0 0.7 shard_map.113
Async XLA Ops:
  7.2 10.1 %copy-start.3 = (f32[3]{0:T(128)S(1)}, f32[3]{0:T(128)}, u32[]{:S(2)}) copy-start(f32[3]{0:T(128)} %t_ref.9) | copy-start | bytes 40
  7.2 53.3 %all-gather.3.cloned.1.call-start = ((), (), s32[]{:S(2)}) async-start(), calls=%async_computation.8 | async-start | bytes 2228224 | tf_op jit(solution)/shard_map/all_gather | solution.py:507
  20.1 7.1 %copy-start = (bf16[128,1280]{1,0:T(8,128)(2,1)S(1)}, bf16[128,1280]{1,0:T(8,128)(2,1)}, u32[]{:S(2)}) copy-start(bf16[128,1280]{1,0:T(8,128)(2,1)} %f0_ref.1) | copy-start | bytes 983044
  20.1 7.1 %copy-start.1 = (bf16[128,1280]{1,0:T(8,128)(2,1)S(1)}, bf16[128,1280]{1,0:T(8,128)(2,1)}, u32[]{:S(2)}) copy-start(bf16[128,1280]{1,0:T(8,128)(2,1)} %f1_ref.1) | copy-start | bytes 983044
  20.1 7.1 %copy-start.2 = (bf16[128,1280]{1,0:T(8,128)(2,1)S(1)}, bf16[128,1280]{1,0:T(8,128)(2,1)}, u32[]{:S(2)}) copy-start(bf16[128,1280]{1,0:T(8,128)(2,1)} %f2_ref.1) | copy-start | bytes 983044
  20.1 39.3 %all-to-all-start.1 = ((bf16[16,2,32,1024]{3,2,1,0:T(8,128)(2,1)}), bf16[16,2,32,1024]{3,2,1,0:T(8,128)(2,1)S(1)}, u32[]{:S(2)}, u32[]{:S(2)}) async-start(bf16[16,2,32,1024]{3,2,1,0:T(8,128)(2,1)} %shard_map.104), calls=%async_computation.1 | async-start | bytes 4194304 | tf_op jit(solution)/shard_map/all_to_all | solution.py:25
  27.1 103.2 %reduce-scatter.2.cloned.1.call-start = ((), (), s32[]{:S(2)}) async-start(), calls=%async_computation.7 | async-start | bytes 1179648 | tf_op jit(solution)/shard_map/reduce_scatter | solution.py:527
  30.6 28.8 %collective-permute-start = (bf16[3,192,128]{2,1,0:T(8,128)(2,1)}, bf16[3,192,128]{2,1,0:T(8,128)(2,1)S(1)}, u32[]{:S(2)}, u32[]{:S(2)}) collective-permute-start(bf16[3,192,128]{2,1,0:T(8,128)(2,1)} %get-tuple-element.33), channel_id=1, source_target_pairs={{0,64},{64,128},{128,192},{192,0},{1,65},{65,129},{129,193},{193,1... | collective-permute-start | bytes 442376 | tf_op jit(solution)/shard_map/ppermute | solution.py:499
  32.5 26.9 %collective-permute-start.1 = (bf16[3,192,128]{2,1,0:T(8,128)(2,1)}, bf16[3,192,128]{2,1,0:T(8,128)(2,1)S(1)}, u32[]{:S(2)}, u32[]{:S(2)}) collective-permute-start(bf16[3,192,128]{2,1,0:T(8,128)(2,1)} %get-tuple-element.34), channel_id=1, source_target_pairs={{0,128},{64,192},{128,0},{192,64},{1,129},{65,193},{129,1},{193,65... | collective-permute-start | bytes 442376 | tf_op jit(solution)/shard_map/ppermute | solution.py:499
  35.2 24.2 %collective-permute-start.2 = (bf16[3,192,128]{2,1,0:T(8,128)(2,1)}, bf16[3,192,128]{2,1,0:T(8,128)(2,1)S(1)}, u32[]{:S(2)}, u32[]{:S(2)}) collective-permute-start(bf16[3,192,128]{2,1,0:T(8,128)(2,1)} %get-tuple-element.35), channel_id=1, source_target_pairs={{0,192},{64,0},{128,64},{192,128},{1,193},{65,1},{129,65},{193,129... | collective-permute-start | bytes 442376 | tf_op jit(solution)/shard_map/ppermute | solution.py:499
  59.5 5.5 %collective-permute-start.3 = (bf16[3,3,192,128]{3,2,1,0:T(8,128)(2,1)S(1)}, bf16[3,3,192,128]{3,2,1,0:T(8,128)(2,1)S(1)}, u32[]{:S(2)}, u32[]{:S(2)}) collective-permute-start(bf16[3,3,192,128]{3,2,1,0:T(8,128)(2,1)S(1)} %pad_maximum_fusion.mine_ref), channel_id=1, source_target_pairs={{0,1},{1,0},{2,3},{3,2},{4,5},{5,4},{6,7},{7,6},{8,9},{9,8},{10,11... | collective-permute-start | bytes 1327112 | tf_op jit(solution)/shard_map/ppermute | solution.py:510
  60.5 26.7 %copy-start.4 = (bf16[32,32,1024]{2,1,0:T(8,128)(2,1)S(1)}, bf16[32,32,1024]{2,1,0:T(8,128)(2,1)}, u32[]{:S(2)}) copy-start(bf16[32,32,1024]{2,1,0:T(8,128)(2,1)} %all-gather.3.cloned.1.call-done) | copy-start | bytes 6291460
  65.0 1.3 collective-permute-start.4
  85.7 1.5 collective-permute-start.5
  91.7 3.7 %collective-permute-start.6 = (bf16[8,2,32,1024]{3,2,1,0:T(8,128)(2,1)S(1)}, bf16[8,2,32,1024]{3,2,1,0:T(8,128)(2,1)S(1)}, u32[]{:S(2)}, u32[]{:S(2)}) collective-permute-start(bf16[8,2,32,1024]{3,2,1,0:T(8,128)(2,1)S(1)} %get-tuple-element.44), channel_id=1, source_target_pairs={{0,1},{1,0},{2,3},{3,2},{4,5},{5,4},{6,7},{7,6},{8,9},{9,8},{10,11... | collective-permute-start | bytes 3145736 | tf_op jit(solution)/shard_map/ppermute | solution.py:523
  130.3 22.2 %copy-start.5 = (bf16[2,3,192,128]{3,2,1,0:T(8,128)(2,1)S(1)}, bf16[2,3,192,128]{3,2,1,0:T(8,128)(2,1)}, u32[]{:S(2)}) copy-start(bf16[2,3,192,128]{3,2,1,0:T(8,128)(2,1)} %get-tuple-element.52.own_ref) | copy-start | bytes 884740
Sparse Core Ops, SparseCore 0:
  18.9 41.5 all-gather.2
  96.9 33.4 reduce-scatter.1
